TPU v7x, 32 devices: a whole 2x2x4 slice. The times are simulated.
32 devices in a mesh: dp: 4 (over y, x), fsdp: 8 (over z, core).
Axes of the slice: x: 2, y: 2, z: 4, core: 2. Of those that a mesh axis runs over, the one named last changes fastest.
Arguments:
- tokens: bfloat16 [2, 2048, 896], P(None, ('dp', 'fsdp')), may hold values from -6 to 6
- cotangent: bfloat16 [2, 2048, 896], P(None, ('dp', 'fsdp')), may hold values from -6 to 6
- lengths: int32 [2, 4, 8], P(None, 'dp'), may hold values from 1 to 128, 512 in all within a row
- deal: int32 [2, 4, 8], P(None, 'dp'), may hold values from 0 to 7, each once within a row
- pool: bfloat16 [2, 96, 128, 896], P(None, ('dp', 'fsdp')), may hold values from -6 to 6
- neighbour_ids: int32 [2, 64, 2], P(None, ('dp', 'fsdp')), may hold values from 0 to 2
- norm1_gain: bfloat16 [896], P(('dp', 'fsdp')), may hold values from 0.5 to 1.5
- attn_qkv: bfloat16 [896, 3072], P(('dp', 'fsdp')), may hold values from -0.1875 to 0.1875
- attn_out: bfloat16 [1024, 896], P(('dp', 'fsdp')), may hold values from -0.5 to 0.5
- attn_out_bias: bfloat16 [896], P(('dp', 'fsdp')), may hold values from -3 to 3
- rel_table: bfloat16 [1024], P(('dp', 'fsdp')), may hold values from -4 to 4
- norm2_gain: bfloat16 [896], P(('dp', 'fsdp')), may hold values from 0.5 to 1.5
- cca_query: bfloat16 [896, 1024], P(('dp', 'fsdp')), may hold values from -0.1875 to 0.1875
- cca_kv: bfloat16 [896, 2048], P(('dp', 'fsdp')), may hold values from -0.1875 to 0.1875
- cca_out: bfloat16 [1024, 896], P(('dp', 'fsdp')), may hold values from -0.5 to 0.5
- cca_out_bias: bfloat16 [896], P(('dp', 'fsdp')), may hold values from -3 to 3
- norm3_gain: bfloat16 [896], P(('dp', 'fsdp')), may hold values from 0.5 to 1.5
- ffw_up: bfloat16 [896, 3584], P(('dp', 'fsdp')), may hold values from -0.1875 to 0.1875
- ffw_up_bias: bfloat16 [3584], P(('dp', 'fsdp')), may hold values from -3 to 3
- ffw_down: bfloat16 [3584, 896], P(('dp', 'fsdp')), may hold values from -0.1875 to 0.1875
- ffw_down_bias: bfloat16 [896], P(('dp', 'fsdp')), may hold values from -3 to 3
Outputs:
- activations: bfloat16 [2, 2048, 896], P(None, ('dp', 'fsdp'))
- input_grad: bfloat16 [2, 2048, 896], P(None, ('dp', 'fsdp'))
- pool_grad: float32 [2, 96, 128, 896], P(None, ('dp', 'fsdp'))
- grad_norm1_gain: float32 [896], P(('dp', 'fsdp'))
- grad_attn_qkv: float32 [896, 3072], P(('dp', 'fsdp'))
- grad_attn_out: float32 [1024, 896], P(('dp', 'fsdp'))
- grad_attn_out_bias: float32 [896], P(('dp', 'fsdp'))
- grad_rel_table: float32 [1024], P(('dp', 'fsdp'))
- grad_norm2_gain: float32 [896], P(('dp', 'fsdp'))
- grad_cca_query: float32 [896, 1024], P(('dp', 'fsdp'))
- grad_cca_kv: float32 [896, 2048], P(('dp', 'fsdp'))
- grad_cca_out: float32 [1024, 896], P(('dp', 'fsdp'))
- grad_cca_out_bias: float32 [896], P(('dp', 'fsdp'))
- grad_norm3_gain: float32 [896], P(('dp', 'fsdp'))
- grad_ffw_up: float32 [896, 3584], P(('dp', 'fsdp'))
- grad_ffw_up_bias: float32 [3584], P(('dp', 'fsdp'))
- grad_ffw_down: float32 [3584, 896], P(('dp', 'fsdp'))
- grad_ffw_down_bias: float32 [896], P(('dp', 'fsdp'))
Inputs may be any that keep to these rules, and one draw needn't show every extreme that they name: Each row's lengths sum to 64 times the devices of fsdp, and every row holds one length of exactly 128. `deal`: each row is a permutation of the fsdp indices.
All inputs are finite; a program needn't handle non-finite values.
Results may differ from a plain program's by a relative error of at most 0.018.
Values may be sent and summed in bfloat16 or wider, within the bound.
A program may use at most 256 MiB of HBM per device.

v0:
```python
from functools import partial

import jax
import jax.numpy as jnp
from jax import lax
from jax.sharding import PartitionSpec as P

HEADS = 16
HEAD_DIM = 64
CH = 64
NL = 128
K_NB = 2
NB = 64


epsilon = 1e-06
masked_score = -1e30
query_block = 512


def matmul(left, right):
    return jnp.dot(left, right, preferred_element_type=jnp.float32)


def matmul_tn(left, right):
    return lax.dot_general(
        left, right, (((0,), (0,)), ((), ())), preferred_element_type=jnp.float32
    )


def matmul_nt(left, right):
    return lax.dot_general(
        left, right, (((1,), (1,)), ((), ())), preferred_element_type=jnp.float32
    )


def norm_forward(values, gain_vec):
    inv_rms = lax.rsqrt(jnp.mean(values * values, -1, keepdims=True) + epsilon)
    return (values * inv_rms * gain_vec.astype(jnp.float32), inv_rms)


def norm_backward(values, inv_rms, gain_vec, incoming):
    unit_rows = values * inv_rms
    gained = incoming * gain_vec.astype(jnp.float32)
    d_gain = jnp.sum(incoming * unit_rows, 0)
    d_values = inv_rms * (gained - unit_rows * jnp.mean(gained * unit_rows, -1, keepdims=True))
    return (d_values, d_gain)


def self_scores(query_part, key_rows, table, first_row, bucket_width):
    count = query_part.shape[0]
    length = key_rows.shape[0]
    factor = query_part.shape[2] ** (-0.5)
    raw = (
        jnp.einsum("ihd,jhd->hij", query_part, key_rows, preferred_element_type=jnp.float32)
        * factor
    )
    distance = (first_row + jnp.arange(count, dtype=jnp.int32))[:, None] - jnp.arange(
        length, dtype=jnp.int32
    )[None, :]
    bucket = jnp.clip(distance, 0, length - 1) // bucket_width
    biased = raw + jnp.transpose(jnp.take(table, bucket, axis=0), (2, 0, 1))
    return (jnp.where(distance[None] >= 0, biased, masked_score), bucket)


def self_forward(query_rows, key_rows, value_rows, table, bucket_width):
    scores, bucket = self_scores(query_rows, key_rows, table, 0, bucket_width)
    log_total = jax.nn.logsumexp(scores, axis=-1)
    soft_rows = jnp.exp(scores - log_total[..., None]).astype(jnp.bfloat16)
    outputs = jnp.einsum("hij,jhd->ihd", soft_rows, value_rows, preferred_element_type=jnp.float32)
    log_totals = [log_total]
    return (outputs, log_totals)


def self_backward(query_rows, key_rows, value_rows, table, bucket_width, log_totals, d_mixed):
    length = query_rows.shape[0]
    block_rows = min(length, query_block)
    factor = query_rows.shape[2] ** (-0.5)
    d_query = []
    d_key = jnp.zeros(key_rows.shape, jnp.float32)
    d_value = jnp.zeros(value_rows.shape, jnp.float32)
    d_table = jnp.zeros(table.shape, jnp.float32)
    for block_index, first_row in enumerate(range(0, length, block_rows)):
        scores, bucket = self_scores(query_rows, key_rows, table, first_row, bucket_width)
        soft_rows = jnp.exp(scores - log_totals[block_index][..., None])
        d_soft = jnp.einsum("ihd,jhd->hij", d_mixed, value_rows, preferred_element_type=jnp.float32)
        d_scores = (soft_rows * (d_soft - jnp.sum(d_soft * soft_rows, -1, keepdims=True))).astype(
            jnp.bfloat16
        )
        d_query.append(
            jnp.einsum("hij,jhd->ihd", d_scores, key_rows, preferred_element_type=jnp.float32)
            * factor
        )
        d_key = (
            jnp.einsum("hij,ihd->jhd", d_scores, query_rows, preferred_element_type=jnp.float32)
            * factor
        )
        d_value = jnp.einsum(
            "hij,ihd->jhd",
            soft_rows.astype(jnp.bfloat16),
            d_mixed,
            preferred_element_type=jnp.float32,
        )

        def lookup(entries):
            return jnp.take(entries, bucket, axis=0)

        unused, pull_table = jax.vjp(lookup, table)
        d_table = pull_table(jnp.transpose(d_scores.astype(jnp.float32), (1, 2, 0)))[0]
    return (d_query[0], d_key, d_value, d_table)


def slot_layer(slot_tokens, slot_cot, neighbours, span_ids, ahead, behind):
    (
        gain_first,
        qkv_weight,
        out_weight,
        out_bias,
        rel_flat,
        gain_second,
        cross_query,
        cross_pair,
        cross_out,
        cross_bias,
        gain_third,
        up_weight,
        up_bias,
        down_weight,
        down_bias,
    ) = ahead
    (
        gain_first_b,
        qkv_weight_b,
        out_weight_b,
        out_bias_b,
        rel_flat_b,
        gain_second_b,
        cross_query_b,
        cross_pair_b,
        cross_out_b,
        cross_bias_b,
        gain_third_b,
        up_weight_b,
        up_bias_b,
        down_weight_b,
        down_bias_b,
    ) = behind
    inputs = slot_tokens.astype(jnp.float32)
    length = inputs.shape[0]
    width = inputs.shape[1]
    heads = HEADS
    inner = HEADS * HEAD_DIM
    factor = HEAD_DIM ** (-0.5)
    bucket_width = length // NB
    pool_count = neighbours.shape[0]
    spans = length // CH
    normed_raw, inv_one = norm_forward(inputs, gain_first)
    normed_one = normed_raw.astype(jnp.bfloat16)
    joined = matmul(normed_one, qkv_weight).astype(jnp.bfloat16)
    query_rows = joined[:, :inner].reshape(length, heads, HEAD_DIM)
    key_rows = joined[:, inner : 2 * inner].reshape(length, heads, HEAD_DIM)
    value_rows = joined[:, 2 * inner :].reshape(length, heads, HEAD_DIM)
    table = rel_flat.astype(jnp.float32).reshape(NB, heads)
    mixed, log_totals = self_forward(query_rows, key_rows, value_rows, table, bucket_width)
    mixed = mixed.reshape(length, inner).astype(jnp.bfloat16)
    hidden_one = inputs + (matmul(mixed, out_weight) + out_bias.astype(jnp.float32))
    normed_raw, inv_two = norm_forward(hidden_one, gain_second)
    normed_two = normed_raw.astype(jnp.bfloat16)
    cross_rows = matmul(normed_two, cross_query).astype(jnp.bfloat16)
    flat_pool = neighbours.reshape(-1, width)
    pair_rows = (
        matmul(flat_pool, cross_pair).astype(jnp.bfloat16).reshape(pool_count, NL, 2 * inner)
    )
    flat_ids = span_ids.reshape(-1)
    chosen = jnp.take(pair_rows, flat_ids, axis=0).reshape(spans, K_NB * NL, 2 * inner)
    key_sets = chosen[..., :inner].reshape(spans, K_NB * NL, heads, HEAD_DIM)
    value_sets = chosen[..., inner:].reshape(spans, K_NB * NL, heads, HEAD_DIM)
    pad_rows = jnp.zeros((CH - 1, inner), jnp.bfloat16)
    shifted = jnp.concatenate([cross_rows[CH - 1 :], pad_rows], 0).reshape(
        spans, CH, heads, HEAD_DIM
    )
    cross_scores = (
        jnp.einsum("uchd,uthd->uhct", shifted, key_sets, preferred_element_type=jnp.float32)
        * factor
    )
    cross_total = jax.nn.logsumexp(cross_scores, axis=-1)
    cross_soft = jnp.exp(cross_scores - cross_total[..., None])
    gathered = jnp.einsum(
        "uhct,uthd->uchd",
        cross_soft.astype(jnp.bfloat16),
        value_sets,
        preferred_element_type=jnp.float32,
    ).reshape(length, inner)
    attended = jnp.concatenate([pad_rows, gathered[: length - CH + 1].astype(jnp.bfloat16)], 0)
    hidden_two = hidden_one + (matmul(attended, cross_out) + cross_bias.astype(jnp.float32))
    normed_raw, inv_three = norm_forward(hidden_two, gain_third)
    normed_three = normed_raw.astype(jnp.bfloat16)
    upward = matmul(normed_three, up_weight) + up_bias.astype(jnp.float32)
    activated = jax.nn.gelu(upward, approximate=True).astype(jnp.bfloat16)
    result = hidden_two + (matmul(activated, down_weight) + down_bias.astype(jnp.float32))
    d_result = slot_cot.astype(jnp.float32)
    d_down = d_result.astype(jnp.bfloat16)
    grad_down_weight = matmul_tn(activated, d_down)
    grad_down_bias = jnp.sum(d_down.astype(jnp.float32), 0)
    d_act = matmul_nt(d_down, down_weight_b)
    unused, gelu_pull = jax.vjp(partial(jax.nn.gelu, approximate=True), upward)
    d_up = gelu_pull(d_act)[0].astype(jnp.bfloat16)
    grad_up_bias = jnp.sum(d_up.astype(jnp.float32), 0)
    grad_up_weight = matmul_tn(normed_three, d_up)
    d_back, grad_gain_third = norm_backward(
        hidden_two, inv_three, gain_third_b, matmul_nt(d_up, up_weight_b)
    )
    d_two = d_result + d_back
    d_cross_out = d_two.astype(jnp.bfloat16)
    grad_cross_out = matmul_tn(attended, d_cross_out)
    grad_cross_bias = jnp.sum(d_cross_out.astype(jnp.float32), 0)
    d_attended = matmul_nt(d_cross_out, cross_out_b).astype(jnp.bfloat16)
    d_shifted = jnp.concatenate([d_attended[CH - 1 :], pad_rows], 0).reshape(
        spans, CH, heads, HEAD_DIM
    )
    d_csoft = jnp.einsum(
        "uchd,uthd->uhct", d_shifted, value_sets, preferred_element_type=jnp.float32
    )
    d_cscores = (cross_soft * (d_csoft - jnp.sum(d_csoft * cross_soft, -1, keepdims=True))).astype(
        jnp.bfloat16
    )
    d_shift_query = (
        jnp.einsum(
            "uhct,uthd->uchd", d_cscores, key_sets, preferred_element_type=jnp.float32
        ).reshape(length, inner)
        * factor
    )
    d_cross_rows = jnp.concatenate(
        [jnp.zeros((CH - 1, inner), jnp.float32), d_shift_query[: length - CH + 1]], 0
    ).astype(jnp.bfloat16)
    d_key_sets = (
        jnp.einsum("uhct,uchd->uthd", d_cscores, shifted, preferred_element_type=jnp.float32)
        * factor
    )
    d_value_sets = jnp.einsum(
        "uhct,uchd->uthd",
        cross_soft.astype(jnp.bfloat16),
        d_shifted,
        preferred_element_type=jnp.float32,
    )
    selector = (jnp.arange(pool_count, dtype=jnp.int32)[:, None] == flat_ids[None, :]).astype(
        jnp.float32
    )
    d_keys_pool = jnp.dot(
        selector, d_key_sets.reshape(spans * K_NB, NL * inner), precision=lax.Precision.HIGHEST
    )
    d_values_pool = jnp.dot(
        selector, d_value_sets.reshape(spans * K_NB, NL * inner), precision=lax.Precision.HIGHEST
    )
    d_pairs = jnp.concatenate(
        [d_keys_pool.reshape(-1, inner), d_values_pool.reshape(-1, inner)], -1
    ).astype(jnp.bfloat16)
    grad_cross_pair = matmul_tn(flat_pool, d_pairs)
    d_pool = matmul_nt(d_pairs, cross_pair_b).reshape(pool_count, NL, width)
    grad_cross_query = matmul_tn(normed_two, d_cross_rows)
    d_back, grad_gain_second = norm_backward(
        hidden_one, inv_two, gain_second_b, matmul_nt(d_cross_rows, cross_query_b)
    )
    d_one = d_two + d_back
    d_attn_out = d_one.astype(jnp.bfloat16)
    grad_out_weight = matmul_tn(mixed, d_attn_out)
    grad_out_bias = jnp.sum(d_attn_out.astype(jnp.float32), 0)
    d_mixed = (
        matmul_nt(d_attn_out, out_weight_b).astype(jnp.bfloat16).reshape(length, heads, HEAD_DIM)
    )
    table_b = rel_flat_b.astype(jnp.float32).reshape(NB, heads)
    d_query, d_key, d_value, grad_table = self_backward(
        query_rows, key_rows, value_rows, table_b, bucket_width, log_totals, d_mixed
    )
    d_joined = jnp.concatenate(
        [
            d_query.reshape(length, inner),
            d_key.reshape(length, inner),
            d_value.reshape(length, inner),
        ],
        -1,
    ).astype(jnp.bfloat16)
    grad_qkv = matmul_tn(normed_one, d_joined)
    d_back, grad_gain_first = norm_backward(
        inputs, inv_one, gain_first_b, matmul_nt(d_joined, qkv_weight_b)
    )
    d_inputs = d_one + d_back
    grads = (
        grad_gain_first,
        grad_qkv,
        grad_out_weight,
        grad_out_bias,
        grad_table.reshape(-1),
        grad_gain_second,
        grad_cross_query,
        grad_cross_pair,
        grad_cross_out,
        grad_cross_bias,
        grad_gain_third,
        grad_up_weight,
        grad_up_bias,
        grad_down_weight,
        grad_down_bias,
    )
    return (result.astype(jnp.bfloat16), d_inputs.astype(jnp.bfloat16), d_pool, grads)


def body(
    tokens,
    cotangent,
    lengths,
    deal,
    pool,
    neighbour_ids,
    norm1_gain,
    attn_qkv,
    attn_out,
    attn_out_bias,
    rel_table,
    norm2_gain,
    cca_query,
    cca_kv,
    cca_out,
    cca_out_bias,
    norm3_gain,
    ffw_up,
    ffw_up_bias,
    ffw_down,
    ffw_down_bias,
):
    shards = (
        norm1_gain,
        attn_qkv,
        attn_out,
        attn_out_bias,
        rel_table,
        norm2_gain,
        cca_query,
        cca_kv,
        cca_out,
        cca_out_bias,
        norm3_gain,
        ffw_up,
        ffw_up_bias,
        ffw_down,
        ffw_down_bias,
    )
    members = lax.axis_size("fsdp")
    member = lax.axis_index("fsdp")
    width = tokens.shape[2]
    tok_rows = tokens.shape[1]
    slot_rows = 2 * tok_rows
    member_ids = jnp.arange(members, dtype=jnp.int32)
    slot_places = jnp.arange(slot_rows, dtype=jnp.int32)
    totals = tuple(
        (
            jnp.zeros(
                (item.shape[0] * lax.axis_size(("dp", "fsdp")),) + item.shape[1:], jnp.float32
            )
            for item in shards
        )
    )
    out_list = []
    grad_list = []
    pool_list = []
    for micro_step in range(tokens.shape[0]):
        seq_lengths = lengths[micro_step, 0]
        dealing = deal[micro_step, 0]
        starts = jnp.cumsum(seq_lengths) - seq_lengths
        own_sequence = jnp.sum(jnp.where(dealing == member, member_ids, 0))
        own_start = jnp.sum(jnp.where(member_ids == own_sequence, starts, 0))
        own_length = jnp.sum(jnp.where(member_ids == own_sequence, seq_lengths, 0))
        wanted = own_start + slot_places
        live = slot_places < own_length
        empty_slot = jnp.zeros((slot_rows, width), jnp.bfloat16)
        partial_slots = (empty_slot, empty_slot)
        pieces = (
            lax.all_gather(tokens[micro_step], "fsdp", axis=0, tiled=True),
            lax.all_gather(cotangent[micro_step], "fsdp", axis=0, tiled=True),
        )
        row_count = pieces[0].shape[0]
        inside = live & (wanted >= 0) & (wanted < row_count)
        row_index = jnp.clip(wanted, 0, row_count - 1)
        slot_tokens, slot_cot = tuple(
            (
                jnp.where(inside[:, None], jnp.take(piece, row_index, axis=0), slot)
                for slot, piece in zip(partial_slots, pieces)
            )
        )
        ahead = (
            lax.all_gather(shards[0], ("dp", "fsdp"), axis=0, tiled=True),
            lax.all_gather(shards[1], ("dp", "fsdp"), axis=0, tiled=True),
            lax.all_gather(shards[2], ("dp", "fsdp"), axis=0, tiled=True),
            lax.all_gather(shards[3], ("dp", "fsdp"), axis=0, tiled=True),
            lax.all_gather(shards[4], ("dp", "fsdp"), axis=0, tiled=True),
            lax.all_gather(shards[5], ("dp", "fsdp"), axis=0, tiled=True),
            lax.all_gather(shards[6], ("dp", "fsdp"), axis=0, tiled=True),
            lax.all_gather(shards[7], ("dp", "fsdp"), axis=0, tiled=True),
            lax.all_gather(shards[8], ("dp", "fsdp"), axis=0, tiled=True),
            lax.all_gather(shards[9], ("dp", "fsdp"), axis=0, tiled=True),
            lax.all_gather(shards[10], ("dp", "fsdp"), axis=0, tiled=True),
            lax.all_gather(shards[11], ("dp", "fsdp"), axis=0, tiled=True),
            lax.all_gather(shards[12], ("dp", "fsdp"), axis=0, tiled=True),
            lax.all_gather(shards[13], ("dp", "fsdp"), axis=0, tiled=True),
            lax.all_gather(shards[14], ("dp", "fsdp"), axis=0, tiled=True),
        )
        behind = (
            lax.all_gather(shards[0], ("dp", "fsdp"), axis=0, tiled=True),
            lax.all_gather(shards[1], ("dp", "fsdp"), axis=0, tiled=True),
            lax.all_gather(shards[2], ("dp", "fsdp"), axis=0, tiled=True),
            lax.all_gather(shards[3], ("dp", "fsdp"), axis=0, tiled=True),
            lax.all_gather(shards[4], ("dp", "fsdp"), axis=0, tiled=True),
            lax.all_gather(shards[5], ("dp", "fsdp"), axis=0, tiled=True),
            lax.all_gather(shards[6], ("dp", "fsdp"), axis=0, tiled=True),
            lax.all_gather(shards[7], ("dp", "fsdp"), axis=0, tiled=True),
            lax.all_gather(shards[8], ("dp", "fsdp"), axis=0, tiled=True),
            lax.all_gather(shards[9], ("dp", "fsdp"), axis=0, tiled=True),
            lax.all_gather(shards[10], ("dp", "fsdp"), axis=0, tiled=True),
            lax.all_gather(shards[11], ("dp", "fsdp"), axis=0, tiled=True),
            lax.all_gather(shards[12], ("dp", "fsdp"), axis=0, tiled=True),
            lax.all_gather(shards[13], ("dp", "fsdp"), axis=0, tiled=True),
            lax.all_gather(shards[14], ("dp", "fsdp"), axis=0, tiled=True),
        )
        out_slot, grad_slot, d_pool, grads = slot_layer(
            slot_tokens, slot_cot, pool[micro_step], neighbour_ids[micro_step], ahead, behind
        )
        totals = tuple((total + grad for total, grad in zip(totals, grads)))
        stream_rows = member * tok_rows + jnp.arange(tok_rows, dtype=jnp.int32)
        which = jnp.sum((starts[None, :] <= stream_rows[:, None]).astype(jnp.int32), 1) - 1
        chosen_seq = which[:, None] == member_ids[None, :]
        row_start = jnp.sum(jnp.where(chosen_seq, starts[None, :], 0), 1)
        row_owner = jnp.sum(jnp.where(chosen_seq, dealing[None, :], 0), 1)
        source = row_owner * slot_rows + stream_rows - row_start

        def place(partial_rows, pieces):
            row_count = pieces[0].shape[0]
            inside = (source >= 0) & (source < row_count)
            row_index = jnp.clip(source, 0, row_count - 1)
            return tuple(
                (
                    jnp.where(inside[:, None], jnp.take(piece, row_index, axis=0), rows_now)
                    for rows_now, piece in zip(partial_rows, pieces)
                )
            )

        empty_rows = jnp.zeros((tok_rows, width), jnp.bfloat16)
        out_rows, grad_rows = place(
            (empty_rows, empty_rows),
            (
                lax.all_gather(out_slot, "fsdp", axis=0, tiled=True),
                lax.all_gather(grad_slot, "fsdp", axis=0, tiled=True),
            ),
        )
        out_list.append(out_rows)
        grad_list.append(grad_rows)
        pool_list.append(d_pool)
    scattered = lax.psum_scatter(totals, ("dp", "fsdp"), scatter_dimension=0, tiled=True)
    return (jnp.stack(out_list, 0), jnp.stack(grad_list, 0), jnp.stack(pool_list, 0)) + tuple(
        scattered
    )


def solution(mesh):
    placed = (
        P(None, ("dp", "fsdp"), None),
        P(None, ("dp", "fsdp"), None),
        P(None, "dp", None),
        P(None, "dp", None),
        P(None, ("dp", "fsdp"), None, None),
        P(None, ("dp", "fsdp"), None),
        P(("dp", "fsdp")),
        P(("dp", "fsdp"), None),
        P(("dp", "fsdp"), None),
        P(("dp", "fsdp")),
        P(("dp", "fsdp")),
        P(("dp", "fsdp")),
        P(("dp", "fsdp"), None),
        P(("dp", "fsdp"), None),
        P(("dp", "fsdp"), None),
        P(("dp", "fsdp")),
        P(("dp", "fsdp")),
        P(("dp", "fsdp"), None),
        P(("dp", "fsdp")),
        P(("dp", "fsdp"), None),
        P(("dp", "fsdp")),
    )
    return jax.shard_map(
        body,
        mesh=mesh,
        in_specs=placed,
        out_specs=(
            P(None, ("dp", "fsdp"), None),
            P(None, ("dp", "fsdp"), None),
            P(None, ("dp", "fsdp"), None, None),
            P(("dp", "fsdp")),
            P(("dp", "fsdp"), None),
            P(("dp", "fsdp"), None),
            P(("dp", "fsdp")),
            P(("dp", "fsdp")),
            P(("dp", "fsdp")),
            P(("dp", "fsdp"), None),
            P(("dp", "fsdp"), None),
            P(("dp", "fsdp"), None),
            P(("dp", "fsdp")),
            P(("dp", "fsdp")),
            P(("dp", "fsdp"), None),
            P(("dp", "fsdp")),
            P(("dp", "fsdp"), None),
            P(("dp", "fsdp")),
        ),
        check_vma=False,
    )
```

profile of v0, /device:TPU:5, one launch (start us, length us, event | category | flops | bytes accessed | tf_op | source)
XLA Modules:
  0.0 1575.5 jit_solution(7877755782772030667)
XLA Ops:
  24.5 17.0 %all-gather.2 = bf16[1,512,896]{2,1,0:T(8,128)(2,1)S(1)} all-gather(bf16[1,64,896]{2,1,0:T(8,128)(2,1)S(1)} %get-tuple-element.198), channel_id=4, replica_groups=mesh['dp'=4,'fsdp'=8] {'fsdp'}, dimensions={1}, use_global_device_ids=true | all-gather | bytes 1032192 | tf_op jit(solution)/shard_map/all_gather | solution.py:379
  41.4 17.2 %all-gather = bf16[1,512,896]{2,1,0:T(8,128)(2,1)S(1)} all-gather(bf16[1,64,896]{2,1,0:T(8,128)(2,1)S(1)} %get-tuple-element.200), channel_id=2, replica_groups=mesh['dp'=4,'fsdp'=8] {'fsdp'}, dimensions={1}, use_global_device_ids=true | all-gather | bytes 1032192 | tf_op jit(solution)/shard_map/all_gather | solution.py:378
  59.8 17.8 %all-gather.3 = bf16[1,512,896]{2,1,0:T(8,128)(2,1)S(1)} all-gather(bf16[1,64,896]{2,1,0:T(8,128)(2,1)S(1)} %get-tuple-element.199), channel_id=5, replica_groups=mesh['dp'=4,'fsdp'=8] {'fsdp'}, dimensions={1}, use_global_device_ids=true | all-gather | bytes 1032192 | tf_op jit(solution)/shard_map/all_gather | solution.py:379
  77.6 18.1 %all-gather.1 = bf16[1,512,896]{2,1,0:T(8,128)(2,1)S(1)} all-gather(bf16[1,64,896]{2,1,0:T(8,128)(2,1)S(1)} %get-tuple-element.201), channel_id=3, replica_groups=mesh['dp'=4,'fsdp'=8] {'fsdp'}, dimensions={1}, use_global_device_ids=true | all-gather | bytes 1032192 | tf_op jit(solution)/shard_map/all_gather | solution.py:378
  98.9 40.4 %all-reduce.32 = (bf16[1024]{0:T(1024)(128)(2,1)S(1)}, bf16[896]{0:T(1024)(128)(2,1)S(1)}, bf16[896]{0:T(1024)(128)(2,1)S(1)}, bf16[896]{0:T(1024)(128)(2,1)S(1)...) all-reduce(bf16[1024]{0:T(1024)(128)(2,1)S(1)} %dynamic-update-slic, ...), channel_id=1, replica_groups=mesh['dp'=4,'fsdp'=8] {'dp','fsdp'}, use_global_device_ids=true, to_apply=%add.9 | all-reduce | flops 9984 | bytes 39936
  144.5 54.4 %gather_fusion.1 = f32[16384,16]{1,0:T(8,128)} fusion(f32[64,16]{1,0:T(8,128)S(1)} %reshape.567, s32[16384]{0:T(1024)S(1)} %bitcast_clamp_fusion), kind=kCustom, calls=%fused_computation.1.clone | custom fusion | bytes 2162688 | tf_op jit(solution)/shard_map/jit(_take)/gather | solution.py:62
  198.9 8.0 copy.218
  210.7 6.5 reshape.709
  249.9 19.3 %reshape.707 = bf16[896,3072]{1,0:T(8,128)(2,1)} reshape(bf16[32,28,3072]{2,1,0:T(8,128)(2,1)} %all-gather.34.cloned.1.call-done) | data formatting | bytes 11010048
  328.8 67.1 %all-gather.40.cloned.1.call-done = bf16[32,28,3584]{2,1,0:T(8,128)(2,1)} async-done(((bf16[1,28,3584]{2,1,0:T(8,128)(2,1)}), bf16[32,28,3584]{2,1,0:T(8,128)(2,1)}) %all-gather.40.cloned.1.call-update) | async-done | bytes 6422544 | tf_op jit(solution)/shard_map/all_gather | solution.py:402
  395.9 8.6 reshape.713
  404.5 5.6 convolution_add_fusion.4
  410.1 57.5 %all-gather.24.cloned.1.call-done = bf16[3584,896]{1,0:T(8,128)(2,1)} async-done(((bf16[112,896]{1,0:T(8,128)(2,1)}), bf16[3584,896]{1,0:T(8,128)(2,1)}) %all-gather.24.cloned.1.call-update) | async-done | bytes 6422544 | tf_op jit(solution)/shard_map/all_gather | solution.py:404
  467.6 5.5 fusion.35
  473.6 6.6 convert_reduce_fusion.1
  480.3 6.0 multiply_reduce_fusion.7
  564.5 6.1 fusion.75
  570.7 5.4 fusion.36
  683.0 6.7 convolution_add_fusion
  701.7 6.0 convolution_add_fusion.2
  707.7 7.1 convolution_add_fusion.1
  714.7 461.7 %fusion.168 = (f32[32,3072]{1,0:T(8,128)S(1)}, f32[32,1024]{1,0:T(8,128)S(1)}, f32[32,3584]{1,0:T(8,128)S(1)}) fusion(f32[896,3072]{1,0:T(8,128)} %convolution_add_fusion.2, f32[896,1024]{1,0:T(8,128)} %convolution_add_fusion.6, f32[896,3584]{1,0:T(8,128)} %convolution_add_fusion.1), kind=kCustom, calls=%all-reduce-scatter.3 | all-reduce-scatter fusion | flops 7864321 | bytes 28508160
  1176.5 5.7 collective-permute-start.6
  1182.2 7.3 collective-permute-start.7
  1210.2 7.4 copy.269
  1217.8 7.5 copy.268
  1225.3 98.7 %scatter_custom_fusion.1 = f32[64,16]{1,0:T(8,128)S(1)} fusion(s32[16384]{0:T(1024)S(1)} %fusion.106, f32[16384,16]{1,0:T(8,128)} %bitcast.288, f32[]{:T(128)} %constant.90.clone.1), kind=kCustom, calls=%fused_computation.261 | custom fusion | flops 262144 | bytes 4608 | tf_op jit(solution)/shard_map/transpose(jvp(jit(_take)))/scatter-add | solution.py:106
  1324.0 98.7 %scatter_custom_fusion = f32[64,16]{1,0:T(8,128)S(1)} fusion(s32[16384]{0:T(1024)S(1)} %fusion.106, f32[16384,16]{1,0:T(8,128)} %bitcast.287, f32[]{:T(128)} %constant.90.clone.1), kind=kCustom, calls=%fused_computation.263 | custom fusion | flops 262144 | bytes 4608 | tf_op jit(solution)/shard_map/transpose(jvp(jit(_take)))/scatter-add | solution.py:106
  1423.1 43.6 %all-reduce.31 = (f32[896]{0:T(1024)S(1)}, f32[896]{0:T(1024)S(1)}, f32[1024]{0:T(1024)S(1)}, f32[896]{0:T(1024)S(1)}, f32[896]{0:T(1024)S(1)}, /*index=5*/f32[8...) all-reduce(f32[896]{0:T(1024)S(1)} %add.464, ...), channel_id=6, replica_groups=mesh['dp'=4,'fsdp'=8] {'dp','fsdp'}, use_global_device_ids=true, to_apply=%region_40.45.clone | all-reduce | flops 9984 | bytes 79872
  1497.1 7.5 concatenate.52
  1505.3 31.7 %collective-permute-done.11 = f32[28,3584]{1,0:T(8,128)} collective-permute-done((f32[28,3584]{1,0:T(8,128)}, f32[28,3584]{1,0:T(8,128)}, u32[]{:S(2)}, u32[]{:S(2)}) %collective-permute-start.11) | collective-permute-done | bytes 401440
  1537.1 14.4 concatenate.54
  (757 shorter events, 387.1 us)
Async XLA Ops:
  7.2 200.7 %all-gather.38.cloned.1.call-start = ((), (), s32[]{:S(2)}) async-start(), calls=%async_computation.15 | async-start | bytes 2162688 | tf_op jit(solution)/shard_map/all_gather | solution.py:397
  7.9 202.7 %all-gather.36.cloned.1.call-start = ((), (), s32[]{:S(2)}) async-start(), calls=%async_computation.14 | async-start | bytes 4325376 | tf_op jit(solution)/shard_map/all_gather | solution.py:398
  8.7 241.2 %all-gather.34.cloned.1.call-start = ((), (), s32[]{:S(2)}) async-start(), calls=%async_computation.13 | async-start | bytes 6488064 | tf_op jit(solution)/shard_map/all_gather | solution.py:392
  9.4 280.5 %all-gather.20.cloned.1.call-start = ((), (), s32[]{:S(2)}) async-start(), calls=%async_computation.3 | async-start | bytes 1892352 | tf_op jit(solution)/shard_map/all_gather | solution.py:393
  10.0 313.5 %all-gather.22.cloned.1.call-start = ((), (), s32[]{:S(2)}) async-start(), calls=%async_computation.4 | async-start | bytes 1892352 | tf_op jit(solution)/shard_map/all_gather | solution.py:399
  10.6 385.3 %all-gather.40.cloned.1.call-start = ((), (), s32[]{:S(2)}) async-start(), calls=%async_computation.16 | async-start | bytes 7569408 | tf_op jit(solution)/shard_map/all_gather | solution.py:402
  11.1 456.4 %all-gather.24.cloned.1.call-start = ((), (), s32[]{:S(2)}) async-start(), calls=%async_computation.5 | async-start | bytes 6623232 | tf_op jit(solution)/shard_map/all_gather | solution.py:404
  11.9 1541.5 %all-gather.26.cloned.1.call-start = ((), (), s32[]{:S(2)}) async-start(), calls=%async_computation.6 | async-start | bytes 2064384 | tf_op jit(solution)/shard_map/all_gather | solution.py:450
  20.5 269.4 %copy-start.149 = (pred[128]{0:T(512)(128)(4,1)}, pred[128]{0:T(512)(128)(4,1)S(1)}, u32[]{:S(2)}) copy-start(pred[128]{0:T(512)(128)(4,1)S(1)} %get-tuple-element.256) | copy-start | bytes 388
  20.5 269.4 %copy-start.153 = (pred[128]{0:T(512)(128)(4,1)}, pred[128]{0:T(512)(128)(4,1)S(1)}, u32[]{:S(2)}) copy-start(pred[128]{0:T(512)(128)(4,1)S(1)} %get-tuple-element.257) | copy-start | bytes 388
  22.5 254.6 %copy-start.141 = (pred[128]{0:T(512)(128)(4,1)}, pred[128]{0:T(512)(128)(4,1)S(1)}, u32[]{:S(2)}) copy-start(pred[128]{0:T(512)(128)(4,1)S(1)} %get-tuple-element.255) | copy-start | bytes 388
  59.5 209.7 %copy-start.48 = (bf16[128,896]{1,0:T(8,128)(2,1)}, bf16[128,896]{1,0:T(8,128)(2,1)S(1)}, u32[]{:S(2)}) copy-start(bf16[128,896]{1,0:T(8,128)(2,1)S(1)} %gather_fusion) | copy-start | bytes 688132
  473.1 1082.9 %all-gather.30.cloned.1.call-start = ((), (), s32[]{:S(2)}) async-start(), calls=%async_computation.8 | async-start | bytes 2064384 | tf_op jit(solution)/shard_map/all_gather | solution.py:451
  570.7 988.1 %all-gather.28.cloned.1.call-start = ((), (), s32[]{:S(2)}) async-start(), calls=%async_computation.7 | async-start | bytes 2064384 | tf_op jit(solution)/shard_map/all_gather | solution.py:450
  576.2 985.2 %all-gather.32.cloned.1.call-start = ((), (), s32[]{:S(2)}) async-start(), calls=%async_computation.9 | async-start | bytes 2064384 | tf_op jit(solution)/shard_map/all_gather | solution.py:451
  613.1 952.7 %all-reduce.36.cloned.1.call-start = ((), (), s32[]{:S(2)}) async-start(), calls=%async_computation.17 | async-start | bytes 14680064
  670.8 898.0 %reduce-scatter.11.cloned.1.call-start = ((), (), s32[]{:S(2)}) async-start(), calls=%async_computation.10 | async-start | bytes 3784704 | tf_op jit(solution)/shard_map/reduce_scatter | solution.py:457
  675.0 893.7 %reduce-scatter.13.cloned.1.call-start = ((), (), s32[]{:S(2)}) async-start(), calls=%async_computation.11 | async-start | bytes 3784704 | tf_op jit(solution)/shard_map/reduce_scatter | solution.py:457
  679.4 889.3 %reduce-scatter.15.cloned.1.call-start = ((), (), s32[]{:S(2)}) async-start(), calls=%async_computation.12 | async-start | bytes 13246464 | tf_op jit(solution)/shard_map/reduce_scatter | solution.py:457
  714.7 474.8 %copy-start.57 = (bf16[384,2048]{1,0:T(8,128)(2,1)S(1)}, bf16[384,2048]{1,0:T(8,128)(2,1)}, u32[]{:S(2)}) copy-start(bf16[384,2048]{1,0:T(8,128)(2,1)} %copy-done.56) | copy-start | bytes 4718596
  1176.5 31.0 %collective-permute-start.6 = (f32[32,1024]{1,0:T(8,128)S(1)}, f32[32,1024]{1,0:T(8,128)S(1)}, u32[]{:S(2)}, u32[]{:S(2)}) collective-permute-start(f32[32,1024]{1,0:T(8,128)S(1)} %get-tuple-element.156), channel_id=1, source_target_pairs={{0,3},{1,4},{2,5},{3,6},{4,7},{5,8},{6,9},{7,10},{8,11},{9,12},{10... | collective-permute-start | bytes 393224
  1182.2 23.3 %collective-permute-start.7 = (f32[28,1024]{1,0:T(8,128)S(1)}, f32[28,1024]{1,0:T(8,128)S(1)}, u32[]{:S(2)}, u32[]{:S(2)}) collective-permute-start(f32[28,1024]{1,0:T(8,128)S(1)} %slice.165), channel_id=1, source_target_pairs={{0,4},{1,5},{2,6},{3,7},{4,8},{5,9},{6,10},{7,11},{8,12},{9,13},{1... | collective-permute-start | bytes 344072
  1197.5 274.6 %collective-permute-start.5 = (f32[32,1024]{1,0:T(8,128)S(1)}, f32[32,1024]{1,0:T(8,128)S(1)}, u32[]{:S(2)}, u32[]{:S(2)}) collective-permute-start(f32[32,1024]{1,0:T(8,128)S(1)} %get-tuple-element.156), channel_id=1, source_target_pairs={{0,2},{1,3},{2,4},{3,5},{4,6},{5,7},{6,8},{7,9},{8,10},{9,11},{10,... | collective-permute-start | bytes 393224
  1200.2 287.1 %collective-permute-start.2 = (f32[32,3072]{1,0:T(8,128)S(1)}, f32[32,3072]{1,0:T(8,128)}, u32[]{:S(2)}, u32[]{:S(2)}) collective-permute-start(f32[32,3072]{1,0:T(8,128)S(1)} %get-tuple-element.155), channel_id=1, source_target_pairs={{0,3},{1,4},{2,5},{3,6},{4,7},{5,8},{6,9},{7,10},{8,11},{9,12},{10... | collective-permute-start | bytes 1179656
  1202.4 289.1 %collective-permute-start.1 = (f32[32,3072]{1,0:T(8,128)S(1)}, f32[32,3072]{1,0:T(8,128)}, u32[]{:S(2)}, u32[]{:S(2)}) collective-permute-start(f32[32,3072]{1,0:T(8,128)S(1)} %get-tuple-element.155), channel_id=1, source_target_pairs={{0,2},{1,3},{2,4},{3,5},{4,6},{5,7},{6,8},{7,9},{8,10},{9,11},{10,... | collective-permute-start | bytes 1179656
  1205.5 291.6 %collective-permute-start = (f32[32,3072]{1,0:T(8,128)S(1)}, f32[32,3072]{1,0:T(8,128)}, u32[]{:S(2)}, u32[]{:S(2)}) collective-permute-start(f32[32,3072]{1,0:T(8,128)S(1)} %get-tuple-element.155), channel_id=1, source_target_pairs={{0,1},{1,2},{2,3},{3,4},{4,5},{5,6},{6,7},{7,8},{8,9},{9,10},{10,1... | collective-permute-start | bytes 1179656
  1207.4 277.9 %collective-permute-start.3 = (f32[28,3072]{1,0:T(8,128)}, f32[28,3072]{1,0:T(8,128)}, u32[]{:S(2)}, u32[]{:S(2)}) collective-permute-start(f32[28,3072]{1,0:T(8,128)} %slice.164), channel_id=1, source_target_pairs={{0,4},{1,5},{2,6},{3,7},{4,8},{5,9},{6,10},{7,11},{8,12},{9,13},{1... | collective-permute-start | bytes 1032200
  1472.1 8.1 collective-permute-start.4
  1480.3 56.8 %collective-permute-start.10 = (f32[32,3584]{1,0:T(8,128)S(1)}, f32[32,3584]{1,0:T(8,128)S(1)}, u32[]{:S(2)}, u32[]{:S(2)}) collective-permute-start(f32[32,3584]{1,0:T(8,128)S(1)} %get-tuple-element.157), channel_id=1, source_target_pairs={{0,3},{1,4},{2,5},{3,6},{4,7},{5,8},{6,9},{7,10},{8,11},{9,12},{10... | collective-permute-start | bytes 1376264
  1485.3 51.7 %collective-permute-start.9 = (f32[32,3584]{1,0:T(8,128)S(1)}, f32[32,3584]{1,0:T(8,128)}, u32[]{:S(2)}, u32[]{:S(2)}) collective-permute-start(f32[32,3584]{1,0:T(8,128)S(1)} %get-tuple-element.157), channel_id=1, source_target_pairs={{0,2},{1,3},{2,4},{3,5},{4,6},{5,7},{6,8},{7,9},{8,10},{9,11},{10,... | collective-permute-start | bytes 1376264
  1487.3 49.8 %collective-permute-start.8 = (f32[32,3584]{1,0:T(8,128)S(1)}, f32[32,3584]{1,0:T(8,128)}, u32[]{:S(2)}, u32[]{:S(2)}) collective-permute-start(f32[32,3584]{1,0:T(8,128)S(1)} %get-tuple-element.157), channel_id=1, source_target_pairs={{0,1},{1,2},{2,3},{3,4},{4,5},{5,6},{6,7},{7,8},{8,9},{9,10},{10,1... | collective-permute-start | bytes 1376264
  1491.5 45.6 %collective-permute-start.11 = (f32[28,3584]{1,0:T(8,128)}, f32[28,3584]{1,0:T(8,128)}, u32[]{:S(2)}, u32[]{:S(2)}) collective-permute-start(f32[28,3584]{1,0:T(8,128)} %slice.166), channel_id=1, source_target_pairs={{0,4},{1,5},{2,6},{3,7},{4,8},{5,9},{6,10},{7,11},{8,12},{9,13},{1... | collective-permute-start | bytes 1204232
  (208 other events, 4950.4 us)
Sparse Core Ops, SparseCore 0:
  11.0 58.5 all-gather.37
  72.6 62.1 all-gather.35
  137.8 68.0 all-gather.33
  208.6 54.4 all-gather.19
  265.8 54.8 all-gather.21
  323.3 72.5 all-gather.39
  398.8 68.7 all-gather.23
  473.2 25.4 all-gather.25
  570.8 25.6 all-gather.29
  597.9 26.4 all-gather.27
  626.1 26.4 all-gather.31
  670.9 209.2 all-reduce.35
  883.1 148.1 reduce-scatter.10
  1034.1 151.2 reduce-scatter.12
  1188.1 199.9 reduce-scatter.14
where the time goes:
time: 1590 us; the launch traced here: 1580 us
  blocking collectives  616 us (39%)
  local copies, waits for them, and re-layouts  310 us (19%)
  other arithmetic  231 us (15%)
  matrix products  196 us (12%)
  waiting for transfers between devices  161 us (10%)
  starting transfers between devices  44.8 us (3%)
  between operations  17.2 us (1%)
    unnamed x3, blocking collectives  546 us
    scatter-add x2, other arithmetic, lookup(): return jnp.take(entries, bucket, axis=0)  197 us
    unnamed x471, local copies, waits for them, and re-layouts  98.5 us
    all_gather x1, waiting for transfers between devices, body(): lax.all_gather(shards[11], ('dp', 'fsdp'), axis=0, tiled=True)  67.1 us
    gather x2, local copies, waits for them, and re-layouts, self_scores(): biased = raw + jnp.transpose(jnp.take(table, bucket, axis=0), (2, 0, 1))  62.4 us
    all_gather x1, waiting for transfers between devices, body(): lax.all_gather(shards[13], ('dp', 'fsdp'), axis=0, tiled=True)  57.5 us
    dot_general x14, matrix products, matmul_nt(): lax.dot_general(left, right, (((1,), (1,)), ((), ())), preferred_element_...  48.6 us
    dot_general x14, matrix products, matmul(): return jnp.dot(left, right, preferred_element_type=jnp.float32)  46 us
  transfers between devices with their start and end apart: 27, of which 3 were waited for; matrix products, arithmetic and copies ran while one was open for 75% of the time, Pallas kernels for 0%

commit v1 on v0

v1 whole, which is shorter than its diff:
```python
from functools import partial

import jax
import jax.numpy as jnp
from jax import lax
from jax.experimental import pallas as pl
from jax.experimental.pallas import tpu as pltpu
from jax.sharding import PartitionSpec as P

MIB = 1 << 20
F32, BF = jnp.float32, jnp.bfloat16
HEADS, HEAD_DIM, CH, NL, K_NB, NB = 16, 64, 64, 128, 2, 64
epsilon = 1e-06
masked_score = -1e30
tile = 512
low_row = 48
GROUPS = 32
SMALLS = 16
G1, G2, G3, BA, BC, BD, REL, UPB = range(8)


def mm(a, b):
    return jnp.dot(a, b, preferred_element_type=F32)
def mm_tn(a, b):
    return lax.dot_general(a, b, (((0,), (0,)), ((), ())), preferred_element_type=F32)
def mm_nt(a, b):
    return lax.dot_general(a, b, (((1,), (1,)), ((), ())), preferred_element_type=F32)
def iota(shape, dim):
    return lax.broadcasted_iota(jnp.int32, shape, dim)
def onehot(cond):
    return jnp.where(cond, 1.0, 0.0).astype(BF)
def split2(v):
    hi = v.astype(BF)
    return hi, (v - hi.astype(F32)).astype(BF)
def columns(i, size):
    return pl.ds(pl.multiple_of(i * size, size), size)
def loop(count, body):
    def step(i, carry):
        body(i)
        return carry
    lax.fori_loop(0, count, step, 0)


def spread(width):
    small = width // GROUPS
    big = (small + 15) // 16 * 16
    row, col = iota((width, GROUPS * big), 0), iota((width, GROUPS * big), 1)
    return onehot((col // big == row // small) & (col % big == row % small))


def dense(v, spread_mat):
    hi, lo = split2(v)
    return mm_nt(hi, spread_mat) + mm_nt(lo, spread_mat)


def small_rows(packed, width):
    per = width // GROUPS
    put = onehot(iota((128, width), 0) == iota((128, width), 1) % per)
    placed = mm(packed, put)
    shape = (GROUPS * SMALLS, width)
    placed = jnp.where(iota(shape, 0) // SMALLS == iota(shape, 1) // per, placed, 0.0).astype(BF)
    take = onehot(iota((SMALLS, GROUPS * SMALLS), 1) % SMALLS == iota((SMALLS, GROUPS * SMALLS), 0))
    return mm(take, placed)


def table_rows(packed, length):
    per = NB * HEADS // GROUPS // HEADS
    width = length // NB
    take = onehot(iota((GROUPS, GROUPS * SMALLS), 1) == iota((GROUPS, GROUPS * SMALLS), 0) * SMALLS + REL)
    held = mm(take, packed).astype(BF)
    far = (length - iota((GROUPS, length), 1)) % length // width
    at = mm_tn(held, onehot(far // per == iota((GROUPS, length), 0)))
    which = (length - iota((HEADS, length), 1)) % length // width % per
    out = jnp.zeros((HEADS, length), F32)
    for k in range(per):
        out = jnp.where(which == k, at[k * HEADS:(k + 1) * HEADS], out)
    return out


def biases(rows, bias):
    length = bias.shape[1]
    below = iota((length, length), 0) >= iota((length, length), 1)
    for h in range(HEADS):
        wide = jnp.broadcast_to(rows[h:h + 1], (length, length))
        bias[h] = jnp.where(below, pltpu.roll(wide, 0, 1, stride=1, stride_axis=0), masked_score)


def rms(v):
    return lax.rsqrt(jnp.mean(v * v, -1, keepdims=True) + epsilon)


def norm(v, gain):
    return (v * rms(v) * gain).astype(BF)


def norm_back(v, gain, dn):
    r = rms(v)
    unit = v * r
    gained = dn * gain
    return r * (gained - unit * jnp.mean(gained * unit, -1, keepdims=True)), jnp.sum(dn * unit, 0, keepdims=True)


def halves(v):
    first = iota(v.shape, 1) < HEAD_DIM
    zero = jnp.zeros(v.shape, v.dtype)
    return jnp.concatenate([jnp.where(first, v, zero), jnp.where(first, zero, v)], 0)


def joined(v):
    n = v.shape[0] // 2
    return jnp.where(iota((n, v.shape[1]), 1) < HEAD_DIM, v[:n], v[n:])


def head_loop(count, body):
    pairs = HEADS // 2
    def step(i, carry):
        m, p = i // pairs, i % pairs
        body(m, p, p * 2 * HEAD_DIM)
        return carry
    lax.fori_loop(0, count * pairs, step, 0, unroll=2)


class Sizes:
    def __init__(self, MB, length, width, att, ff, pool):
        self.MB, self.length, self.width, self.att, self.ff, self.pool = MB, length, width, att, ff, pool
        self.rows = MB * length
        self.win = length - low_row
        self.wide = GROUPS * ((width // GROUPS + 15) // 16 * 16)
        self.keys = pool * NL


def fwd_self(z, join, bias, ps, att):
    factor = HEAD_DIM ** -0.5
    def body(m, p, c):
        rows = pl.ds(pl.multiple_of(m * z.length, 128), z.length)
        at = lambda part: pl.ds(pl.multiple_of(part * z.att + c, 128), 128)
        q, k, v = join[rows, at(0)], join[rows, at(1)], join[rows, at(2)]
        s = mm_nt(halves(q), k) * factor + jnp.concatenate([bias[2 * p], bias[2 * p + 1]], 0)
        e = jnp.exp(s - jnp.max(s, -1, keepdims=True))
        soft = e * (1.0 / jnp.sum(e, -1, keepdims=True))
        ps[m, p] = soft
        att[rows, at(0)] = joined(mm(soft.astype(BF), v)).astype(BF)
    head_loop(z.MB, body)


def fwd_cross(z, cq, ckv, times, pc, c_out):
    factor = HEAD_DIM ** -0.5
    for m in range(z.MB):
        c_out[m * z.length:m * z.length + low_row] = jnp.zeros((low_row, z.att), BF)
    def body(m, p, c):
        rows = pl.ds(pl.multiple_of(m * z.length + low_row, 16), z.win)
        keys = pl.ds(pl.multiple_of(m * z.keys, 128), z.keys)
        at = lambda part: pl.ds(pl.multiple_of(part * z.att + c, 128), 128)
        q, k, v = cq[rows, at(0)], ckv[keys, at(0)], ckv[keys, at(1)]
        cnt = times[m]
        cnt = jnp.concatenate([cnt, cnt], 0)
        s = jnp.where(cnt > 0, mm_nt(halves(q), k) * factor, masked_score)
        e = jnp.exp(s - jnp.max(s, -1, keepdims=True))
        total = jnp.sum(e * cnt, -1, keepdims=True)
        soft = e * (1.0 / jnp.where(total > 0, total, 1.0))
        pc[m, p] = soft
        c_out[rows, at(0)] = joined(mm((soft.astype(BF).astype(F32) * cnt).astype(BF), v)).astype(BF)
    head_loop(z.MB, body)


def gelu_parts(u):
    k = 0.7978845608028654
    t = jnp.tanh(k * (u + 0.044715 * u * u * u))
    half = 0.5 * (1.0 + t)
    return u * half, half + 0.5 * u * (1.0 - t * t) * k * (1.0 + 3 * 0.044715 * u * u)


def fwd_up(z, n3, up, upb, gl, slope):
    def body(i):
        at = columns(i, tile)
        u = mm(n3[...], up[:, at]) + upb[:, at]
        value, d = gelu_parts(u)
        gl[:, at] = value.astype(BF)
        slope[:, at] = d
    loop(z.ff // tile, body)


def project(left, weight, out, size=tile):
    def body(i):
        at = columns(i, size)
        out[:, at] = mm(left[...], weight[:, at]).astype(out.dtype)
    loop(out.shape[1] // size, body)


def project_nt(left, weight, out, size=tile):
    def body(i):
        at = columns(i, size)
        out[:, at] = mm_nt(left[...], weight[at, :]).astype(out.dtype)
    loop(out.shape[1] // size, body)


def outer(left, right, out, size=256):
    def body(i):
        at = columns(i, size)
        out[at, :] = mm_tn(left[:, at], right[...]).astype(out.dtype)
    loop(out.shape[0] // size, body)


def bwd_self(z, join, ps, da, dq, table_sum):
    factor = HEAD_DIM ** -0.5
    def body(m, p, c):
        rows = pl.ds(pl.multiple_of(m * z.length, 128), z.length)
        at = lambda part: pl.ds(pl.multiple_of(part * z.att + c, 128), 128)
        q, k, v = join[rows, at(0)], join[rows, at(1)], join[rows, at(2)]
        d = halves(da[rows, at(0)])
        soft = ps[m, p]
        dp = mm_nt(d, v)
        ds = (soft * (dp - jnp.sum(dp * soft, -1, keepdims=True))).astype(BF)
        dq[rows, at(0)] = (joined(mm(ds, k)) * factor).astype(BF)
        dq[rows, at(1)] = (mm_tn(ds, halves(q)) * factor).astype(BF)
        dq[rows, at(2)] = mm_tn(soft.astype(BF), d).astype(BF)
        wide = ds.astype(F32)
        for k in range(2):
            heads = pl.ds(pl.multiple_of((2 * p + k) * z.length, 128), z.length)
            table_sum[:, heads] += wide[k * z.length:(k + 1) * z.length]
    head_loop(z.MB, body)


def bwd_cross(z, cq, ckv, times, pc, dc, dcq, dckv):
    factor = HEAD_DIM ** -0.5
    for m in range(z.MB):
        dcq[m * z.length:m * z.length + low_row] = jnp.zeros((low_row, z.att), BF)
    def body(m, p, c):
        rows = pl.ds(pl.multiple_of(m * z.length + low_row, 16), z.win)
        keys = pl.ds(pl.multiple_of(m * z.keys, 128), z.keys)
        at = lambda part: pl.ds(pl.multiple_of(part * z.att + c, 128), 128)
        q, k, v = cq[rows, at(0)], ckv[keys, at(0)], ckv[keys, at(1)]
        d = halves(dc[rows, at(0)])
        cnt = times[m]
        cnt = jnp.concatenate([cnt, cnt], 0)
        soft = pc[m, p]
        dp = mm_nt(d, v)
        ds = (soft * (dp - jnp.sum(dp * soft * cnt, -1, keepdims=True))).astype(BF)
        ds = (ds.astype(F32) * cnt).astype(BF)
        pb = (soft.astype(BF).astype(F32) * cnt).astype(BF)
        dcq[rows, at(0)] = (joined(mm(ds, k)) * factor).astype(BF)
        dckv[keys, at(0)] = (mm_tn(ds, halves(q)) * factor).astype(BF)
        dckv[keys, at(1)] = mm_tn(pb, d).astype(BF)
    head_loop(z.MB, body)


def exact(a, b, dims):
    return lax.dot_general(a, b, (dims, ((), ())), precision=lax.Precision.HIGHEST, preferred_element_type=F32)


def table_grad(table_sum):
    length = table_sum.shape[0]
    flip = onehot(iota((length, length), 0) + iota((length, length), 1) == length - 1)
    hi, lo = split2(table_sum)
    flipped = mm(flip, hi) + mm(flip, lo)
    rows = []
    for h in range(HEADS):
        turned = pltpu.roll(flipped[:, h * length:(h + 1) * length], 0, 1, stride=1, stride_axis=0)
        rows.append(jnp.sum(turned, 0, keepdims=True))
    return jnp.concatenate(rows, 0)


WEIGHTS = ("qkv", "ao", "cq", "kv", "co", "up", "dn")


def forward_steps(z, ready, r):
    sp = spread(z.width)
    r.sp[...] = sp
    packed = ready("small")[...]
    r.vec[...] = small_rows(packed, z.width)
    def upb(i):
        at = columns(i, tile)
        per = z.ff // GROUPS
        put = onehot(iota((128, tile), 0) == (iota((128, tile), 1) + i * tile) % per)
        placed = mm(packed, put)
        shape = (GROUPS * SMALLS, tile)
        mine = (iota(shape, 0) // SMALLS == (iota(shape, 1) + i * tile) // per) & (iota(shape, 0) % SMALLS == UPB)
        r.upb[:, at] = jnp.sum(jnp.where(mine, placed, 0.0), 0, keepdims=True)
    loop(z.ff // tile, upb)
    biases(table_rows(packed, z.length), r.bias)
    kv = ready("kv")
    half = z.keys // 2
    def pool_part(i):
        rows = pl.ds(pl.multiple_of(i * half, 64), half)
        r.ep[rows, :] = mm(r.pool[rows, :], r.sp[...]).astype(BF)
    loop(z.MB * 2, pool_part)
    project(r.ep, kv, r.ckv, 256)
    tok = ready("tok")
    stream = tok.shape[1]
    for m in range(z.MB):
        rows = slice(m * z.length, (m + 1) * z.length)
        pick = onehot(r.wanted[rows, :1] == iota((z.length, stream), 1))
        r.x[rows] = mm(pick, tok[m])
    x = r.x[...]
    r.n1[...] = mm(norm(x, r.vec[G1:G1 + 1]), r.sp[...]).astype(BF)
    project(r.n1, ready("qkv"), r.join)
    fwd_self(z, r.join, r.bias, r.ps, r.a)
    h1 = x + (mm(r.a[...], ready("ao")[...]) + r.vec[BA:BA + 1])
    r.h1[...] = h1
    r.n2[...] = mm(norm(h1, r.vec[G2:G2 + 1]), r.sp[...]).astype(BF)
    project(r.n2, ready("cq"), r.cq)
    fwd_cross(z, r.cq, r.ckv, r.times, r.pc, r.c)
    h2 = r.h1[...] + (mm(r.c[...], ready("co")[...]) + r.vec[BC:BC + 1])
    r.h2[...] = h2
    r.n3[...] = mm(norm(h2, r.vec[G3:G3 + 1]), r.sp[...]).astype(BF)
    fwd_up(z, r.n3, ready("up"), r.upb, r.gl, r.slope)
    y = (r.h2[...] + (mm(r.gl[...], ready("dn")[...]) + r.vec[BD:BD + 1])).astype(BF)
    ct = ready("ct")
    for m in range(z.MB):
        rows = slice(m * z.length, (m + 1) * z.length)
        pick = onehot(r.wanted[rows, :1] == iota((z.length, stream), 1))
        r.back_y[m] = mm_tn(pick, y[rows]).astype(BF)
        r.ct[rows] = mm(pick, ct[m]).astype(BF)


def backward_steps(z, ready, emit, r):
    vec, sp = r.vec, r.sp
    e3 = r.ct[...]
    small = {}
    ones = lambda v: jnp.sum(v.astype(F32), 0, keepdims=True)
    small[BD] = ones(e3)
    dn = ready("dn")
    for i in range(z.ff // tile):
        at = slice(i * tile, (i + 1) * tile)
        du = (mm_nt(e3, dn[at, :]) * r.slope_tile(i)).astype(BF)
        r.du[:, at] = du
        r.upb_sum[:, at] = ones(du)
    emit("dn", lambda out: outer(r.gl, r.ct, out))
    dw, small[G3] = norm_back(r.h2[...], vec[G3:G3 + 1], dense(mm_nt(r.du[...], ready("up")[...]), sp[...]))
    emit("up", lambda out: outer(r.n3, r.du, out))
    dh = e3.astype(F32) + dw
    r.dh[...] = dh
    r.e[...] = dh.astype(BF)
    small[BC] = ones(r.e[...])
    project_nt(r.e, ready("co"), r.dc)
    emit("co", lambda out: outer(r.c, r.e, out))
    bwd_cross(z, r.cq, r.ckv, r.times, r.pc, r.dc, r.dcq, r.dckv)
    kv = ready("kv")
    part = z.keys // 2
    for i in range(z.MB * 2):
        rows = slice(i * part, (i + 1) * part)
        r.put_pool(i, dense(mm_nt(r.dckv[rows, :], kv[...]), sp[...]))
    emit("kv", lambda out: outer(r.ep, r.dckv, out))
    dw, small[G2] = norm_back(r.h1[...], vec[G2:G2 + 1], dense(mm_nt(r.dcq[...], ready("cq")[...]), sp[...]))
    emit("cq", lambda out: outer(r.n2, r.dcq, out))
    dh = r.dh[...] + dw
    r.dh[...] = dh
    r.e[...] = dh.astype(BF)
    small[BA] = ones(r.e[...])
    project_nt(r.e, ready("ao"), r.dc)
    emit("ao", lambda out: outer(r.a, r.e, out))
    r.table[...] = jnp.zeros(r.table.shape, F32)
    bwd_self(z, r.join, r.ps, r.dc, r.dq, r.table)
    dw, small[G1] = norm_back(r.x[...], vec[G1:G1 + 1], dense(mm_nt(r.dq[...], ready("qkv")[...]), sp[...]))
    dx = (r.dh[...] + dw).astype(BF)
    stream = r.back_x.shape[1]
    for m in range(z.MB):
        rows = slice(m * z.length, (m + 1) * z.length)
        pick = onehot(r.wanted[rows, :1] == iota((z.length, stream), 1))
        r.back_x[m] = mm_tn(pick, dx[rows]).astype(BF)
    pack_smalls(z, small, r)
    emit("qkv", lambda out: outer(r.n1, r.dq, out))


def pack_smalls(z, small, r):
    rows = (GROUPS * 8, z.width)
    vecs = jnp.concatenate([small.get(i, jnp.zeros((1, z.width), F32)) for i in range(8)], 0)
    spot = lambda shape, per, off=0: iota(shape, 0) // 8 == (iota(shape, 1) + off) // per
    ask = lambda cond: jnp.where(cond, 1.0, 0.0)
    per = z.width // GROUPS
    take = ask(iota((GROUPS * 8, 8), 0) % 8 == iota((GROUPS * 8, 8), 1))
    wide = exact(take, vecs, ((1,), (0,)))
    put = ask(iota((z.width, 128), 0) % per == iota((z.width, 128), 1))
    total = exact(jnp.where(spot(rows, per), wide, 0.0), put, ((1,), (0,)))
    per = z.ff // GROUPS
    for i in range(z.ff // tile):
        part = r.upb_sum[:, i * tile:(i + 1) * tile]
        shape = (GROUPS * 8, tile)
        mine = spot(shape, per, i * tile) & (iota(shape, 0) % 8 == UPB)
        put = ask((iota((tile, 128), 0) + i * tile) % per == iota((tile, 128), 1))
        total += exact(jnp.where(mine, jnp.broadcast_to(part, shape), 0.0), put, ((1,), (0,)))
    lanes = table_grad(r.table[...])
    width = z.length // NB
    per = NB // GROUPS
    far = lambda shape, dim: (z.length - 1 - iota(shape, dim)) // width
    shape = (GROUPS * 8, z.length)
    for k in range(per):
        mine = ask((iota(shape, 0) % 8 == REL) & (far(shape, 1) == iota(shape, 0) // 8 * per + k))
        by_head = exact(mine, lanes, ((1,), (1,)))
        put = ask(iota((HEADS, 128), 0) + k * HEADS == iota((HEADS, 128), 1))
        total += exact(by_head, put, ((1,), (0,)))
    r.small_grad[...] = total


class Refs:
    def __init__(self, names, refs):
        for n, ref in zip(names, refs): setattr(self, n, ref)


def weight_shapes(z):
    return {"qkv": (z.wide, 3 * z.att), "ao": (z.att, z.width), "cq": (z.wide, z.att), "kv": (z.wide, 2 * z.att),
            "co": (z.att, z.width), "up": (z.wide, z.ff), "dn": (z.ff, z.width)}


def saved_shapes(z):
    R = z.rows
    S = jax.ShapeDtypeStruct
    pairs = HEADS // 2
    return {"sp": S((z.width, z.wide), BF), "vec": S((SMALLS, z.width), F32), "ep": S((z.MB * z.keys, z.wide), BF),
            "ckv": S((z.MB * z.keys, 2 * z.att), BF), "x": S((R, z.width), F32), "n1": S((R, z.wide), BF),
            "join": S((R, 3 * z.att), BF), "ps": S((z.MB, pairs, 2 * z.length, z.length), F32), "a": S((R, z.att), BF),
            "h1": S((R, z.width), F32), "n2": S((R, z.wide), BF), "cq": S((R, z.att), BF),
            "pc": S((z.MB, pairs, 2 * z.win, z.keys), F32), "c": S((R, z.att), BF), "h2": S((R, z.width), F32),
            "n3": S((R, z.wide), BF), "gl": S((R, z.ff), BF), "slope": S((R, z.ff), F32), "ct": S((R, z.width), BF)}


def forward_plain(z, gathered, wanted, times, pool):
    names = list(gathered)
    saved = saved_shapes(z)
    outs = {**saved, "back_y": jax.ShapeDtypeStruct(gathered["tok"].shape, BF)}
    share = {"up": "qkv", "ct": "tok"}
    room = {k: gathered[k].shape for k in names if k not in share}
    room["qkv"] = gathered["up"].shape
    def kernel(*refs):
        n = len(names)
        held = dict(zip(names, refs[:n]))
        r = Refs(["wanted", "times", "pool"], refs[n:n + 3])
        r.__dict__.update(zip(outs, refs[n + 3:n + 3 + len(outs)]))
        scratch = refs[n + 3 + len(outs):]
        sems, r.bias, r.upb = scratch[:3]
        bufs = dict(zip(room, scratch[3:]))
        def view(k):
            return bufs["qkv"].at[:, :gathered[k].shape[1]] if k in ("qkv", "up") else bufs[share.get(k, k)]
        def copy(k):
            return pltpu.make_async_copy(held[k], view(k), sems.at[names.index(k)])
        for k in room:
            copy(k).start()
        def ready(k):
            if k in share:
                copy(k).start()
            copy(k).wait()
            return view(k)
        forward_steps(z, ready, r)
    V = pl.BlockSpec(memory_space=pltpu.VMEM)
    A = pl.BlockSpec(memory_space=pl.ANY)
    return dict(zip(outs, pl.pallas_call(kernel, name="layer_forward", out_shape=list(outs.values()),
        in_specs=[A] * len(names) + [V] * 3, out_specs=[V] * len(outs),
        scratch_shapes=[pltpu.SemaphoreType.DMA((len(names),)), pltpu.VMEM((HEADS, z.length, z.length), F32), pltpu.VMEM((1, z.ff), F32)]
            + [pltpu.VMEM(v, BF) for v in room.values()],
        compiler_params=pltpu.CompilerParams(vmem_limit_bytes=63 * MIB))(*gathered.values(), wanted, times, pool)))


def backward_plain(z, weights, saved, wanted, times):
    names = list(WEIGHTS)
    shapes = weight_shapes(z)
    ins = list(saved)
    S = jax.ShapeDtypeStruct
    outs = {"pool_grad": S((z.MB * z.keys, z.width), F32), "back_x": S((z.MB, z.stream, z.width), BF), "small_grad": S((GROUPS * 8, 128), F32)}
    part = z.keys // 2
    local = {"du": ((z.rows, z.ff), BF), "upb_sum": ((1, z.ff), F32), "dh": ((z.rows, z.width), F32), "e": ((z.rows, z.width), BF),
             "dc": ((z.rows, z.att), BF), "dcq": ((z.rows, z.att), BF), "dckv": ((z.MB * z.keys, 2 * z.att), BF),
             "table": ((z.length, HEADS * z.length), F32), "tiles": ((2, z.rows, tile), F32), "pool_tiles": ((2, part, z.width), F32)}
    kept = [k for k in names if k != "qkv"]

    def kernel(*refs):
        refs = list(refs)
        take = lambda k: [refs.pop(0) for _ in range(k)]
        held = dict(zip(names, take(len(names))))
        r = Refs(ins + ["wanted", "times"], take(len(ins) + 2))
        grads = dict(zip(names, take(len(names))))
        r.__dict__.update(zip(outs, take(len(outs))))
        sems, gsem, tsem, psem = take(4)
        bufs = dict(zip(kept, take(len(kept))))
        bufs["qkv"] = bufs["up"].at[:, :shapes["qkv"][1]]
        r.__dict__.update(zip(local, take(len(local))))
        r.dq = r.du.at[:, :3 * z.att]
        load = lambda k: pltpu.make_async_copy(held[k], bufs[k], sems.at[names.index(k)])
        store = lambda k: pltpu.make_async_copy(bufs[k], grads[k], gsem.at[names.index(k)])
        slope = lambda i: pltpu.make_async_copy(r.slope.at[:, i * tile:(i + 1) * tile], r.tiles.at[i % 2], tsem.at[i % 2])
        slope(0).start()
        for k in ("dn", "up", "co", "kv", "cq", "ao"):
            load(k).start()
        def slope_tile(i):
            if i + 1 < z.ff // tile:
                slope(i + 1).start()
            slope(i).wait()
            return r.tiles[i % 2]
        pool_copy = lambda i: pltpu.make_async_copy(r.pool_tiles.at[i % 2], r.pool_grad.at[i * part:(i + 1) * part], psem.at[i % 2])
        def put_pool(i, value):
            if i >= 2:
                pool_copy(i - 2).wait()
            r.pool_tiles[i % 2] = value
            pool_copy(i).start()
        r.slope_tile, r.put_pool = slope_tile, put_pool
        def ready(k):
            load(k).wait()
            return bufs[k]
        def emit(k, write):
            write(bufs[k])
            store(k).start()
            if k == "co":
                store("up").wait()
                load("qkv").start()
        backward_steps(z, ready, emit, r)
        for k in names:
            if k != "up":
                store(k).wait()
        for i in (z.MB * 2 - 2, z.MB * 2 - 1):
            pool_copy(i).wait()
    V = pl.BlockSpec(memory_space=pltpu.VMEM)
    A = pl.BlockSpec(memory_space=pl.ANY)
    D = pltpu.SemaphoreType.DMA
    res = pl.pallas_call(kernel, name="layer_backward", out_shape=[S(shapes[k], BF) for k in names] + list(outs.values()),
        in_specs=[A] * len(names) + [A if k == "slope" else V for k in ins] + [V] * 2, out_specs=[A] * (len(names) + 1) + [V] * 2,
        scratch_shapes=[D((len(names),)), D((len(names),)), D((2,)), D((2,))] + [pltpu.VMEM(shapes[k], BF) for k in kept]
            + [pltpu.VMEM(*v) for v in local.values()],
        compiler_params=pltpu.CompilerParams(vmem_limit_bytes=63 * MIB))(*[weights[k] for k in names], *saved.values(), wanted, times)
    return dict(zip(names, res)), dict(zip(outs, res[len(names):]))


MESH = pl.DeviceIdType.MESH

def when(pred, fn):
    if pred is None: fn()
    else: pl.when(pred)(fn)

def both(a, b):
    if a is None: return b
    if b is None: return a
    return jnp.logical_and(a, b)

class Place:
    def __init__(self, nz):
        dp, fs = lax.axis_index("dp"), lax.axis_index("fsdp")
        self.nz = nz
        self.y, self.x = dp // 2, lax.rem(dp, 2)
        self.z, self.c = fs // 2, lax.rem(fs, 2)
        y, x, z, c = self.y, self.x, self.z, self.c
        self.y1, self.x1 = y + c * (1 - 2 * y), x + (1 - c) * (1 - 2 * x)
        self.y2, self.x2 = y + (1 - c) * (1 - 2 * y), x + c * (1 - 2 * x)
        self.yo, self.xo = 1 - y, 1 - x
        self.first = {"dp": self.y1 * 2 + self.x1, "fsdp": fs}
        self.second = {"dp": self.y2 * 2 + self.x2, "fsdp": fs}
        self.pair = {"dp": dp, "fsdp": z * 2 + 1 - c}
        self.up = {"dp": dp, "fsdp": fs + 2}
        self.down = {"dp": dp, "fsdp": fs - 2}
        self.has_up, self.has_down = z < nz - 1, z > 0

    def barrier(self):
        bar = pltpu.get_barrier_semaphore()
        ways = [(None, self.pair), (None, self.first), (None, self.second), (self.has_up, self.up), (self.has_down, self.down)]
        for pred, dev in ways:
            when(pred, lambda dev=dev: pl.semaphore_signal(bar, inc=1, device_id=dev, device_id_type=MESH))
        pl.semaphore_wait(bar, 3 + jnp.minimum(self.z, 1) + jnp.minimum(self.nz - 1 - self.z, 1))

class Gather:
    def __init__(self, at, block, out, sems, line_only=False):
        self.at, self.block, self.out, self.line_only = at, block, out, line_only
        self.zs, self.zr, self.ps, self.pr, self.own = sems
        self.late = []

    def cell(self, z, c):
        p = self.at
        return self.out.at[:, z, c] if self.line_only else self.out.at[p.y, p.x, z, c]
    def line(self, y, x, c):
        return self.out.at[:, :, c] if self.line_only else self.out.at[y, x, :, c]
    def copy(self, src, dst, s, r, dev):
        return pltpu.make_async_remote_copy(src_ref=src, dst_ref=dst, send_sem=s, recv_sem=r, device_id=dev, device_id_type=MESH)
    def send(self, pred, src, dst, s, r, dev):
        def go():
            self.copy(src, dst, s, r, dev).start()
        when(pred, go)
        def done():
            self.copy(src, dst, s, r, dev).wait_send()
        self.late.append((pred, done))
    def arrived(self, pred, ref, s, r):
        when(pred, lambda: self.copy(ref, ref, s, r, self.at.pair).wait_recv())

    def start(self):
        p = self.at
        mine = self.cell(p.z, p.c)
        pltpu.make_async_copy(self.block, mine, self.own).start()
        self.send(p.has_up, self.block, mine, self.zs.at[0, 0], self.zr.at[0, 0], p.up)
        self.send(p.has_down, self.block, mine, self.zs.at[1, 0], self.zr.at[1, 0], p.down)
    def along_z(self):
        p = self.at
        for j in range(1, p.nz):
            below, above = p.z >= j, p.z < p.nz - j
            ref = self.cell(p.z - j, p.c)
            self.arrived(below, ref, self.zs.at[0, j - 1], self.zr.at[0, j - 1])
            if j < p.nz - 1:
                self.send(both(below, p.has_up), ref, ref, self.zs.at[0, j], self.zr.at[0, j], p.up)
            ref = self.cell(p.z + j, p.c)
            self.arrived(above, ref, self.zs.at[1, j - 1], self.zr.at[1, j - 1])
            if j < p.nz - 1:
                self.send(both(above, p.has_down), ref, ref, self.zs.at[1, j], self.zr.at[1, j], p.down)
        pltpu.make_async_copy(self.block, self.cell(p.z, p.c), self.own).wait()
        mine = self.line(p.y, p.x, p.c)
        self.send(None, mine, mine, self.ps.at[0], self.pr.at[0], p.pair)
        if not self.line_only:
            self.send(None, mine, mine, self.ps.at[4], self.pr.at[4], p.first)
            self.send(None, mine, mine, self.ps.at[5], self.pr.at[5], p.second)
    def after_first(self):
        p = self.at
        if self.line_only: return
        got = self.line(p.y1, p.x1, p.c)
        self.arrived(None, got, self.ps.at[4], self.pr.at[4])
        self.send(None, got, got, self.ps.at[6], self.pr.at[6], p.second)
        self.send(None, got, got, self.ps.at[1], self.pr.at[1], p.pair)
    def after_second(self):
        p = self.at
        if self.line_only: return
        for k, (y, x) in enumerate(((p.y2, p.x2), (p.yo, p.xo))):
            got = self.line(y, x, p.c)
            self.arrived(None, got, self.ps.at[5 + k], self.pr.at[5 + k])
            self.send(None, got, got, self.ps.at[2 + k], self.pr.at[2 + k], p.pair)
    def whole(self):
        p = self.at
        lines = [(p.y, p.x)] if self.line_only else [(p.y, p.x), (p.y2, p.x2), (p.y1, p.x1), (p.yo, p.xo)]
        for k, (y, x) in enumerate(lines):
            self.arrived(None, self.line(y, x, 1 - p.c), self.ps.at[k], self.pr.at[k])
    def drain(self):
        for pred, done in self.late:
            when(pred, done)

def sem_shapes(n, nz):
    D = pltpu.SemaphoreType.DMA
    return [D((n, 2, nz)), D((n, 2, nz)), D((n, 8)), D((n, 8)), D((n,))]


def pad16(r):
    return (r + 15) // 16 * 16


SENDS = (("small", 1), ("kv", 2), ("tok", 1), ("qkv", 3), ("ao", 1), ("cq", 1), ("co", 1), ("up", 4), ("dn", 2), ("ct", 1))
lines_only = ("tok", "ct")


def piece(ref, name, c, cut):
    if cut == 1:
        return ref
    lead = (slice(None),) * (len(ref.shape) - 2)
    if name == "dn":
        tiles = ref.shape[-2] // 16
        return ref.at[lead + (slice(tiles * c // cut * 16, tiles * (c + 1) // cut * 16),)]
    cols = ref.shape[-1] // cut
    return ref.at[lead + (slice(None), slice(c * cols, (c + 1) * cols))]


def gather_kernel(n, nz, pieces, ahead, *refs):
    blocks, outs, stage = refs[:n], refs[n:2 * n], refs[2 * n:3 * n]
    zs, zr, ps, pr, own = refs[3 * n:]
    at = Place(nz)
    for b, s in zip(blocks, stage):
        if s.shape == b.shape:
            s[...] = b[...]
        else:
            s[...] = jnp.zeros(s.shape, s.dtype)
            s[:b.shape[0], :] = b[...]
    at.barrier()
    gs = []
    for i, (k, cut) in enumerate(pieces):
        for c in range(cut):
            part = lambda ref: piece(ref, k, c, cut)
            j = len(gs)
            gs.append(Gather(at, part(stage[i]), part(outs[i]), [s.at[j] for s in (zs, zr, ps, pr, own)], k in lines_only))
    for g in gs[:ahead]:
        g.start()
    for t in range(len(gs) + 2):
        if t + ahead < len(gs):
            gs[t + ahead].start()
        if t < len(gs):
            gs[t].along_z()
        if 1 <= t <= len(gs):
            gs[t - 1].after_first()
        if 2 <= t:
            gs[t - 2].after_second()
    for g in gs:
        g.whole()
    for g in gs:
        g.drain()


def gather_named(arrays, z, nz):
    pieces = SENDS
    names = [k for k, _ in pieces]
    n, total = len(names), sum(cut for _, cut in pieces)
    blocks = [arrays[k] for k in names]
    outs, stages = [], []
    for k, b in zip(names, blocks):
        if k in lines_only:
            outs.append(jax.ShapeDtypeStruct((b.shape[0], nz, 2) + b.shape[1:], b.dtype))
            stages.append(pltpu.VMEM(b.shape, b.dtype))
        else:
            r = pad16(b.shape[0])
            outs.append(jax.ShapeDtypeStruct((2, 2, nz, 2, r, b.shape[1]), b.dtype))
            stages.append(pltpu.VMEM((r, b.shape[1]), b.dtype))
    got = pl.pallas_call(partial(gather_kernel, n, nz, pieces, 2), name="gather_weights", out_shape=outs,
        in_specs=[pl.BlockSpec(memory_space=pltpu.VMEM)] * n, out_specs=[pl.BlockSpec(memory_space=pl.ANY)] * n,
        scratch_shapes=stages + sem_shapes(total, nz),
        compiler_params=pltpu.CompilerParams(collective_id=1, has_side_effects=True, vmem_limit_bytes=40 * MIB))(*blocks)
    flat = lambda k, v: v.reshape(v.shape[0], -1, v.shape[-1]) if k in lines_only else v.reshape(-1, v.shape[-1])
    return {k: flat(k, v) for k, v in zip(names, got)}


def scatter_named(lines, small, grads, shards, z, nz):
    S = jax.ShapeDtypeStruct
    tok = z.length // 2
    as_line = lambda v: v.reshape(z.MB, nz, 2, tok, z.width)
    as_blocks = lambda v: v.reshape(2, 2, nz, 2, v.shape[0] // GROUPS, v.shape[1])
    order = ["dn", "up", "co", "kv", "cq", "ao", "qkv"]
    srcs = [as_line(lines["y"])] + [as_blocks(grads[k]) for k in order] + [as_blocks(small), as_line(lines["x"])]
    line = [True] + [False] * 8 + [True]
    outs = [S((z.MB, tok, z.width), BF)] + [S(shards[k].shape, F32) for k in order] + [S((8, 128), F32), S((z.MB, tok, z.width), BF)]
    got = scatter_all(srcs, line, outs, nz)
    return got[0], got[-1], got[-2], dict(zip(order, got[1:-2]))


class Scatter:
    def __init__(self, at, src, out, bufs, sems, line_only=False):
        self.at, self.src, self.out, self.line_only = at, src, out, line_only
        if line_only: self.acc, self.rc, self.ru, self.rd = bufs
        else: self.acc, self.rc, self.r2, self.r1, self.ru, self.rd = bufs
        self.ps, self.pr, self.us, self.ur, self.ds, self.dr, self.own = sems
        self.late = []
    def copy(self, src, dst, s, r, dev):
        return pltpu.make_async_remote_copy(src_ref=src, dst_ref=dst, send_sem=s, recv_sem=r, device_id=dev, device_id_type=MESH)
    def send(self, pred, src, dst, s, r, dev):
        when(pred, lambda: self.copy(src, dst, s, r, dev).start())
        self.late.append((pred, lambda: self.copy(src, dst, s, r, dev).wait_send()))
    def arrived(self, ref, s, r):
        self.copy(ref, ref, s, r, self.at.pair).wait_recv()
    def add(self, mine, theirs):
        lead = mine.shape[:-2]
        count = 1
        for n in lead: count *= n
        def step(i, carry):
            at, rest = [], i
            for n in reversed(lead):
                at.append(lax.rem(rest, n)); rest = rest // n
            at = tuple(reversed(at))
            mine[at] = (mine[at].astype(F32) + theirs[at].astype(F32)).astype(mine.dtype)
            return carry
        lax.fori_loop(0, count, step, 0)
    def part(self, c):
        return self.src.at[:, :, c] if self.line_only else self.src.at[:, :, :, c]
    def start(self):
        p = self.at
        pltpu.make_async_copy(self.part(p.c), self.acc, self.own).start()
        self.send(None, self.part(1 - p.c), self.rc, self.ps.at[0], self.pr.at[0], p.pair)
    def after_pair(self):
        p = self.at
        pltpu.make_async_copy(self.part(p.c), self.acc, self.own).wait()
        self.arrived(self.rc, self.ps.at[0], self.pr.at[0])
        if self.line_only:
            self.add(self.acc, self.rc)
            return
        for k, (y, x) in enumerate(((p.y2, p.x2), (p.yo, p.xo))):
            self.add(self.acc.at[y, x], self.rc.at[y, x])
            self.send(None, self.acc.at[y, x], self.r2.at[k], self.ps.at[1 + k], self.pr.at[1 + k], p.second)
        for y, x in ((p.y1, p.x1), (p.y, p.x)):
            self.add(self.acc.at[y, x], self.rc.at[y, x])
    def after_second(self):
        p = self.at
        if self.line_only: return
        self.arrived(self.r2.at[1], self.ps.at[2], self.pr.at[2])
        self.add(self.acc.at[p.y1, p.x1], self.r2.at[1])
        self.send(None, self.acc.at[p.y1, p.x1], self.r1, self.ps.at[3], self.pr.at[3], p.first)
        self.arrived(self.r2.at[0], self.ps.at[1], self.pr.at[1])
        self.add(self.acc.at[p.y, p.x], self.r2.at[0])
    def after_first(self):
        p = self.at
        if self.line_only: return
        self.arrived(self.r1, self.ps.at[3], self.pr.at[3])
        self.add(self.acc.at[p.y, p.x], self.r1)
    def cell(self, z):
        return self.acc.at[:, z] if self.line_only else self.acc.at[self.at.y, self.at.x, z]
    def z_step(self, h):
        p, nz = self.at, self.at.nz
        for j in range(nz - h, 0, -1):
            here = p.z == h - 1
            if h > 1:
                def up():
                    self.arrived(self.ru.at[j], self.us.at[j + 1], self.ur.at[j])
                    self.add(self.cell(h - 1 + j), self.ru.at[j])
                when(here, up)
            self.send(here, self.cell(h - 1 + j), self.ru.at[j - 1], self.us.at[j], self.ur.at[j - 1], p.up)
            here = p.z == nz - h
            if h > 1:
                def down():
                    self.arrived(self.rd.at[j], self.ds.at[j + 1], self.dr.at[j])
                    self.add(self.cell(nz - h - j), self.rd.at[j])
                when(here, down)
            self.send(here, self.cell(nz - h - j), self.rd.at[j - 1], self.ds.at[j], self.dr.at[j - 1], p.down)
    def finish(self):
        p = self.at
        mine = self.cell(p.z)
        def up():
            self.arrived(self.ru.at[0], self.us.at[1], self.ur.at[0])
            self.add(mine, self.ru.at[0])
        when(p.has_down, up)
        def down():
            self.arrived(self.rd.at[0], self.ds.at[1], self.dr.at[0])
            self.add(mine, self.rd.at[0])
        when(p.has_up, down)
        if self.line_only: self.out[...] = mine[...].astype(self.out.dtype)
        else: self.out[...] = mine[...][:self.out.shape[0]].astype(self.out.dtype)
    def drain(self):
        for pred, done in self.late: when(pred, done)

def rs_bufs(src, line_only, nz):
    V = pltpu.VMEM
    if line_only:
        m, _, _, r, n = src.shape
        return [V((m, nz, r, n), src.dtype), V((m, nz, r, n), src.dtype), V((nz - 1, m, r, n), src.dtype), V((nz - 1, m, r, n), src.dtype)]
    r, n = src.shape[-2:]
    b = (r, n)
    return [V((2, 2, nz) + b, src.dtype), V((2, 2, nz) + b, src.dtype), V((2, nz) + b, src.dtype), V((nz,) + b, src.dtype), V((nz - 1,) + b, src.dtype), V((nz - 1,) + b, src.dtype)]

def scatter_kernel(n, nz, line_only, ahead, *refs):
    refs = list(refs)
    take = lambda k: [refs.pop(0) for _ in range(k)]
    srcs, outs = take(n), take(n)
    bufs = [take(4 if lo else 6) for lo in line_only]
    sems = take(7)
    at = Place(nz)
    at.barrier()
    ss = [Scatter(at, srcs[i], outs[i], bufs[i], [s.at[i] for s in sems], line_only[i]) for i in range(n)]
    for s in ss[:ahead]: s.start()
    for t in range(n + nz + 2):
        def stage(k): return ss[t - k] if 0 <= t - k < n else None
        if t + ahead < n: ss[t + ahead].start()
        if stage(0): stage(0).after_pair()
        if stage(1): stage(1).after_second()
        if stage(2):
            stage(2).after_first(); stage(2).z_step(1)
        for h in range(2, nz):
            if stage(h + 1): stage(h + 1).z_step(h)
        if stage(nz + 1): stage(nz + 1).finish()
    for s in ss: s.drain()

def scatter_all(srcs, line_only, outs, nz, ahead=2, name="scatter_grads", cid=2):
    n = len(srcs)
    D = pltpu.SemaphoreType.DMA
    scratch = [b for s, lo in zip(srcs, line_only) for b in rs_bufs(s, lo, nz)]
    return pl.pallas_call(partial(scatter_kernel, n, nz, line_only, ahead), name=name, out_shape=outs,
        in_specs=[pl.BlockSpec(memory_space=pl.ANY)] * n, out_specs=[pl.BlockSpec(memory_space=pltpu.VMEM)] * n,
        scratch_shapes=scratch + [D((n, 4)), D((n, 4)), D((n, nz + 1)), D((n, nz + 1)), D((n, nz + 1)), D((n, nz + 1)), D((n,))],
        compiler_params=pltpu.CompilerParams(collective_id=cid, has_side_effects=True, vmem_limit_bytes=63 * MIB))(*srcs)


def vectors(norm1_gain, norm2_gain, norm3_gain, attn_out_bias, cca_out_bias, ffw_down_bias, rel_table, ffw_up_bias):
    return [norm1_gain, norm2_gain, norm3_gain, attn_out_bias, cca_out_bias, ffw_down_bias, rel_table, ffw_up_bias]


def to_groups(v):
    small = v.shape[0] // GROUPS
    big = (small + 15) // 16 * 16
    return jnp.pad(v.reshape(GROUPS, small, -1), ((0, 0), (0, big - small), (0, 0))).reshape(GROUPS * big, -1)


def from_groups(v, rows):
    return v.reshape(GROUPS, v.shape[0] // GROUPS, -1)[:, :rows // GROUPS].reshape(rows, -1)


def body(tokens, cotangent, lengths, deal, pool, neighbour_ids, norm1_gain, attn_qkv, attn_out, attn_out_bias, rel_table,
         norm2_gain, cca_query, cca_kv, cca_out, cca_out_bias, norm3_gain, ffw_up, ffw_up_bias, ffw_down, ffw_down_bias):
    members, member = lax.axis_size("fsdp"), lax.axis_index("fsdp")
    devices = members * lax.axis_size("dp")
    MB, tok_rows, width = tokens.shape
    length = 2 * tok_rows
    z = Sizes(MB, length, width, HEADS * HEAD_DIM, ffw_up.shape[1], pool.shape[1])
    z.stream = members * tok_rows
    shards = {"qkv": attn_qkv, "ao": attn_out, "cq": cca_query, "kv": cca_kv, "co": cca_out, "up": ffw_up, "dn": ffw_down}
    vecs = vectors(norm1_gain, norm2_gain, norm3_gain, attn_out_bias, cca_out_bias, ffw_down_bias, rel_table, ffw_up_bias)

    ids = jnp.arange(members, dtype=jnp.int32)
    lens, dealt = lengths[:, 0], deal[:, 0]
    starts = jnp.sum(jnp.where(ids[None, :, None] > ids[None, None, :], lens[:, None, :], 0), 2)
    mine = dealt == member
    own_start = jnp.sum(jnp.where(mine, starts, 0), 1)
    own_len = jnp.sum(jnp.where(mine, lens, 0), 1)
    place = jnp.arange(length, dtype=jnp.int32)
    wanted = jnp.where(place[None] < own_len[:, None], own_start[:, None] + place[None], -1).reshape(-1)
    wanted = jnp.broadcast_to(wanted[:, None], (MB * length, 128))
    spans = length // CH
    ids3 = neighbour_ids.reshape(MB, spans, K_NB)
    held = jnp.sum((ids3[..., None] == jnp.arange(z.pool, dtype=jnp.int32)).astype(F32), 2)
    row = jnp.arange(low_row, length, dtype=jnp.int32)
    in_span = ((row[:, None] - (CH - 1)) // CH == jnp.arange(spans, dtype=jnp.int32)) & (row[:, None] >= CH - 1)
    times = jnp.sum(jnp.where(in_span[None, :, :, None], held[:, None], 0.0), 2)
    times = jnp.broadcast_to(times[..., None], times.shape + (NL,)).reshape(MB, z.win, z.keys)
    neighbours = pool.reshape(MB * z.keys, width)

    direct = lax.axis_size("dp") == 4 and members % 2 == 0 and devices == GROUPS
    nz = members // 2
    if direct:
        packed = jnp.concatenate([jnp.pad(v[None], ((0, 0), (0, 128 - v.shape[0]))) for v in vecs] + [jnp.zeros((SMALLS - 8, 128), BF)], 0)
        gathered = gather_named({"small": packed, "tok": tokens, "ct": cotangent, **shards}, z, nz)
    else:
        whole = lambda v: lax.all_gather(v, ("dp", "fsdp"), axis=0, tiled=True)
        rows = [jnp.pad(w, ((0, 0), (0, 128 - w.shape[1])))[:, None] for w in [whole(v).reshape(GROUPS, -1) for v in vecs]]
        packed = jnp.concatenate(rows + [jnp.zeros((GROUPS, SMALLS - 8, 128), BF)], 1).reshape(GROUPS * SMALLS, 128)
        gathered = {"small": packed, **{k: to_groups(whole(v)) for k, v in shards.items()},
                    "tok": lax.all_gather(tokens, "fsdp", axis=1, tiled=True), "ct": lax.all_gather(cotangent, "fsdp", axis=1, tiled=True)}
    saved = forward_plain(z, gathered, wanted, times, neighbours)
    back_y = saved.pop("back_y")
    grads, outs = backward_plain(z, {k: gathered[k] for k in WEIGHTS}, saved, wanted, times)
    back_x, small = outs["back_x"], outs["small_grad"]
    if direct:
        lines = {"y": back_y, "x": back_x}
        act, dx, small, mine = scatter_named(lines, small, grads, shards, z, nz)
        parts = [small[i, :v.shape[0]] for i, v in enumerate(vecs)]
    else:
        down = lambda v: lax.psum_scatter(v.astype(F32), ("dp", "fsdp"), scatter_dimension=0, tiled=True)
        line = lambda v: lax.psum_scatter(v, "fsdp", scatter_dimension=1, tiled=True)
        act, dx = line(back_y), line(back_x)
        mine = {k: down(from_groups(grads[k], shards[k].shape[0] * devices)) for k in shards}
        small = small.reshape(GROUPS, 8, 128)
        parts = [down(small[:, i, :v.shape[0] * devices // GROUPS].reshape(-1)) for i, v in enumerate(vecs)]
    g1, g2, g3, ba, bc, bd, rel, upb = parts
    return (act, dx, outs["pool_grad"].reshape(pool.shape), g1, mine["qkv"], mine["ao"], ba, rel, g2, mine["cq"], mine["kv"],
            mine["co"], bc, g3, mine["up"], upb, mine["dn"], bd)


def solution(mesh):
    everywhere = ("dp", "fsdp")
    rows, vec = P(everywhere, None), P(everywhere)
    slots = P(None, everywhere, None)
    return jax.shard_map(
        body,
        mesh=mesh,
        in_specs=(slots, slots, P(None, "dp", None), P(None, "dp", None), P(None, everywhere, None, None), slots,
                  vec, rows, rows, vec, vec, vec, rows, rows, rows, vec, vec, rows, vec, rows, vec),
        out_specs=(slots, slots, P(None, everywhere, None, None), vec, rows, rows, vec, vec, vec, rows, rows, rows, vec, vec,
                   rows, vec, rows, vec),
        check_vma=False,
    )
```

time: 1590 us -> 516 us (0.32)
  the two profiles are of different devices: /device:TPU:5 before, /device:TPU:0 now
where the time goes in v1:
time: 516 us; the launch traced here: 507 us
  Pallas kernels  465 us (90%)
  local copies, waits for them, and re-layouts  37.4 us (7%)
    pallas_call x1, Pallas kernels, scatter_all(): pl.pallas_call(partial(scatter_kernel, n, nz, line_only, ahead), name=nam...  171 us
    pallas_call x1, Pallas kernels, gather_named(): pl.pallas_call(partial(gather_kernel, n, nz, pieces, 2), name='gather_wei...  154 us
    pallas_call x1, Pallas kernels, backward_plain(): pl.pallas_call(kernel, name='layer_backward', out_shape=[S(shapes[k], BF)...  87 us
    pallas_call x1, Pallas kernels, forward_plain(): pl.pallas_call(kernel, name='layer_forward', out_shape=list(outs.values()...  52.9 us
    unnamed x47, local copies, waits for them, and re-layouts  26.2 us

profile of v1, /device:TPU:0, one launch (start us, length us, event | category | flops | bytes accessed | tf_op | source)
XLA Modules:
  0.0 506.7 jit_solution(4670128049310917252)
XLA Ops:
  6.7 0.8 select_reduce_fusion
  7.5 0.8 fusion.2
  8.4 0.8 fusion
  9.6 0.8 broadcast_in_dim.114.refs_10_.refs_26_
  10.6 0.8 reshape.250.refs_11_.refs_27_
  11.4 0.9 copy-done.5
  12.3 0.9 copy-done.6
  13.3 0.9 copy-done.7
  14.2 0.9 copy-done.8
  15.1 0.9 copy-done.9
  16.1 0.9 copy-done.11
  17.0 0.8 copy-done.12
  17.8 0.8 copy-done.13
  18.6 0.8 copy-done.14
  19.4 153.7 %gather_weights.1 = (bf16[2,2,4,2,16,128]{5,4,3,2,1,0:T(8,128)(2,1)S(1)}, bf16[2,2,4,2,32,2048]{5,4,3,2,1,0:T(8,128)(2,1)}, bf16[2,4,2,64,896]{4,3,2,1,0:T(8,128...) custom-call(bf16[16,128]{1,0:T(8,128)(2,1)S(1)} %concatenate.3.refs_, ...), custom_call_target="tpu_custom_call" | custom-call | tf_op jit(solution)/shard_map/gather_weights/pallas_call | solution.py:698
  173.1 1.3 copy-done
  174.5 1.2 copy-done.1
  175.7 1.3 copy-done.2
  177.0 1.2 copy-done.3
  178.3 1.3 copy-done.4
  180.2 52.9 %layer_forward.1 = (bf16[896,1024]{1,0:T(8,128)(2,1)}, f32[16,896]{1,0:T(8,128)}, bf16[768,1024]{1,0:T(8,128)(2,1)}, bf16[768,2048]{1,0:T(8,128)(2,1)}, f32[256,...) custom-call(bf16[512,128]{1,0:T(8,128)(2,1)} %bitcast.64, ...), custom_call_target="tpu_custom_call" | custom-call | tf_op jit(solution)/shard_map/layer_forward/pallas_call | solution.py:446
  233.1 87.0 %layer_backward.1 = (bf16[1024,3072]{1,0:T(8,128)(2,1)}, bf16[1024,896]{1,0:T(8,128)(2,1)}, bf16[1024,1024]{1,0:T(8,128)(2,1)}, bf16[1024,2048]{1,0:T(8,128)(2,1...) custom-call(bf16[1024,3072]{1,0:T(8,128)(2,1)} %bitcast.70, ...), custom_call_target="tpu_custom_call" | custom-call | tf_op jit(solution)/shard_map/layer_backward/pallas_call | solution.py:513
  320.1 171.2 %scatter_grads.1 = (bf16[2,64,896]{2,1,0:T(8,128)(2,1)}, f32[112,896]{1,0:T(8,128)}, f32[28,3584]{1,0:T(8,128)}, f32[32,896]{1,0:T(8,128)}, f32[28,2048]{1,0:T(8...) custom-call(bf16[2,4,2,64,896]{4,3,2,1,0:T(8,128)(2,1)} %bitcast.78,, ...), custom_call_target="tpu_custom_call" | custom-call | tf_op jit(solution)/shard_map/scatter_grads/pallas_call | solution.py:846
  491.4 1.3 slice_bitcast_fusion.5
  492.6 1.2 slice_bitcast_fusion.1
  493.8 1.4 slice_bitcast_fusion
  495.2 1.6 copy.53
  496.9 1.6 copy.54
  498.5 1.8 copy.55
  500.3 1.6 copy.56
  501.9 1.6 copy.57
  504.8 0.8 copy.60
  (47 shorter events, 9.5 us)
Async XLA Ops:
  11.4 0.9 copy-start.5
  12.3 0.9 copy-start.6
  13.3 0.9 copy-start.7
  14.2 0.9 copy-start.8
  15.1 0.9 copy-start.9
  16.1 0.9 copy-start.11
  17.0 0.8 copy-start.12
  17.8 0.8 copy-start.13
  18.6 0.8 copy-start.14
  173.1 1.4 copy-start
  174.5 1.2 copy-start.1
  175.7 1.3 copy-start.2
  177.0 1.2 copy-start.3
  178.3 1.3 copy-start.4
  179.5 0.7 copy-start.10
  491.3 12.1 %copy-start.17 = (f32[28,2048]{1,0:T(8,128)S(1)}, f32[28,2048]{1,0:T(8,128)}, u32[]{:S(2)}) copy-start(f32[28,2048]{1,0:T(8,128)} %get-tuple-element.154) | copy-start | bytes 688132
  491.3 12.8 %copy-start.18 = (f32[32,896]{1,0:T(8,128)S(1)}, f32[32,896]{1,0:T(8,128)}, u32[]{:S(2)}) copy-start(f32[32,896]{1,0:T(8,128)} %get-tuple-element.155) | copy-start | bytes 344068
  491.3 13.4 %copy-start.15 = (f32[28,3584]{1,0:T(8,128)S(1)}, f32[28,3584]{1,0:T(8,128)}, u32[]{:S(2)}) copy-start(f32[28,3584]{1,0:T(8,128)} %get-tuple-element.158) | copy-start | bytes 1204228
  491.3 14.2 %copy-start.16 = (f32[112,896]{1,0:T(8,128)S(1)}, f32[112,896]{1,0:T(8,128)}, u32[]{:S(2)}) copy-start(f32[112,896]{1,0:T(8,128)} %get-tuple-element.160) | copy-start | bytes 1204228

commit v2 on v1

--- a/solution.py
+++ b/solution.py
@@ -111,13 +111,16 @@
     return jnp.where(iota((n, v.shape[1]), 1) < HEAD_DIM, v[:n], v[n:])
 
 
-def head_loop(count, body):
+def head_parts(count, parts, body):
     pairs = HEADS // 2
+    total = count * pairs
     def step(i, carry):
         m, p = i // pairs, i % pairs
         body(m, p, p * 2 * HEAD_DIM)
         return carry
-    lax.fori_loop(0, count * pairs, step, 0, unroll=2)
+    for k in range(parts):
+        lax.fori_loop(total * k // parts, total * (k + 1) // parts, step, 0, unroll=2)
+        yield
 
 
 class Sizes:
@@ -140,7 +143,7 @@
         soft = e * (1.0 / jnp.sum(e, -1, keepdims=True))
         ps[m, p] = soft
         att[rows, at(0)] = joined(mm(soft.astype(BF), v)).astype(BF)
-    head_loop(z.MB, body)
+    yield from head_parts(z.MB, 4, body)
 
 
 def fwd_cross(z, cq, ckv, times, pc, c_out):
@@ -160,7 +163,7 @@
         soft = e * (1.0 / jnp.where(total > 0, total, 1.0))
         pc[m, p] = soft
         c_out[rows, at(0)] = joined(mm((soft.astype(BF).astype(F32) * cnt).astype(BF), v)).astype(BF)
-    head_loop(z.MB, body)
+    yield from head_parts(z.MB, 4, body)
 
 
 def gelu_parts(u):
@@ -170,35 +173,32 @@
     return u * half, half + 0.5 * u * (1.0 - t * t) * k * (1.0 + 3 * 0.044715 * u * u)
 
 
-def fwd_up(z, n3, up, upb, gl, slope):
-    def body(i):
-        at = columns(i, tile)
-        u = mm(n3[...], up[:, at]) + upb[:, at]
-        value, d = gelu_parts(u)
-        gl[:, at] = value.astype(BF)
-        slope[:, at] = d
-    loop(z.ff // tile, body)
+def fwd_up(z, n3, up, upb, gl, slope, at):
+    u = mm(n3[...], up[:, at]) + upb[:, at]
+    value, d = gelu_parts(u)
+    gl[:, at] = value.astype(BF)
+    slope[:, at] = d
 
 
 def project(left, weight, out, size=tile):
-    def body(i):
-        at = columns(i, size)
+    for i in range(out.shape[1] // size):
+        at = slice(i * size, (i + 1) * size)
         out[:, at] = mm(left[...], weight[:, at]).astype(out.dtype)
-    loop(out.shape[1] // size, body)
+        yield
 
 
 def project_nt(left, weight, out, size=tile):
-    def body(i):
-        at = columns(i, size)
+    for i in range(out.shape[1] // size):
+        at = slice(i * size, (i + 1) * size)
         out[:, at] = mm_nt(left[...], weight[at, :]).astype(out.dtype)
-    loop(out.shape[1] // size, body)
+        yield
 
 
 def outer(left, right, out, size=256):
-    def body(i):
-        at = columns(i, size)
+    for i in range(out.shape[0] // size):
+        at = slice(i * size, (i + 1) * size)
         out[at, :] = mm_tn(left[:, at], right[...]).astype(out.dtype)
-    loop(out.shape[0] // size, body)
+        yield
 
 
 def bwd_self(z, join, ps, da, dq, table_sum):
@@ -218,7 +218,7 @@
         for k in range(2):
             heads = pl.ds(pl.multiple_of((2 * p + k) * z.length, 128), z.length)
             table_sum[:, heads] += wide[k * z.length:(k + 1) * z.length]
-    head_loop(z.MB, body)
+    yield from head_parts(z.MB, 4, body)
 
 
 def bwd_cross(z, cq, ckv, times, pc, dc, dcq, dckv):
@@ -241,7 +241,7 @@
         dcq[rows, at(0)] = (joined(mm(ds, k)) * factor).astype(BF)
         dckv[keys, at(0)] = (mm_tn(ds, halves(q)) * factor).astype(BF)
         dckv[keys, at(1)] = mm_tn(pb, d).astype(BF)
-    head_loop(z.MB, body)
+    yield from head_parts(z.MB, 4, body)
 
 
 def exact(a, b, dims):
@@ -264,10 +264,13 @@
 
 
 def forward_steps(z, ready, r):
-    sp = spread(z.width)
-    r.sp[...] = sp
+    yield "small"
+    r.sp[...] = spread(z.width)
+    r.save("sp")
     packed = ready("small")[...]
     r.vec[...] = small_rows(packed, z.width)
+    r.save("vec")
+    yield
     def upb(i):
         at = columns(i, tile)
         per = z.ff // GROUPS
@@ -278,88 +281,157 @@
         r.upb[:, at] = jnp.sum(jnp.where(mine, placed, 0.0), 0, keepdims=True)
     loop(z.ff // tile, upb)
     biases(table_rows(packed, z.length), r.bias)
+    half = z.keys // 2
+    for i in range(z.MB * 2):
+        rows = slice(i * half, (i + 1) * half)
+        r.ep[rows, :] = mm(r.pool[rows, :], r.sp[...]).astype(BF)
+        yield
+    r.save("ep")
+    yield "kv"
     kv = ready("kv")
-    half = z.keys // 2
-    def pool_part(i):
-        rows = pl.ds(pl.multiple_of(i * half, 64), half)
-        r.ep[rows, :] = mm(r.pool[rows, :], r.sp[...]).astype(BF)
-    loop(z.MB * 2, pool_part)
-    project(r.ep, kv, r.ckv, 256)
+    yield from project(r.ep, kv, r.ckv, 256)
+    r.save("ckv")
+    yield "tok"
     tok = ready("tok")
     stream = tok.shape[1]
     for m in range(z.MB):
         rows = slice(m * z.length, (m + 1) * z.length)
         pick = onehot(r.wanted[rows, :1] == iota((z.length, stream), 1))
         r.x[rows] = mm(pick, tok[m])
-    x = r.x[...]
-    r.n1[...] = mm(norm(x, r.vec[G1:G1 + 1]), r.sp[...]).astype(BF)
-    project(r.n1, ready("qkv"), r.join)
-    fwd_self(z, r.join, r.bias, r.ps, r.a)
-    h1 = x + (mm(r.a[...], ready("ao")[...]) + r.vec[BA:BA + 1])
+    r.save("x")
+    yield
+    r.n1[...] = mm(norm(r.x[...], r.vec[G1:G1 + 1]), r.sp[...]).astype(BF)
+    r.save("n1")
+    yield "qkv"
+    yield from project(r.n1, ready("qkv"), r.join)
+    r.save("join")
+    yield from fwd_self(z, r.join, r.bias, r.ps, r.a)
+    r.save("ps")
+    r.save("a")
+    yield "ao"
+    h1 = r.x[...] + (mm(r.a[...], ready("ao")[...]) + r.vec[BA:BA + 1])
     r.h1[...] = h1
+    r.save("h1")
     r.n2[...] = mm(norm(h1, r.vec[G2:G2 + 1]), r.sp[...]).astype(BF)
-    project(r.n2, ready("cq"), r.cq)
-    fwd_cross(z, r.cq, r.ckv, r.times, r.pc, r.c)
+    r.save("n2")
+    yield "cq"
+    yield from project(r.n2, ready("cq"), r.cq)
+    r.save("cq")
+    yield from fwd_cross(z, r.cq, r.ckv, r.times, r.pc, r.c)
+    r.save("pc")
+    r.save("c")
+    yield "co"
     h2 = r.h1[...] + (mm(r.c[...], ready("co")[...]) + r.vec[BC:BC + 1])
     r.h2[...] = h2
+    r.save("h2")
     r.n3[...] = mm(norm(h2, r.vec[G3:G3 + 1]), r.sp[...]).astype(BF)
-    fwd_up(z, r.n3, ready("up"), r.upb, r.gl, r.slope)
-    y = (r.h2[...] + (mm(r.gl[...], ready("dn")[...]) + r.vec[BD:BD + 1])).astype(BF)
+    r.save("n3")
+    yield "ct"
     ct = ready("ct")
     for m in range(z.MB):
         rows = slice(m * z.length, (m + 1) * z.length)
         pick = onehot(r.wanted[rows, :1] == iota((z.length, stream), 1))
+        r.ct[rows] = mm(pick, ct[m]).astype(BF)
+    r.save("ct")
+    step = z.ff // 4
+    for i in range(4):
+        yield "up" + str(i)
+        cut = (step // 2 + 127) // 128 * 128
+        for lo, hi in ((0, cut), (cut, step)):
+            fwd_up(z, r.n3, ready("up"), r.upb, r.gl, r.slope, slice(i * step + lo, i * step + hi))
+            yield
+    r.save("gl")
+    r.save("slope")
+    yield "dn"
+    dn = ready("dn")
+    out = mm(r.gl[...], dn[...])
+    y = (r.h2[...] + (out + r.vec[BD:BD + 1])).astype(BF)
+    for m in range(z.MB):
+        rows = slice(m * z.length, (m + 1) * z.length)
+        pick = onehot(r.wanted[rows, :1] == iota((z.length, stream), 1))
         r.back_y[m] = mm_tn(pick, y[rows]).astype(BF)
-        r.ct[rows] = mm(pick, ct[m]).astype(BF)
-
-
-def backward_steps(z, ready, emit, r):
+    r.save("back_y")
+
+
+def backward_steps(z, ready, r):
     vec, sp = r.vec, r.sp
-    e3 = r.ct[...]
     small = {}
     ones = lambda v: jnp.sum(v.astype(F32), 0, keepdims=True)
-    small[BD] = ones(e3)
+    yield "saved", ("ct",)
+    yield "weight", "dn"
     dn = ready("dn")
+    small[BD] = ones(r.ct[...])
     for i in range(z.ff // tile):
         at = slice(i * tile, (i + 1) * tile)
-        du = (mm_nt(e3, dn[at, :]) * r.slope_tile(i)).astype(BF)
+        du = (mm_nt(r.ct[...], dn[at, :]) * r.slope_tile(i)).astype(BF)
         r.du[:, at] = du
         r.upb_sum[:, at] = ones(du)
-    emit("dn", lambda out: outer(r.gl, r.ct, out))
-    dw, small[G3] = norm_back(r.h2[...], vec[G3:G3 + 1], dense(mm_nt(r.du[...], ready("up")[...]), sp[...]))
-    emit("up", lambda out: outer(r.n3, r.du, out))
-    dh = e3.astype(F32) + dw
+        yield
+    yield "saved", ("gl",)
+    yield from outer(r.gl, r.ct, ready("dn"))
+    yield "grad", "dn"
+    yield "saved", ("sp", "vec", "h2", "n3")
+    yield "weight", "up"
+    dn3 = dense(mm_nt(r.du[...], ready("up")[...]), sp[...])
+    dw, small[G3] = norm_back(r.h2[...], vec[G3:G3 + 1], dn3)
+    dh = r.ct[...].astype(F32) + dw
     r.dh[...] = dh
     r.e[...] = dh.astype(BF)
-    small[BC] = ones(r.e[...])
-    project_nt(r.e, ready("co"), r.dc)
-    emit("co", lambda out: outer(r.c, r.e, out))
-    bwd_cross(z, r.cq, r.ckv, r.times, r.pc, r.dc, r.dcq, r.dckv)
+    small[BC] = ones(dh.astype(BF))
+    yield
+    yield from outer(r.n3, r.du, ready("up"))
+    yield "grad", "up"
+    yield "weight", "co"
+    yield from project_nt(r.e, ready("co"), r.dc)
+    yield "saved", ("c",)
+    yield from outer(r.c, r.e, ready("co"))
+    yield "grad", "co"
+    yield "saved", ("cq", "ckv", "pc")
+    yield from bwd_cross(z, r.cq, r.ckv, r.times, r.pc, r.dc, r.dcq, r.dckv)
+    yield "weight", "kv"
     kv = ready("kv")
     part = z.keys // 2
     for i in range(z.MB * 2):
         rows = slice(i * part, (i + 1) * part)
         r.put_pool(i, dense(mm_nt(r.dckv[rows, :], kv[...]), sp[...]))
-    emit("kv", lambda out: outer(r.ep, r.dckv, out))
-    dw, small[G2] = norm_back(r.h1[...], vec[G2:G2 + 1], dense(mm_nt(r.dcq[...], ready("cq")[...]), sp[...]))
-    emit("cq", lambda out: outer(r.n2, r.dcq, out))
+        yield
+    yield "saved", ("ep",)
+    yield from outer(r.ep, r.dckv, kv)
+    yield "grad", "kv"
+    yield "weight", "cq"
+    yield "saved", ("h1", "n2")
+    dn2 = dense(mm_nt(r.dcq[...], ready("cq")[...]), sp[...])
+    dw, small[G2] = norm_back(r.h1[...], vec[G2:G2 + 1], dn2)
+    yield
+    yield from outer(r.n2, r.dcq, ready("cq"))
+    yield "grad", "cq"
     dh = r.dh[...] + dw
     r.dh[...] = dh
     r.e[...] = dh.astype(BF)
-    small[BA] = ones(r.e[...])
-    project_nt(r.e, ready("ao"), r.dc)
-    emit("ao", lambda out: outer(r.a, r.e, out))
+    small[BA] = ones(dh.astype(BF))
+    yield "weight", "ao"
+    yield from project_nt(r.e, ready("ao"), r.dc)
+    yield "saved", ("a",)
+    yield from outer(r.a, r.e, ready("ao"))
+    yield "grad", "ao"
+    yield "saved", ("join", "ps")
     r.table[...] = jnp.zeros(r.table.shape, F32)
-    bwd_self(z, r.join, r.ps, r.dc, r.dq, r.table)
-    dw, small[G1] = norm_back(r.x[...], vec[G1:G1 + 1], dense(mm_nt(r.dq[...], ready("qkv")[...]), sp[...]))
+    yield from bwd_self(z, r.join, r.ps, r.dc, r.dq, r.table)
+    yield "weight", "qkv"
+    yield "saved", ("x", "n1")
+    dn1 = dense(mm_nt(r.dq[...], ready("qkv")[...]), sp[...])
+    dw, small[G1] = norm_back(r.x[...], vec[G1:G1 + 1], dn1)
     dx = (r.dh[...] + dw).astype(BF)
     stream = r.back_x.shape[1]
     for m in range(z.MB):
         rows = slice(m * z.length, (m + 1) * z.length)
         pick = onehot(r.wanted[rows, :1] == iota((z.length, stream), 1))
         r.back_x[m] = mm_tn(pick, dx[rows]).astype(BF)
+    yield "grad", "x"
+    yield from outer(r.n1, r.dq, ready("qkv"))
+    yield "grad", "qkv"
     pack_smalls(z, small, r)
-    emit("qkv", lambda out: outer(r.n1, r.dq, out))
+    yield "grad", "small"
 
 
 def pack_smalls(z, small, r):
@@ -435,12 +507,12 @@
             return pltpu.make_async_copy(held[k], view(k), sems.at[names.index(k)])
         for k in room:
             copy(k).start()
-        def ready(k):
-            if k in share:
-                copy(k).start()
-            copy(k).wait()
-            return view(k)
-        forward_steps(z, ready, r)
+        r.save = lambda k: None
+        for k in forward_steps(z, view, r):
+            if k in ("up0", "ct"):
+                copy(k.rstrip("0")).start()
+            if k == "up0" or k in names:
+                copy(k.rstrip("0")).wait()
     V = pl.BlockSpec(memory_space=pltpu.VMEM)
     A = pl.BlockSpec(memory_space=pl.ANY)
     return dict(zip(outs, pl.pallas_call(kernel, name="layer_forward", out_shape=list(outs.values()),
@@ -492,16 +564,15 @@
             r.pool_tiles[i % 2] = value
             pool_copy(i).start()
         r.slope_tile, r.put_pool = slope_tile, put_pool
-        def ready(k):
-            load(k).wait()
-            return bufs[k]
-        def emit(k, write):
-            write(bufs[k])
-            store(k).start()
-            if k == "co":
-                store("up").wait()
-                load("qkv").start()
-        backward_steps(z, ready, emit, r)
+        for event in backward_steps(z, lambda k: bufs[k], r):
+            kind, k = event or (None, None)
+            if kind == "weight":
+                load(k).wait()
+            if kind == "grad" and k in names:
+                store(k).start()
+                if k == "co":
+                    store("up").wait()
+                    load("qkv").start()
         for k in names:
             if k != "up":
                 store(k).wait()
@@ -576,30 +647,35 @@
     def arrived(self, pred, ref, s, r):
         when(pred, lambda: self.copy(ref, ref, s, r, self.at.pair).wait_recv())
 
+    def across(self, pred, ref, block=None):
+        p = self.at
+        src = ref if block is None else block
+        if not self.line_only:
+            for k, dev in ((4, p.first), (5, p.second)):
+                when(pred, lambda k=k, dev=dev: self.copy(src, ref, self.ps.at[k], self.pr.at[k], dev).start())
     def start(self):
         p = self.at
         mine = self.cell(p.z, p.c)
-        pltpu.make_async_copy(self.block, mine, self.own).start()
         self.send(p.has_up, self.block, mine, self.zs.at[0, 0], self.zr.at[0, 0], p.up)
         self.send(p.has_down, self.block, mine, self.zs.at[1, 0], self.zr.at[1, 0], p.down)
-    def along_z(self):
-        p = self.at
-        for j in range(1, p.nz):
-            below, above = p.z >= j, p.z < p.nz - j
-            ref = self.cell(p.z - j, p.c)
-            self.arrived(below, ref, self.zs.at[0, j - 1], self.zr.at[0, j - 1])
+        self.across(None, mine, self.block)
+        pltpu.make_async_copy(self.block, mine, self.own).start()
+    def hop(self, j):
+        p = self.at
+        for way, pred, more, ref, dev in ((0, p.z >= j, p.has_up, self.cell(p.z - j, p.c), p.up),
+                                          (1, p.z < p.nz - j, p.has_down, self.cell(p.z + j, p.c), p.down)):
+            self.arrived(pred, ref, self.zs.at[way, j - 1], self.zr.at[way, j - 1])
             if j < p.nz - 1:
-                self.send(both(below, p.has_up), ref, ref, self.zs.at[0, j], self.zr.at[0, j], p.up)
-            ref = self.cell(p.z + j, p.c)
-            self.arrived(above, ref, self.zs.at[1, j - 1], self.zr.at[1, j - 1])
-            if j < p.nz - 1:
-                self.send(both(above, p.has_down), ref, ref, self.zs.at[1, j], self.zr.at[1, j], p.down)
+                self.send(both(pred, more), ref, ref, self.zs.at[way, j], self.zr.at[way, j], dev)
+            self.across(pred, ref)
+    def z_done(self):
+        p = self.at
         pltpu.make_async_copy(self.block, self.cell(p.z, p.c), self.own).wait()
         mine = self.line(p.y, p.x, p.c)
         self.send(None, mine, mine, self.ps.at[0], self.pr.at[0], p.pair)
         if not self.line_only:
-            self.send(None, mine, mine, self.ps.at[4], self.pr.at[4], p.first)
-            self.send(None, mine, mine, self.ps.at[5], self.pr.at[5], p.second)
+            for k in (4, 5):
+                self.late.append((None, lambda k=k: self.copy(mine, mine, self.ps.at[k], self.pr.at[k], p.pair).wait_send()))
     def after_first(self):
         p = self.at
         if self.line_only: return
@@ -626,94 +702,6 @@
 def sem_shapes(n, nz):
     D = pltpu.SemaphoreType.DMA
     return [D((n, 2, nz)), D((n, 2, nz)), D((n, 8)), D((n, 8)), D((n,))]
-
-
-def pad16(r):
-    return (r + 15) // 16 * 16
-
-
-SENDS = (("small", 1), ("kv", 2), ("tok", 1), ("qkv", 3), ("ao", 1), ("cq", 1), ("co", 1), ("up", 4), ("dn", 2), ("ct", 1))
-lines_only = ("tok", "ct")
-
-
-def piece(ref, name, c, cut):
-    if cut == 1:
-        return ref
-    lead = (slice(None),) * (len(ref.shape) - 2)
-    if name == "dn":
-        tiles = ref.shape[-2] // 16
-        return ref.at[lead + (slice(tiles * c // cut * 16, tiles * (c + 1) // cut * 16),)]
-    cols = ref.shape[-1] // cut
-    return ref.at[lead + (slice(None), slice(c * cols, (c + 1) * cols))]
-
-
-def gather_kernel(n, nz, pieces, ahead, *refs):
-    blocks, outs, stage = refs[:n], refs[n:2 * n], refs[2 * n:3 * n]
-    zs, zr, ps, pr, own = refs[3 * n:]
-    at = Place(nz)
-    for b, s in zip(blocks, stage):
-        if s.shape == b.shape:
-            s[...] = b[...]
-        else:
-            s[...] = jnp.zeros(s.shape, s.dtype)
-            s[:b.shape[0], :] = b[...]
-    at.barrier()
-    gs = []
-    for i, (k, cut) in enumerate(pieces):
-        for c in range(cut):
-            part = lambda ref: piece(ref, k, c, cut)
-            j = len(gs)
-            gs.append(Gather(at, part(stage[i]), part(outs[i]), [s.at[j] for s in (zs, zr, ps, pr, own)], k in lines_only))
-    for g in gs[:ahead]:
-        g.start()
-    for t in range(len(gs) + 2):
-        if t + ahead < len(gs):
-            gs[t + ahead].start()
-        if t < len(gs):
-            gs[t].along_z()
-        if 1 <= t <= len(gs):
-            gs[t - 1].after_first()
-        if 2 <= t:
-            gs[t - 2].after_second()
-    for g in gs:
-        g.whole()
-    for g in gs:
-        g.drain()
-
-
-def gather_named(arrays, z, nz):
-    pieces = SENDS
-    names = [k for k, _ in pieces]
-    n, total = len(names), sum(cut for _, cut in pieces)
-    blocks = [arrays[k] for k in names]
-    outs, stages = [], []
-    for k, b in zip(names, blocks):
-        if k in lines_only:
-            outs.append(jax.ShapeDtypeStruct((b.shape[0], nz, 2) + b.shape[1:], b.dtype))
-            stages.append(pltpu.VMEM(b.shape, b.dtype))
-        else:
-            r = pad16(b.shape[0])
-            outs.append(jax.ShapeDtypeStruct((2, 2, nz, 2, r, b.shape[1]), b.dtype))
-            stages.append(pltpu.VMEM((r, b.shape[1]), b.dtype))
-    got = pl.pallas_call(partial(gather_kernel, n, nz, pieces, 2), name="gather_weights", out_shape=outs,
-        in_specs=[pl.BlockSpec(memory_space=pltpu.VMEM)] * n, out_specs=[pl.BlockSpec(memory_space=pl.ANY)] * n,
-        scratch_shapes=stages + sem_shapes(total, nz),
-        compiler_params=pltpu.CompilerParams(collective_id=1, has_side_effects=True, vmem_limit_bytes=40 * MIB))(*blocks)
-    flat = lambda k, v: v.reshape(v.shape[0], -1, v.shape[-1]) if k in lines_only else v.reshape(-1, v.shape[-1])
-    return {k: flat(k, v) for k, v in zip(names, got)}
-
-
-def scatter_named(lines, small, grads, shards, z, nz):
-    S = jax.ShapeDtypeStruct
-    tok = z.length // 2
-    as_line = lambda v: v.reshape(z.MB, nz, 2, tok, z.width)
-    as_blocks = lambda v: v.reshape(2, 2, nz, 2, v.shape[0] // GROUPS, v.shape[1])
-    order = ["dn", "up", "co", "kv", "cq", "ao", "qkv"]
-    srcs = [as_line(lines["y"])] + [as_blocks(grads[k]) for k in order] + [as_blocks(small), as_line(lines["x"])]
-    line = [True] + [False] * 8 + [True]
-    outs = [S((z.MB, tok, z.width), BF)] + [S(shards[k].shape, F32) for k in order] + [S((8, 128), F32), S((z.MB, tok, z.width), BF)]
-    got = scatter_all(srcs, line, outs, nz)
-    return got[0], got[-1], got[-2], dict(zip(order, got[1:-2]))
 
 
 class Scatter:
@@ -849,6 +837,169 @@
         compiler_params=pltpu.CompilerParams(collective_id=cid, has_side_effects=True, vmem_limit_bytes=63 * MIB))(*srcs)
 
 
+def pad16(r):
+    return (r + 15) // 16 * 16
+
+
+PIECES = (("small", 0), ("kv", 0), ("tok", 0), ("kv", 1), ("tok", 1), ("qkv", 0), ("qkv", 1), ("qkv", 2), ("ao", 0), ("ct", 0), ("cq", 0),
+          ("co", 0), ("ct", 1), ("up", 0), ("up", 1), ("up", 2), ("up", 3), ("dn", 0), ("dn", 1))
+lines_only = ("tok", "ct")
+hop_lag, first_lag, second_lag, whole_lag, send_ahead, units_per_step = 0, 3, 4, 5, 2, 4
+
+
+def piece(ref, name, c):
+    cut = sum(k == name for k, _ in PIECES)
+    if cut == 1:
+        return ref
+    if name in lines_only:
+        return ref.at[c:c + 1]
+    lead = (slice(None),) * (len(ref.shape) - 2)
+    if name == "dn":
+        tiles = ref.shape[-2] // 16
+        return ref.at[lead + (slice(tiles * c // cut * 16, tiles * (c + 1) // cut * 16),)]
+    cols = ref.shape[-1] // cut
+    return ref.at[lead + (slice(None), slice(c * cols, (c + 1) * cols))]
+
+
+def forward_gather(z, arrays, wanted, times, pool, nz):
+    names = list(arrays)
+    S = jax.ShapeDtypeStruct
+    whole, stages = {}, []
+    for k, b in arrays.items():
+        if k in lines_only:
+            whole[k] = S((b.shape[0], nz, 2) + b.shape[1:], b.dtype)
+            stages.append(pltpu.VMEM(b.shape, b.dtype))
+        else:
+            r = pad16(b.shape[0])
+            whole[k] = S((2, 2, nz, 2, r, b.shape[1]), b.dtype)
+            stages.append(pltpu.VMEM((r, b.shape[1]), b.dtype))
+    saved = {**saved_shapes(z), "back_y": S((z.MB, z.stream, z.width), BF)}
+    share = {"up": "qkv", "ct": "tok"}
+    room = {k: whole[k] for k in names if k not in share}
+    room["qkv"] = whole["up"]
+    count = len(PIECES)
+
+    def kernel(*refs):
+        refs = list(refs)
+        take = lambda k: [refs.pop(0) for _ in range(k)]
+        blocks = dict(zip(names, take(len(names))))
+        r = Refs(["wanted", "times", "pool"], take(3))
+        landed = dict(zip(names, take(len(names))))
+        kept = dict(zip(saved, take(len(saved))))
+        stage = dict(zip(names, take(len(names))))
+        r.__dict__.update(zip(saved, take(len(saved))))
+        bufs = dict(zip(room, take(len(room))))
+        r.bias, r.upb, loads, saves = take(4)
+        sems = take(5)
+        at = Place(nz)
+        for k in names:
+            b, s = blocks[k], stage[k]
+            if s.shape == b.shape:
+                s[...] = b[...]
+            else:
+                s[...] = jnp.zeros(s.shape, s.dtype)
+                s[:b.shape[0], :] = b[...]
+        at.barrier()
+        gs = [Gather(at, piece(stage[k], k, c), piece(landed[k], k, c), [s.at[j] for s in sems], k in lines_only)
+              for j, (k, c) in enumerate(PIECES)]
+
+        def save(k):
+            pltpu.make_async_copy(getattr(r, k), kept[k], saves.at[list(saved).index(k)]).start()
+        r.save = save
+        def buffer(k):
+            if k in ("qkv", "up"):
+                return bufs["qkv"].at[:, :, :, :, :, :whole[k].shape[-1]]
+            return bufs[share.get(k, k)]
+        def load(j):
+            k, c = PIECES[j]
+            return pltpu.make_async_copy(piece(landed[k], k, c), piece(buffer(k), k, c), loads.at[j])
+        def ready(k):
+            b = bufs[share.get(k, k)]
+            if k in lines_only:
+                return b.reshape(z.MB, z.stream, z.width)
+            flat = b.reshape(GROUPS * b.shape[-2], b.shape[-1])
+            return flat.at[:, :whole[k].shape[-1]] if k in ("qkv", "up") else flat
+
+        there, started, waited = set(), set(), set()
+        free = set(room)
+        work = forward_steps(z, ready, r)
+        state = {"need": next(work), "done": False}
+        def start_loads():
+            for j in sorted(there - started):
+                if PIECES[j][0] in free:
+                    load(j).start()
+                    started.add(j)
+        def advance(units):
+            while units and not state["done"]:
+                need = state["need"]
+                if need:
+                    if need == "ao":
+                        free.add("up")
+                    if need == "qkv":
+                        free.add("ct")
+                    start_loads()
+                    ask = {j for j, (k, c) in enumerate(PIECES) if k == need or k + str(c) == need}
+                    if not ask <= started:
+                        return
+                    for j in sorted(ask - waited):
+                        load(j).wait()
+                    waited.update(ask)
+                try:
+                    state["need"] = next(work)
+                except StopIteration:
+                    state["done"] = True
+                units -= 1
+
+        for g in gs[:send_ahead]:
+            g.start()
+        for t in range(count + whole_lag):
+            def stage_of(lag):
+                return gs[t - lag] if 0 <= t - lag < count else None
+            if t + send_ahead < count:
+                gs[t + send_ahead].start()
+            for j in range(1, nz):
+                if g := stage_of(j - 1):
+                    g.hop(j)
+            if g := stage_of(nz - 2):
+                g.z_done()
+            if g := stage_of(first_lag):
+                g.after_first()
+            if g := stage_of(second_lag):
+                g.after_second()
+            if g := stage_of(whole_lag):
+                g.whole()
+                there.add(t - whole_lag)
+                start_loads()
+            advance(units_per_step if t < count + whole_lag - 1 else 1 << 20)
+        for g in gs:
+            g.drain()
+        for i, k in enumerate(saved):
+            pltpu.make_async_copy(getattr(r, k), kept[k], saves.at[i]).wait()
+
+    V = pl.BlockSpec(memory_space=pltpu.VMEM)
+    A = pl.BlockSpec(memory_space=pl.ANY)
+    D = pltpu.SemaphoreType.DMA
+    got = pl.pallas_call(kernel, name="gather_forward", out_shape=list(whole.values()) + list(saved.values()),
+        in_specs=[V] * (len(names) + 3), out_specs=[A] * (len(names) + len(saved)),
+        scratch_shapes=stages + [pltpu.VMEM(s.shape, s.dtype) for s in saved.values()] + [pltpu.VMEM(s.shape, s.dtype) for s in room.values()]
+            + [pltpu.VMEM((HEADS, z.length, z.length), F32), pltpu.VMEM((1, z.ff), F32), D((count,)), D((len(saved),))] + sem_shapes(count, nz),
+        compiler_params=pltpu.CompilerParams(collective_id=1, has_side_effects=True, vmem_limit_bytes=63 * MIB))(*arrays.values(), wanted, times, pool)
+    flat = lambda k, v: v.reshape(-1, v.shape[-1])
+    return {k: flat(k, v) for k, v in zip(names, got) if k in WEIGHTS}, dict(zip(saved, got[len(names):]))
+
+def scatter_named(lines, small, grads, shards, z, nz):
+    S = jax.ShapeDtypeStruct
+    tok = z.length // 2
+    as_line = lambda v: v.reshape(z.MB, nz, 2, tok, z.width)
+    as_blocks = lambda v: v.reshape(2, 2, nz, 2, v.shape[0] // GROUPS, v.shape[1])
+    order = ["dn", "up", "co", "kv", "cq", "ao", "qkv"]
+    srcs = [as_line(lines["y"])] + [as_blocks(grads[k]) for k in order] + [as_blocks(small), as_line(lines["x"])]
+    line = [True] + [False] * 8 + [True]
+    outs = [S((z.MB, tok, z.width), BF)] + [S(shards[k].shape, F32) for k in order] + [S((8, 128), F32), S((z.MB, tok, z.width), BF)]
+    got = scatter_all(srcs, line, outs, nz)
+    return got[0], got[-1], got[-2], dict(zip(order, got[1:-2]))
+
+
 def vectors(norm1_gain, norm2_gain, norm3_gain, attn_out_bias, cca_out_bias, ffw_down_bias, rel_table, ffw_up_bias):
     return [norm1_gain, norm2_gain, norm3_gain, attn_out_bias, cca_out_bias, ffw_down_bias, rel_table, ffw_up_bias]
 
@@ -896,16 +1047,17 @@
     nz = members // 2
     if direct:
         packed = jnp.concatenate([jnp.pad(v[None], ((0, 0), (0, 128 - v.shape[0]))) for v in vecs] + [jnp.zeros((SMALLS - 8, 128), BF)], 0)
-        gathered = gather_named({"small": packed, "tok": tokens, "ct": cotangent, **shards}, z, nz)
+        weights, saved = forward_gather(z, {"small": packed, "tok": tokens, "ct": cotangent, **shards}, wanted, times, neighbours, nz)
     else:
         whole = lambda v: lax.all_gather(v, ("dp", "fsdp"), axis=0, tiled=True)
         rows = [jnp.pad(w, ((0, 0), (0, 128 - w.shape[1])))[:, None] for w in [whole(v).reshape(GROUPS, -1) for v in vecs]]
         packed = jnp.concatenate(rows + [jnp.zeros((GROUPS, SMALLS - 8, 128), BF)], 1).reshape(GROUPS * SMALLS, 128)
         gathered = {"small": packed, **{k: to_groups(whole(v)) for k, v in shards.items()},
                     "tok": lax.all_gather(tokens, "fsdp", axis=1, tiled=True), "ct": lax.all_gather(cotangent, "fsdp", axis=1, tiled=True)}
-    saved = forward_plain(z, gathered, wanted, times, neighbours)
+        weights = {k: gathered[k] for k in WEIGHTS}
+        saved = forward_plain(z, gathered, wanted, times, neighbours)
     back_y = saved.pop("back_y")
-    grads, outs = backward_plain(z, {k: gathered[k] for k in WEIGHTS}, saved, wanted, times)
+    grads, outs = backward_plain(z, weights, saved, wanted, times)
     back_x, small = outs["back_x"], outs["small_grad"]
     if direct:
         lines = {"y": back_y, "x": back_x}

time: 516 us -> 443 us (0.86)
  Pallas kernels: 465 us -> 411 us
  local copies, waits for them, and re-layouts: 37.4 us -> 23.5 us
    pallas_call x2 -> x1, Pallas kernels: 207 us -> 158 us  [forward_gather(): pl.pallas_call(kernel, name='gather_forward', out_shape=list(whole.values...]
    unnamed x47 -> x17, local copies, waits for them, and re-layouts: 26.2 us -> 11.1 us
    pallas_call x1, Pallas kernels: 87 us -> 77.9 us  [backward_plain(): pl.pallas_call(kernel, name='layer_backward', out_shape=[S(shapes[k], BF)...]
where the time goes in v2:
time: 443 us; the launch traced here: 439 us
  Pallas kernels  411 us (93%)
  local copies, waits for them, and re-layouts  23.5 us (5%)
    pallas_call x1, Pallas kernels, scatter_all(): pl.pallas_call(partial(scatter_kernel, n, nz, line_only, ahead), name=nam...  175 us
    pallas_call x1, Pallas kernels, forward_gather(): pl.pallas_call(kernel, name='gather_forward', out_shape=list(whole.values...  158 us
    pallas_call x1, Pallas kernels, backward_plain(): pl.pallas_call(kernel, name='layer_backward', out_shape=[S(shapes[k], BF)...  77.9 us
    unnamed x17, local copies, waits for them, and re-layouts  11.1 us

profile of v2, /device:TPU:0, one launch (start us, length us, event | category | flops | bytes accessed | tf_op | source)
XLA Modules:
  0.0 438.8 jit_solution(1103421488529383222)
XLA Ops:
  0.7 0.7 broadcast_compare_fusion
  1.3 0.7 pad.27
  2.0 0.7 pad.30
  2.7 0.7 pad.33
  3.3 0.7 pad.28
  4.0 0.7 pad.31
  4.7 0.7 pad.29
  5.3 0.7 pad.34
  6.0 0.7 pad.32
  6.7 0.8 select_reduce_fusion
  7.5 0.8 fusion.2
  8.4 0.8 fusion
  9.4 1.2 concatenate.3.refs_0_
  10.6 0.1 copy.40
  10.7 0.8 broadcast_in_dim.114.refs_10_.refs_26_
  11.5 0.2 broadcast_in_dim.118
  11.7 0.8 reshape.231.refs_11_.refs_27_
  12.5 157.8 %gather_forward.1 = (bf16[2,2,4,2,16,128]{5,4,3,2,1,0:T(8,128)(2,1)}, bf16[2,4,2,64,896]{4,3,2,1,0:T(8,128)(2,1)}, bf16[2,4,2,64,896]{4,3,2,1,0:T(8,128)(2,1)}, ...) custom-call(bf16[16,128]{1,0:T(8,128)(2,1)} %concatenate.3.refs_0_, ...), custom_call_target="tpu_custom_call" | custom-call | tf_op jit(solution)/shard_map/gather_forward/pallas_call | solution.py:982
  170.4 77.9 %layer_backward.1 = (bf16[1024,3072]{1,0:T(8,128)(2,1)}, bf16[1024,896]{1,0:T(8,128)(2,1)}, bf16[1024,1024]{1,0:T(8,128)(2,1)}, bf16[1024,2048]{1,0:T(8,128)(2,1...) custom-call(bf16[1024,3072]{1,0:T(8,128)(2,1)} %bitcast.58, ...), custom_call_target="tpu_custom_call" | custom-call | tf_op jit(solution)/shard_map/layer_backward/pallas_call | solution.py:584
  248.2 175.4 %scatter_grads.1 = (bf16[2,64,896]{2,1,0:T(8,128)(2,1)}, f32[112,896]{1,0:T(8,128)}, f32[28,3584]{1,0:T(8,128)}, f32[32,896]{1,0:T(8,128)}, f32[28,2048]{1,0:T(8...) custom-call(bf16[2,4,2,64,896]{4,3,2,1,0:T(8,128)(2,1)} %bitcast.63,, ...), custom_call_target="tpu_custom_call" | custom-call | tf_op jit(solution)/shard_map/scatter_grads/pallas_call | solution.py:834
  423.7 1.3 slice_bitcast_fusion.5
  424.9 1.2 slice_bitcast_fusion.1
  426.1 1.4 slice_bitcast_fusion
  427.6 1.6 copy.53
  429.2 1.6 copy.54
  430.8 1.8 copy.55
  432.6 1.6 copy.56
  434.2 1.6 copy.57
  435.7 0.7 copy.58
  436.4 0.6 copy.59
  437.1 0.8 copy.60
  437.9 0.7 copy.61
  (16 shorter events, 0.3 us)
Async XLA Ops:
  423.6 12.1 %copy-start.2 = (f32[28,2048]{1,0:T(8,128)S(1)}, f32[28,2048]{1,0:T(8,128)}, u32[]{:S(2)}) copy-start(f32[28,2048]{1,0:T(8,128)} %get-tuple-element.148) | copy-start | bytes 688132
  423.6 12.8 %copy-start.3 = (f32[32,896]{1,0:T(8,128)S(1)}, f32[32,896]{1,0:T(8,128)}, u32[]{:S(2)}) copy-start(f32[32,896]{1,0:T(8,128)} %get-tuple-element.149) | copy-start | bytes 344068
  423.6 13.4 %copy-start = (f32[28,3584]{1,0:T(8,128)S(1)}, f32[28,3584]{1,0:T(8,128)}, u32[]{:S(2)}) copy-start(f32[28,3584]{1,0:T(8,128)} %get-tuple-element.152) | copy-start | bytes 1204228
  423.6 14.2 %copy-start.1 = (f32[112,896]{1,0:T(8,128)S(1)}, f32[112,896]{1,0:T(8,128)}, u32[]{:S(2)}) copy-start(f32[112,896]{1,0:T(8,128)} %get-tuple-element.154) | copy-start | bytes 1204228

commit v3 on v2

v3 whole, which is shorter than its diff:
```python
from functools import partial

import jax
import jax.numpy as jnp
from jax import lax
from jax.experimental import pallas as pl
from jax.experimental.pallas import tpu as pltpu
from jax.sharding import PartitionSpec as P

K_0 = "0"
K_A = "a"
K_AO = "ao"
K_BACK_X = "back_x"
K_BACK_Y = "back_y"
K_C = "c"
K_CKV = "ckv"
K_CO = "co"
K_CQ = "cq"
K_CT = "ct"
K_DC = "dc"
K_DH = "dh"
K_DN = "dn"
K_DONE = "done"
K_DP = "dp"
K_DU = "du"
K_E = "e"
K_EP = "ep"
K_FINISH = "finish"
K_FIRST = "first"
K_FSDP = "fsdp"
K_GL = "gl"
K_GRAD = "grad"
K_H1 = "h1"
K_H2 = "h2"
K_JOIN = "join"
K_KV = "kv"
K_N1 = "n1"
K_N2 = "n2"
K_N3 = "n3"
K_NEED = "need"
K_PAIR = "pair"
K_PC = "pc"
K_POOL = "pool"
K_POOL_GRAD = "pool_grad"
K_PS = "ps"
K_QKV = "qkv"
K_SAVED = "saved"
K_SECOND = "second"
K_SLOPE = "slope"
K_SMALL = "small"
K_SMALL_GRAD = "small_grad"
K_SPT = "spt"
K_TABLE = "table"
K_TILE = "tile"
K_TILES = "tiles"
K_TIMES = "times"
K_TOK = "tok"
K_UP = "up"
K_UP0 = "up0"
K_UPB_SUM = "upb_sum"
K_VEC = "vec"
K_WANTED = "wanted"
K_WEIGHT = "weight"
K_X = "x"
K_Y = "y"
MIB = 1 << 20
F32, BF = jnp.float32, jnp.bfloat16
HEADS, HEAD_DIM, CH, NL, K_NB, NB = 16, 64, 64, 128, 2, 64
epsilon = 1e-06
masked_score = -1e30
tile = 512
unroll = 4
low_row = 48
GROUPS = 32
SMALLS = 16
G1, G2, G3, BA, BC, BD, REL, UPB = range(8)


def mm(a, b):
    return jnp.dot(a, b, preferred_element_type=F32)
def mm_tn(a, b):
    return lax.dot_general(a, b, (((0,), (0,)), ((), ())), preferred_element_type=F32)
def mm_nt(a, b):
    return lax.dot_general(a, b, (((1,), (1,)), ((), ())), preferred_element_type=F32)
def iota(shape, dim):
    return lax.broadcasted_iota(jnp.int32, shape, dim)
def onehot(cond):
    return jnp.where(cond, 1.0, 0.0).astype(BF)
def split2(v):
    hi = v.astype(BF)
    return hi, (v - hi.astype(F32)).astype(BF)
def columns(i, size):
    return pl.ds(pl.multiple_of(i * size, size), size)
def loop(count, body):
    def step(i, carry):
        body(i)
        return carry
    lax.fori_loop(0, count, step, 0)


def spread(width):
    small = width // GROUPS
    big = (small + 15) // 16 * 16
    row, col = iota((width, GROUPS * big), 0), iota((width, GROUPS * big), 1)
    return onehot((col // big == row // small) & (col % big == row % small))


def gather_up(width):
    small = width // GROUPS
    big = (small + 15) // 16 * 16
    row, col = iota((GROUPS * big, width), 1), iota((GROUPS * big, width), 0)
    return onehot((col // big == row // small) & (col % big == row % small))


def dense(v, back):
    hi, lo = split2(v)
    return mm(hi, back) + mm(lo, back)


def small_rows(packed, width):
    per = width // GROUPS
    put = onehot(iota((128, width), 0) == iota((128, width), 1) % per)
    placed = mm(packed, put)
    shape = (GROUPS * SMALLS, width)
    placed = jnp.where(iota(shape, 0) // SMALLS == iota(shape, 1) // per, placed, 0.0).astype(BF)
    take = onehot(iota((SMALLS, GROUPS * SMALLS), 1) % SMALLS == iota((SMALLS, GROUPS * SMALLS), 0))
    return mm(take, placed)


def table_rows(packed, length):
    per = NB * HEADS // GROUPS // HEADS
    width = length // NB
    take = onehot(iota((GROUPS, GROUPS * SMALLS), 1) == iota((GROUPS, GROUPS * SMALLS), 0) * SMALLS + REL)
    held = mm(take, packed).astype(BF)
    far = (length - iota((GROUPS, length), 1)) % length // width
    at = mm_tn(held, onehot(far // per == iota((GROUPS, length), 0)))
    which = (length - iota((HEADS, length), 1)) % length // width % per
    out = jnp.zeros((HEADS, length), F32)
    for k in range(per):
        out = jnp.where(which == k, at[k * HEADS:(k + 1) * HEADS], out)
    return out


def biases(rows, bias):
    length = bias.shape[1]
    below = iota((length, length), 0) >= iota((length, length), 1)
    for h in range(HEADS):
        wide = jnp.broadcast_to(rows[h:h + 1], (length, length))
        bias[h] = jnp.where(below, pltpu.roll(wide, 0, 1, stride=1, stride_axis=0), masked_score)


def rms(v):
    return lax.rsqrt(jnp.mean(v * v, -1, keepdims=True) + epsilon)


def norm(v, gain):
    return (v * rms(v) * gain).astype(BF)


def norm_back(v, gain, dn):
    r = rms(v)
    unit = v * r
    gained = dn * gain
    return r * (gained - unit * jnp.mean(gained * unit, -1, keepdims=True)), jnp.sum(dn * unit, 0, keepdims=True)


def halves(v):
    first = iota(v.shape, 1) < HEAD_DIM
    zero = jnp.zeros(v.shape, v.dtype)
    return jnp.concatenate([jnp.where(first, v, zero), jnp.where(first, zero, v)], 0)


def joined(v):
    n = v.shape[0] // 2
    return jnp.where(iota((n, v.shape[1]), 1) < HEAD_DIM, v[:n], v[n:])


def head_parts(count, parts, body):
    pairs = HEADS // 2
    total = count * pairs
    def step(i, carry):
        m, p = i // pairs, i % pairs
        body(m, p, p * 2 * HEAD_DIM)
        return carry
    for k in range(parts):
        lax.fori_loop(total * k // parts, total * (k + 1) // parts, step, 0, unroll=unroll)
        yield


class Sizes:
    def __init__(self, MB, length, width, att, ff, pool):
        self.MB, self.length, self.width, self.att, self.ff, self.pool = MB, length, width, att, ff, pool
        self.rows = MB * length
        self.win = length - low_row
        self.wide = GROUPS * ((width // GROUPS + 15) // 16 * 16)
        self.keys = pool * NL


def fwd_self(z, join, bias, ps, att):
    factor = HEAD_DIM ** -0.5
    def body(m, p, c):
        rows = pl.ds(pl.multiple_of(m * z.length, 128), z.length)
        at = lambda part: pl.ds(pl.multiple_of(part * z.att + c, 128), 128)
        q, k, v = join[rows, at(0)], join[rows, at(1)], join[rows, at(2)]
        s = mm_nt(halves(q), k) * factor + jnp.concatenate([bias[2 * p], bias[2 * p + 1]], 0)
        e = jnp.exp(s - jnp.max(s, -1, keepdims=True))
        soft = e * (1.0 / jnp.sum(e, -1, keepdims=True))
        ps[m, p] = soft
        att[rows, at(0)] = joined(mm(soft.astype(BF), v)).astype(BF)
    yield from head_parts(z.MB, 4, body)


def fwd_cross(z, cq, ckv, times, pc, c_out):
    factor = HEAD_DIM ** -0.5
    for m in range(z.MB):
        c_out[m * z.length:m * z.length + low_row] = jnp.zeros((low_row, z.att), BF)
    def body(m, p, c):
        rows = pl.ds(pl.multiple_of(m * z.length + low_row, 16), z.win)
        keys = pl.ds(pl.multiple_of(m * z.keys, 128), z.keys)
        at = lambda part: pl.ds(pl.multiple_of(part * z.att + c, 128), 128)
        q, k, v = cq[rows, at(0)], ckv[keys, at(0)], ckv[keys, at(1)]
        cnt = times[m]
        cnt = jnp.concatenate([cnt, cnt], 0)
        s = jnp.where(cnt > 0, mm_nt(halves(q), k) * factor, masked_score)
        e = jnp.exp(s - jnp.max(s, -1, keepdims=True))
        total = jnp.sum(e * cnt, -1, keepdims=True)
        soft = e * (1.0 / jnp.where(total > 0, total, 1.0))
        for k in range(z.keys // NL):
            pc[m, p, k] = soft[:, k * NL:(k + 1) * NL]
        c_out[rows, at(0)] = joined(mm((soft.astype(BF).astype(F32) * cnt).astype(BF), v)).astype(BF)
    yield from head_parts(z.MB, 4, body)


def gelu_parts(u):
    k = 0.7978845608028654
    t = jnp.tanh(k * (u + 0.044715 * u * u * u))
    half = 0.5 * (1.0 + t)
    return u * half, half + 0.5 * u * (1.0 - t * t) * k * (1.0 + 3 * 0.044715 * u * u)


def fwd_up(z, n3, up, upb, gl, slope, at):
    u = mm(n3[...], up[:, at]) + upb[:, at]
    value, d = gelu_parts(u)
    gl[:, at] = value.astype(BF)
    slope[:, at] = d


def project(left, weight, out, size=tile):
    for i in range(out.shape[1] // size):
        at = slice(i * size, (i + 1) * size)
        out[:, at] = mm(left[...], weight[:, at]).astype(out.dtype)
        yield


def project_nt(left, weight, out, size=tile):
    for i in range(out.shape[1] // size):
        at = slice(i * size, (i + 1) * size)
        out[:, at] = mm_nt(left[...], weight[at, :]).astype(out.dtype)
        yield


def outer(left, right, out, lo, hi, size=256):
    for i in range(out.shape[0] // size):
        at = slice(i * size, (i + 1) * size)
        out[at, lo:hi] = mm_tn(left[:, at], right[:, lo:hi]).astype(out.dtype)
        yield


def bwd_self(z, join, ps, da, dq, table_sum):
    factor = HEAD_DIM ** -0.5
    def body(m, p, c):
        rows = pl.ds(pl.multiple_of(m * z.length, 128), z.length)
        at = lambda part: pl.ds(pl.multiple_of(part * z.att + c, 128), 128)
        q, k, v = join[rows, at(0)], join[rows, at(1)], join[rows, at(2)]
        d = halves(da[rows, at(0)])
        soft = ps[m, p]
        dp = mm_nt(d, v)
        ds = (soft * (dp - jnp.sum(dp * soft, -1, keepdims=True))).astype(BF)
        dq[rows, at(0)] = (joined(mm(ds, k)) * factor).astype(BF)
        dq[rows, at(1)] = (mm_tn(ds, halves(q)) * factor).astype(BF)
        dq[rows, at(2)] = mm_tn(soft.astype(BF), d).astype(BF)
        wide = ds.astype(F32)
        for k in range(2):
            heads = pl.ds(pl.multiple_of((2 * p + k) * z.length, 128), z.length)
            table_sum[:, heads] += wide[k * z.length:(k + 1) * z.length]
    yield from head_parts(z.MB, 4, body)


def bwd_cross(z, cq, ckv, times, pc, dc, dcq, dckv):
    factor = HEAD_DIM ** -0.5
    for m in range(z.MB):
        dcq[m * z.length:m * z.length + low_row] = jnp.zeros((low_row, z.att), BF)
    def body(m, p, c):
        rows = pl.ds(pl.multiple_of(m * z.length + low_row, 16), z.win)
        keys = pl.ds(pl.multiple_of(m * z.keys, 128), z.keys)
        at = lambda part: pl.ds(pl.multiple_of(part * z.att + c, 128), 128)
        q, k, v = cq[rows, at(0)], ckv[keys, at(0)], ckv[keys, at(1)]
        d = halves(dc[rows, at(0)])
        cnt = times[m]
        cnt = jnp.concatenate([cnt, cnt], 0)
        soft = jnp.concatenate([pc[m, p, k] for k in range(z.keys // NL)], 1)
        dp = mm_nt(d, v)
        ds = (soft * (dp - jnp.sum(dp * soft * cnt, -1, keepdims=True))).astype(BF)
        ds = (ds.astype(F32) * cnt).astype(BF)
        pb = (soft.astype(BF).astype(F32) * cnt).astype(BF)
        dcq[rows, at(0)] = (joined(mm(ds, k)) * factor).astype(BF)
        dckv[keys, at(0)] = (mm_tn(ds, halves(q)) * factor).astype(BF)
        dckv[keys, at(1)] = mm_tn(pb, d).astype(BF)
    yield from head_parts(z.MB, 4, body)


def exact(a, b, dims):
    return lax.dot_general(a, b, (dims, ((), ())), precision=lax.Precision.HIGHEST, preferred_element_type=F32)


def table_grad(table_sum):
    length = table_sum.shape[0]
    flip = onehot(iota((length, length), 0) + iota((length, length), 1) == length - 1)
    hi, lo = split2(table_sum)
    flipped = mm(flip, hi) + mm(flip, lo)
    rows = []
    for h in range(HEADS):
        turned = pltpu.roll(flipped[:, h * length:(h + 1) * length], 0, 1, stride=1, stride_axis=0)
        rows.append(jnp.sum(turned, 0, keepdims=True))
    return jnp.concatenate(rows, 0)


WEIGHTS = (K_QKV, K_AO, K_CQ, K_KV, K_CO, K_UP, K_DN)


def forward_steps(z, ready, r):
    yield K_SMALL
    r.sp[...] = spread(z.width)
    r.spt[...] = gather_up(z.width)
    r.save(K_SPT)
    packed = ready(K_SMALL)[...]
    r.vec[...] = small_rows(packed, z.width)
    r.save(K_VEC)
    yield
    def upb(i):
        at = columns(i, tile)
        per = z.ff // GROUPS
        put = onehot(iota((128, tile), 0) == (iota((128, tile), 1) + i * tile) % per)
        placed = mm(packed, put)
        shape = (GROUPS * SMALLS, tile)
        mine = (iota(shape, 0) // SMALLS == (iota(shape, 1) + i * tile) // per) & (iota(shape, 0) % SMALLS == UPB)
        r.upb[:, at] = jnp.sum(jnp.where(mine, placed, 0.0), 0, keepdims=True)
    loop(z.ff // tile, upb)
    biases(table_rows(packed, z.length), r.bias)
    half = z.keys // 2
    for i in range(z.MB * 2):
        rows = slice(i * half, (i + 1) * half)
        r.ep[rows, :] = mm(r.pool[rows, :], r.sp[...]).astype(BF)
        yield
    r.save(K_EP)
    yield K_KV
    kv = ready(K_KV)
    yield from project(r.ep, kv, r.ckv, 256)
    r.save(K_CKV)
    yield K_TOK
    tok = ready(K_TOK)
    stream = tok.shape[1]
    for m in range(z.MB):
        rows = slice(m * z.length, (m + 1) * z.length)
        pick = onehot(r.wanted[rows, :1] == iota((z.length, stream), 1))
        r.x[rows] = mm(pick, tok[m])
    r.save(K_X)
    yield
    r.n1[...] = mm(norm(r.x[...], r.vec[G1:G1 + 1]), r.sp[...]).astype(BF)
    r.save(K_N1)
    yield K_QKV
    yield from project(r.n1, ready(K_QKV), r.join)
    r.save(K_JOIN)
    yield from fwd_self(z, r.join, r.bias, r.ps, r.a)
    r.save(K_PS)
    r.save(K_A)
    yield K_AO
    h1 = r.x[...] + (mm(r.a[...], ready(K_AO)[...]) + r.vec[BA:BA + 1])
    r.h1[...] = h1
    r.save(K_H1)
    r.n2[...] = mm(norm(h1, r.vec[G2:G2 + 1]), r.sp[...]).astype(BF)
    r.save(K_N2)
    yield K_CQ
    yield from project(r.n2, ready(K_CQ), r.cq)
    r.save(K_CQ)
    yield from fwd_cross(z, r.cq, r.ckv, r.times, r.pc, r.c)
    r.save(K_PC)
    r.save(K_C)
    yield K_CO
    h2 = r.h1[...] + (mm(r.c[...], ready(K_CO)[...]) + r.vec[BC:BC + 1])
    r.h2[...] = h2
    r.save(K_H2)
    r.n3[...] = mm(norm(h2, r.vec[G3:G3 + 1]), r.sp[...]).astype(BF)
    r.save(K_N3)
    yield K_CT
    ct = ready(K_CT)
    for m in range(z.MB):
        rows = slice(m * z.length, (m + 1) * z.length)
        pick = onehot(r.wanted[rows, :1] == iota((z.length, stream), 1))
        r.ct[rows] = mm(pick, ct[m]).astype(BF)
    r.save(K_CT)
    step = z.ff // 4
    for i in range(4):
        yield K_UP + str(i)
        cut = (step // 2 + 127) // 128 * 128
        for lo, hi in ((0, cut), (cut, step)):
            fwd_up(z, r.n3, ready(K_UP), r.upb, r.gl, r.slope, slice(i * step + lo, i * step + hi))
            yield
    r.save(K_GL)
    r.save(K_SLOPE)
    yield K_DN
    dn = ready(K_DN)
    out = mm(r.gl[...], dn[...])
    y = (r.h2[...] + (out + r.vec[BD:BD + 1])).astype(BF)
    for m in range(z.MB):
        rows = slice(m * z.length, (m + 1) * z.length)
        pick = onehot(r.wanted[rows, :1] == iota((z.length, stream), 1))
        r.back_y[m] = mm_tn(pick, y[rows]).astype(BF)
    r.save(K_BACK_Y)


def backward_steps(z, ready, r):
    vec, back = r.vec, r.spt
    small = {}
    ones = lambda v: jnp.sum(v.astype(F32), 0, keepdims=True)
    def pieces(name, left, right):
        out, count = ready(name), r.cuts[name]
        size = out.shape[1] // count
        for c in range(count):
            yield from outer(left, right, out, c * size, (c + 1) * size)
            yield K_GRAD, name, c
    yield K_SAVED, (K_CT,)
    dn = ready(K_DN)
    small[BD] = ones(r.ct[...])
    step = z.ff // 4
    for i in range(4):
        at = slice(i * step, (i + 1) * step)
        yield K_TILE, i
        du = (mm_nt(r.ct[...], dn[at, :]) * r.slope_tile(i)).astype(BF)
        r.du[:, at] = du
        r.upb_sum[:, at] = ones(du)
    yield K_SAVED, (K_GL,)
    yield from outer(r.gl, r.ct, ready(K_DN), 0, z.width)
    yield K_GRAD, K_DN, 0
    yield K_GRAD, K_DN, 1
    yield K_SAVED, (K_SPT, K_VEC, K_H2, K_N3)
    yield K_WEIGHT, K_UP
    dn3 = dense(mm_nt(r.du[...], ready(K_UP)[...]), back[...])
    dw, small[G3] = norm_back(r.h2[...], vec[G3:G3 + 1], dn3)
    dh = r.ct[...].astype(F32) + dw
    r.dh[...] = dh
    r.e[...] = dh.astype(BF)
    small[BC] = ones(dh.astype(BF))
    yield
    yield from pieces(K_UP, r.n3, r.du)
    yield K_WEIGHT, K_CO
    yield from project_nt(r.e, ready(K_CO), r.dc)
    yield K_SAVED, (K_C,)
    yield from pieces(K_CO, r.c, r.e)
    yield K_SAVED, (K_CQ, K_CKV, K_PC)
    yield from bwd_cross(z, r.cq, r.ckv, r.times, r.pc, r.dc, r.dcq, r.dckv)
    yield K_SAVED, (K_EP,)
    yield from pieces(K_KV, r.ep, r.dckv)
    yield K_WEIGHT, K_CQ
    yield K_SAVED, (K_H1, K_N2)
    dn2 = dense(mm_nt(r.dcq[...], ready(K_CQ)[...]), back[...])
    dw, small[G2] = norm_back(r.h1[...], vec[G2:G2 + 1], dn2)
    dh = r.dh[...] + dw
    r.dh[...] = dh
    r.e[...] = dh.astype(BF)
    small[BA] = ones(dh.astype(BF))
    yield
    yield from pieces(K_CQ, r.n2, r.dcq)
    yield K_WEIGHT, K_AO
    yield from project_nt(r.e, ready(K_AO), r.dc)
    yield K_SAVED, (K_A,)
    yield from pieces(K_AO, r.a, r.e)
    yield K_SAVED, (K_JOIN, K_PS)
    r.table[...] = jnp.zeros(r.table.shape, F32)
    yield from bwd_self(z, r.join, r.ps, r.dc, r.dq, r.table)
    yield K_WEIGHT, K_QKV
    yield K_SAVED, (K_X, K_N1)
    dn1 = dense(mm_nt(r.dq[...], ready(K_QKV)[...]), back[...])
    dw, small[G1] = norm_back(r.x[...], vec[G1:G1 + 1], dn1)
    dx = (r.dh[...] + dw).astype(BF)
    stream = r.back_x.shape[1]
    for m in range(z.MB):
        rows = slice(m * z.length, (m + 1) * z.length)
        pick = onehot(r.wanted[rows, :1] == iota((z.length, stream), 1))
        r.back_x[m] = mm_tn(pick, dx[rows]).astype(BF)
    yield K_GRAD, K_X, 0
    pack_smalls(z, small, r)
    yield K_GRAD, K_SMALL, 0
    yield from pieces(K_QKV, r.n1, r.dq)


def pool_steps(z, ready, r):
    yield K_WEIGHT, K_KV
    kv = ready(K_KV)
    size = z.wide // 4
    for i in range(4):
        at = slice(i * size, (i + 1) * size)
        r.pool_hi[:, at], r.pool_lo[:, at] = split2(mm_nt(r.dckv[...], kv[at, :]))
        yield
    part = z.keys // 2
    for i in range(z.MB * 2):
        rows = slice(i * part, (i + 1) * part)
        r.put_pool(i, mm(r.pool_hi[rows, :], r.spt[...]) + mm(r.pool_lo[rows, :], r.spt[...]))
        yield


def pack_smalls(z, small, r):
    vecs = jnp.concatenate([small.get(i, jnp.zeros((1, z.width), F32)) for i in range(8)], 0)
    per = z.width // GROUPS
    shape = (GROUPS * 8, z.width)
    mine = iota(shape, 0) // 8 == iota(shape, 1) // per
    take = onehot(iota((GROUPS * 8, 8), 0) % 8 == iota((GROUPS * 8, 8), 1))
    put = onehot(iota((z.width, 128), 0) % per == iota((z.width, 128), 1))
    total = jnp.zeros((GROUPS * 8, 128), F32)
    for v in split2(vecs):
        total += mm(jnp.where(mine, mm(take, v), 0.0).astype(BF), put)
    per = z.ff // GROUPS
    bias = jnp.zeros((GROUPS, 128), F32)
    for i in range(z.ff // tile):
        shape = (GROUPS, tile)
        mine = iota(shape, 0) == (iota(shape, 1) + i * tile) // per
        put = onehot((iota((tile, 128), 0) + i * tile) % per == iota((tile, 128), 1))
        for v in split2(r.upb_sum[:, i * tile:(i + 1) * tile]):
            bias += mm(jnp.where(mine, jnp.broadcast_to(v.astype(F32), shape), 0.0).astype(BF), put)
    width = z.length // NB
    per = NB // GROUPS
    shape = (GROUPS, z.length)
    table = jnp.zeros((GROUPS, 128), F32)
    for v in split2(table_grad(r.table[...])):
        for k in range(per):
            mine = onehot((z.length - 1 - iota(shape, 1)) // width == iota(shape, 0) * per + k)
            put = onehot(iota((HEADS, 128), 0) + k * HEADS == iota((HEADS, 128), 1))
            table += mm(mm_nt(mine, v).astype(BF), put)
    for which, v in ((UPB, bias), (REL, table)):
        take = onehot(iota((GROUPS * 8, GROUPS), 0) == iota((GROUPS * 8, GROUPS), 1) * 8 + which)
        for part in split2(v):
            total += mm(take, part)
    r.small_grad[...] = total


class Refs:
    def __init__(self, names, refs):
        for n, ref in zip(names, refs): setattr(self, n, ref)


def weight_shapes(z):
    return {K_QKV: (z.wide, 3 * z.att), K_AO: (z.att, z.width), K_CQ: (z.wide, z.att), K_KV: (z.wide, 2 * z.att),
            K_CO: (z.att, z.width), K_UP: (z.wide, z.ff), K_DN: (z.ff, z.width)}


def saved_shapes(z):
    R = z.rows
    S = jax.ShapeDtypeStruct
    pairs = HEADS // 2
    return {K_SPT: S((z.wide, z.width), BF), K_VEC: S((SMALLS, z.width), F32), K_EP: S((z.MB * z.keys, z.wide), BF),
            K_CKV: S((z.MB * z.keys, 2 * z.att), BF), K_X: S((R, z.width), F32), K_N1: S((R, z.wide), BF),
            K_JOIN: S((R, 3 * z.att), BF), K_PS: S((z.MB, pairs, 2 * z.length, z.length), F32), K_A: S((R, z.att), BF),
            K_H1: S((R, z.width), F32), K_N2: S((R, z.wide), BF), K_CQ: S((R, z.att), BF),
            K_PC: S((z.MB, pairs, z.keys // NL, 2 * z.win, NL), F32), K_C: S((R, z.att), BF), K_H2: S((R, z.width), F32),
            K_N3: S((R, z.wide), BF), K_GL: S((R, z.ff), BF), K_SLOPE: S((R, z.ff), F32), K_CT: S((R, z.width), BF)}


def forward_plain(z, gathered, wanted, times, pool):
    names = list(gathered)
    saved = saved_shapes(z)
    outs = {**saved, K_BACK_Y: jax.ShapeDtypeStruct(gathered[K_TOK].shape, BF)}
    share = {K_UP: K_QKV, K_CT: K_TOK}
    room = {k: gathered[k].shape for k in names if k not in share}
    room[K_QKV] = gathered[K_UP].shape
    def kernel(*refs):
        n = len(names)
        held = dict(zip(names, refs[:n]))
        r = Refs([K_WANTED, K_TIMES, K_POOL], refs[n:n + 3])
        r.__dict__.update(zip(outs, refs[n + 3:n + 3 + len(outs)]))
        scratch = refs[n + 3 + len(outs):]
        sems, r.bias, r.upb, r.sp = scratch[:4]
        bufs = dict(zip(room, scratch[4:]))
        def view(k):
            return bufs[K_QKV].at[:, :gathered[k].shape[1]] if k in (K_QKV, K_UP) else bufs[share.get(k, k)]
        def copy(k):
            return pltpu.make_async_copy(held[k], view(k), sems.at[names.index(k)])
        for k in room:
            copy(k).start()
        r.save = lambda k: None
        for k in forward_steps(z, view, r):
            if k in (K_UP0, K_CT):
                copy(k.rstrip(K_0)).start()
            if k == K_UP0 or k in names:
                copy(k.rstrip(K_0)).wait()
    V = pl.BlockSpec(memory_space=pltpu.VMEM)
    A = pl.BlockSpec(memory_space=pl.ANY)
    return dict(zip(outs, pl.pallas_call(kernel, name="layer_forward", out_shape=list(outs.values()),
        in_specs=[A] * len(names) + [V] * 3, out_specs=[V] * len(outs),
        scratch_shapes=[pltpu.SemaphoreType.DMA((len(names),)), pltpu.VMEM((HEADS, z.length, z.length), F32), pltpu.VMEM((1, z.ff), F32), pltpu.VMEM((z.width, z.wide), BF)]
            + [pltpu.VMEM(v, BF) for v in room.values()],
        compiler_params=pltpu.CompilerParams(vmem_limit_bytes=63 * MIB))(*gathered.values(), wanted, times, pool)))


def backward_plain(z, weights, saved, wanted, times):
    names = list(WEIGHTS)
    shapes = weight_shapes(z)
    ins = list(saved)
    S = jax.ShapeDtypeStruct
    outs = {K_POOL_GRAD: S((z.MB * z.keys, z.width), F32), K_BACK_X: S((z.MB, z.stream, z.width), BF), K_SMALL_GRAD: S((GROUPS * 8, 128), F32)}
    part = z.keys // 2
    local = {K_DU: ((z.rows, z.ff), BF), K_UPB_SUM: ((1, z.ff), F32), K_DH: ((z.rows, z.width), F32), K_E: ((z.rows, z.width), BF),
             K_DC: ((z.rows, z.att), BF), "dcq": ((z.rows, z.att), BF), "dckv": ((z.MB * z.keys, 2 * z.att), BF),
             K_TABLE: ((z.length, HEADS * z.length), F32), K_TILES: ((2, max(z.rows, part), z.ff // 4), F32)}
    kept = [k for k in names if k != K_QKV]

    def kernel(*refs):
        refs = list(refs)
        take = lambda k: [refs.pop(0) for _ in range(k)]
        held = dict(zip(names, take(len(names))))
        r = Refs(ins + [K_WANTED, K_TIMES], take(len(ins) + 2))
        grads = dict(zip(names, take(len(names))))
        r.__dict__.update(zip(outs, take(len(outs))))
        sems, gsem, tsem, psem = take(4)
        bufs = dict(zip(kept, take(len(kept))))
        bufs[K_QKV] = bufs[K_UP].at[:, :shapes[K_QKV][1]]
        r.__dict__.update(zip(local, take(len(local))))
        r.dq = r.du.at[:, :3 * z.att]
        load = lambda k: pltpu.make_async_copy(held[k], bufs[k], sems.at[names.index(k)])
        store = lambda k: pltpu.make_async_copy(bufs[k], grads[k], gsem.at[names.index(k)])
        step = z.ff // 4
        r.slope_tiles, r.pool_tiles = r.tiles.at[:, :z.rows], r.tiles.at[:, :part, :z.width]
        r.pool_hi, r.pool_lo = r.ep, bufs[K_UP].at[:z.MB * z.keys, :z.wide]
        slope = lambda i: pltpu.make_async_copy(r.slope.at[:, i * step:(i + 1) * step], r.slope_tiles.at[i % 2], tsem.at[i % 2])
        slope(0).start()
        for k in (K_DN, K_UP, K_CO, K_CQ, K_AO):
            load(k).start()
        def slope_tile(i):
            if i + 1 < 4:
                slope(i + 1).start()
            slope(i).wait()
            return r.slope_tiles[i % 2]
        pool_copy = lambda i: pltpu.make_async_copy(r.pool_tiles.at[i % 2], r.pool_grad.at[i * part:(i + 1) * part], psem.at[i % 2])
        def put_pool(i, value):
            if i >= 2:
                pool_copy(i - 2).wait()
            r.pool_tiles[i % 2] = value
            pool_copy(i).start()
        r.slope_tile, r.put_pool = slope_tile, put_pool
        r.cuts = dict.fromkeys(names, 1)
        load(K_DN).wait()
        for event in backward_steps(z, lambda k: bufs[k], r):
            kind, k = (event or (None, None))[:2]
            if kind == K_WEIGHT:
                load(k).wait()
            if kind == K_GRAD and k in names and event[2] == int(k == K_DN):
                store(k).start()
                if k == K_CO:
                    store(K_UP).wait()
                    load(K_QKV).start()
        store(K_KV).wait()
        store(K_QKV).wait()
        load(K_KV).start()
        for event in pool_steps(z, lambda k: bufs[k], r):
            if event:
                load(K_KV).wait()
        for k in names:
            if k not in (K_UP, K_KV, K_QKV):
                store(k).wait()
        for i in (z.MB * 2 - 2, z.MB * 2 - 1):
            pool_copy(i).wait()
    V = pl.BlockSpec(memory_space=pltpu.VMEM)
    A = pl.BlockSpec(memory_space=pl.ANY)
    D = pltpu.SemaphoreType.DMA
    res = pl.pallas_call(kernel, name="layer_backward", out_shape=[S(shapes[k], BF) for k in names] + list(outs.values()),
        in_specs=[A] * len(names) + [A if k == K_SLOPE else V for k in ins] + [V] * 2, out_specs=[A] * (len(names) + 1) + [V] * 2,
        scratch_shapes=[D((len(names),)), D((len(names),)), D((2,)), D((2,))] + [pltpu.VMEM(shapes[k], BF) for k in kept]
            + [pltpu.VMEM(*v) for v in local.values()],
        compiler_params=pltpu.CompilerParams(vmem_limit_bytes=63 * MIB))(*[weights[k] for k in names], *saved.values(), wanted, times)
    return dict(zip(names, res)), dict(zip(outs, res[len(names):]))


MESH = pl.DeviceIdType.MESH

def when(pred, fn):
    if pred is None: fn()
    else: pl.when(pred)(fn)

def both(a, b):
    if a is None: return b
    if b is None: return a
    return jnp.logical_and(a, b)

class Place:
    def __init__(self, nz):
        dp, fs = lax.axis_index(K_DP), lax.axis_index(K_FSDP)
        self.nz = nz
        self.y, self.x = dp // 2, lax.rem(dp, 2)
        self.z, self.c = fs // 2, lax.rem(fs, 2)
        y, x, z, c = self.y, self.x, self.z, self.c
        self.y1, self.x1 = y + c * (1 - 2 * y), x + (1 - c) * (1 - 2 * x)
        self.y2, self.x2 = y + (1 - c) * (1 - 2 * y), x + c * (1 - 2 * x)
        self.yo, self.xo = 1 - y, 1 - x
        self.first = {K_DP: self.y1 * 2 + self.x1, K_FSDP: fs}
        self.second = {K_DP: self.y2 * 2 + self.x2, K_FSDP: fs}
        self.pair = {K_DP: dp, K_FSDP: z * 2 + 1 - c}
        self.up = {K_DP: dp, K_FSDP: fs + 2}
        self.down = {K_DP: dp, K_FSDP: fs - 2}
        self.has_up, self.has_down = z < nz - 1, z > 0

    def barrier(self):
        bar = pltpu.get_barrier_semaphore()
        ways = [(None, self.pair), (None, self.first), (None, self.second), (self.has_up, self.up), (self.has_down, self.down)]
        for pred, dev in ways:
            when(pred, lambda dev=dev: pl.semaphore_signal(bar, inc=1, device_id=dev, device_id_type=MESH))
        pl.semaphore_wait(bar, 3 + jnp.minimum(self.z, 1) + jnp.minimum(self.nz - 1 - self.z, 1))

class Gather:
    def __init__(self, at, block, out, sems, line_only=False):
        self.at, self.block, self.out, self.line_only = at, block, out, line_only
        self.zs, self.zr, self.ps, self.pr, self.own = sems
        self.late = []

    def cell(self, z, c):
        p = self.at
        return self.out.at[:, z, c] if self.line_only else self.out.at[p.y, p.x, z, c]
    def line(self, y, x, c):
        return self.out.at[:, :, c] if self.line_only else self.out.at[y, x, :, c]
    def copy(self, src, dst, s, r, dev):
        return pltpu.make_async_remote_copy(src_ref=src, dst_ref=dst, send_sem=s, recv_sem=r, device_id=dev, device_id_type=MESH)
    def send(self, pred, src, dst, s, r, dev):
        def go():
            self.copy(src, dst, s, r, dev).start()
        when(pred, go)
        def done():
            self.copy(src, dst, s, r, dev).wait_send()
        self.late.append((pred, done))
    def arrived(self, pred, ref, s, r):
        when(pred, lambda: self.copy(ref, ref, s, r, self.at.pair).wait_recv())

    def across(self, pred, ref, block=None):
        p = self.at
        src = ref if block is None else block
        if not self.line_only:
            for k, dev in ((4, p.first), (5, p.second)):
                when(pred, lambda k=k, dev=dev: self.copy(src, ref, self.ps.at[k], self.pr.at[k], dev).start())
    def start(self):
        p = self.at
        mine = self.cell(p.z, p.c)
        self.send(p.has_up, self.block, mine, self.zs.at[0, 0], self.zr.at[0, 0], p.up)
        self.send(p.has_down, self.block, mine, self.zs.at[1, 0], self.zr.at[1, 0], p.down)
        self.across(None, mine, self.block)
        pltpu.make_async_copy(self.block, mine, self.own).start()
    def hop(self, j):
        p = self.at
        for way, pred, more, ref, dev in ((0, p.z >= j, p.has_up, self.cell(p.z - j, p.c), p.up),
                                          (1, p.z < p.nz - j, p.has_down, self.cell(p.z + j, p.c), p.down)):
            self.arrived(pred, ref, self.zs.at[way, j - 1], self.zr.at[way, j - 1])
            if j < p.nz - 1:
                self.send(both(pred, more), ref, ref, self.zs.at[way, j], self.zr.at[way, j], dev)
            self.across(pred, ref)
    def z_done(self):
        p = self.at
        pltpu.make_async_copy(self.block, self.cell(p.z, p.c), self.own).wait()
        mine = self.line(p.y, p.x, p.c)
        self.send(None, mine, mine, self.ps.at[0], self.pr.at[0], p.pair)
        if not self.line_only:
            for k in (4, 5):
                self.late.append((None, lambda k=k: self.copy(mine, mine, self.ps.at[k], self.pr.at[k], p.pair).wait_send()))
    def after_first(self):
        p = self.at
        if self.line_only: return
        got = self.line(p.y1, p.x1, p.c)
        self.arrived(None, got, self.ps.at[4], self.pr.at[4])
        self.send(None, got, got, self.ps.at[6], self.pr.at[6], p.second)
        self.send(None, got, got, self.ps.at[1], self.pr.at[1], p.pair)
    def after_second(self):
        p = self.at
        if self.line_only: return
        for k, (y, x) in enumerate(((p.y2, p.x2), (p.yo, p.xo))):
            got = self.line(y, x, p.c)
            self.arrived(None, got, self.ps.at[5 + k], self.pr.at[5 + k])
            self.send(None, got, got, self.ps.at[2 + k], self.pr.at[2 + k], p.pair)
    def whole(self):
        p = self.at
        lines = [(p.y, p.x)] if self.line_only else [(p.y, p.x), (p.y2, p.x2), (p.y1, p.x1), (p.yo, p.xo)]
        for k, (y, x) in enumerate(lines):
            self.arrived(None, self.line(y, x, 1 - p.c), self.ps.at[k], self.pr.at[k])
    def drain(self):
        for pred, done in self.late:
            when(pred, done)

def sem_shapes(n, nz):
    D = pltpu.SemaphoreType.DMA
    return [D((n, 2, nz)), D((n, 2, nz)), D((n, 8)), D((n, 8)), D((n,))]


def pad16(r):
    return (r + 15) // 16 * 16


PIECES = ((K_SMALL, 0), (K_KV, 0), (K_TOK, 0), (K_KV, 1), (K_TOK, 1), (K_QKV, 0), (K_QKV, 1), (K_QKV, 2), (K_AO, 0), (K_CT, 0), (K_CQ, 0),
          (K_CO, 0), (K_CT, 1), (K_UP, 0), (K_UP, 1), (K_UP, 2), (K_UP, 3), (K_DN, 0), (K_DN, 1))
lines_only = (K_TOK, K_CT)
hop_lag, first_lag, second_lag, whole_lag, send_ahead, units_per_step = 0, 3, 4, 5, 2, 4


def piece(ref, name, c):
    cut = sum(k == name for k, _ in PIECES)
    if cut == 1:
        return ref
    if name in lines_only:
        return ref.at[c:c + 1]
    lead = (slice(None),) * (len(ref.shape) - 2)
    if name == K_DN:
        tiles = ref.shape[-2] // 16
        return ref.at[lead + (slice(tiles * c // cut * 16, tiles * (c + 1) // cut * 16),)]
    cols = ref.shape[-1] // cut
    return ref.at[lead + (slice(None), slice(c * cols, (c + 1) * cols))]


def forward_gather(z, arrays, wanted, times, pool, nz):
    names = list(arrays)
    S = jax.ShapeDtypeStruct
    whole, stages = {}, []
    for k, b in arrays.items():
        if k in lines_only:
            whole[k] = S((b.shape[0], nz, 2) + b.shape[1:], b.dtype)
            stages.append(pltpu.VMEM(b.shape, b.dtype))
        else:
            r = pad16(b.shape[0])
            whole[k] = S((2, 2, nz, 2, r, b.shape[1]), b.dtype)
            stages.append(pltpu.VMEM((r, b.shape[1]), b.dtype))
    saved = {**saved_shapes(z), K_BACK_Y: S((z.MB, z.stream, z.width), BF)}
    share = {K_UP: K_QKV, K_CT: K_TOK}
    room = {k: whole[k] for k in names if k not in share}
    room[K_QKV] = whole[K_UP]
    count = len(PIECES)

    def kernel(*refs):
        refs = list(refs)
        take = lambda k: [refs.pop(0) for _ in range(k)]
        blocks = dict(zip(names, take(len(names))))
        r = Refs([K_WANTED, K_TIMES, K_POOL], take(3))
        landed = dict(zip(names, take(len(names))))
        kept = dict(zip(saved, take(len(saved))))
        stage = dict(zip(names, take(len(names))))
        r.__dict__.update(zip(saved, take(len(saved))))
        bufs = dict(zip(room, take(len(room))))
        r.bias, r.upb, r.sp, loads, saves = take(5)
        sems = take(5)
        at = Place(nz)
        for k in names:
            b, s = blocks[k], stage[k]
            if s.shape == b.shape:
                s[...] = b[...]
            else:
                s[...] = jnp.zeros(s.shape, s.dtype)
                s[:b.shape[0], :] = b[...]
        at.barrier()
        gs = [Gather(at, piece(stage[k], k, c), piece(landed[k], k, c), [s.at[j] for s in sems], k in lines_only)
              for j, (k, c) in enumerate(PIECES)]

        def save(k):
            pltpu.make_async_copy(getattr(r, k), kept[k], saves.at[list(saved).index(k)]).start()
        r.save = save
        def buffer(k):
            if k in (K_QKV, K_UP):
                return bufs[K_QKV].at[:, :, :, :, :, :whole[k].shape[-1]]
            return bufs[share.get(k, k)]
        def load(j):
            k, c = PIECES[j]
            return pltpu.make_async_copy(piece(landed[k], k, c), piece(buffer(k), k, c), loads.at[j])
        def ready(k):
            b = bufs[share.get(k, k)]
            if k in lines_only:
                return b.reshape(z.MB, z.stream, z.width)
            flat = b.reshape(GROUPS * b.shape[-2], b.shape[-1])
            return flat.at[:, :whole[k].shape[-1]] if k in (K_QKV, K_UP) else flat

        there, started, waited = set(), set(), set()
        free = set(room)
        work = forward_steps(z, ready, r)
        state = {K_NEED: next(work), K_DONE: False}
        def start_loads():
            for j in sorted(there - started):
                if PIECES[j][0] in free:
                    load(j).start()
                    started.add(j)
        def advance(units):
            while units and not state[K_DONE]:
                need = state[K_NEED]
                if need:
                    if need == K_AO:
                        free.add(K_UP)
                    if need == K_QKV:
                        free.add(K_CT)
                    start_loads()
                    ask = {j for j, (k, c) in enumerate(PIECES) if k == need or k + str(c) == need}
                    if not ask <= started:
                        return
                    for j in sorted(ask - waited):
                        load(j).wait()
                    waited.update(ask)
                try:
                    state[K_NEED] = next(work)
                except StopIteration:
                    state[K_DONE] = True
                units -= 1

        for g in gs[:send_ahead]:
            g.start()
        for t in range(count + whole_lag):
            def stage_of(lag):
                return gs[t - lag] if 0 <= t - lag < count else None
            if t + send_ahead < count:
                gs[t + send_ahead].start()
            for j in range(1, nz):
                if g := stage_of(j - 1):
                    g.hop(j)
            if g := stage_of(nz - 2):
                g.z_done()
            if g := stage_of(first_lag):
                g.after_first()
            if g := stage_of(second_lag):
                g.after_second()
            if g := stage_of(whole_lag):
                g.whole()
                there.add(t - whole_lag)
                start_loads()
            advance(units_per_step if t < count + whole_lag - 1 else 1 << 20)
        for g in gs:
            g.drain()
        for i, k in enumerate(saved):
            pltpu.make_async_copy(getattr(r, k), kept[k], saves.at[i]).wait()

    V = pl.BlockSpec(memory_space=pltpu.VMEM)
    A = pl.BlockSpec(memory_space=pl.ANY)
    D = pltpu.SemaphoreType.DMA
    got = pl.pallas_call(kernel, name="gather_forward", out_shape=list(whole.values()) + list(saved.values()),
        in_specs=[V] * (len(names) + 3), out_specs=[A] * (len(names) + len(saved)),
        scratch_shapes=stages + [pltpu.VMEM(s.shape, s.dtype) for s in saved.values()] + [pltpu.VMEM(s.shape, s.dtype) for s in room.values()]
            + [pltpu.VMEM((HEADS, z.length, z.length), F32), pltpu.VMEM((1, z.ff), F32), pltpu.VMEM((z.width, z.wide), BF), D((count,)), D((len(saved),))] + sem_shapes(count, nz),
        compiler_params=pltpu.CompilerParams(collective_id=1, has_side_effects=True, vmem_limit_bytes=63 * MIB))(*arrays.values(), wanted, times, pool)
    flat = lambda k, v: v.reshape(-1, v.shape[-1])
    return {k: flat(k, v) for k, v in zip(names, got) if k in WEIGHTS}, dict(zip(saved, got[len(names):]))


CUTS = {K_DN: 2, K_UP: 4, K_CO: 1, K_KV: 2, K_CQ: 1, K_AO: 1, K_QKV: 6}
SUMS = tuple((k, c) for k in (K_Y, K_DN, K_UP, K_CO, K_KV, K_CQ, K_AO, K_X, K_SMALL, K_QKV) for c in range(CUTS.get(k, 1)))
early_lags, late_lags, late_pieces = (1, 3, 5, 7), (1, 2, 3, 4), 4


def lags_of(i, nz):
    pair, second, first, along = early_lags if i < len(SUMS) - late_pieces else late_lags
    return {K_PAIR: pair, K_SECOND: second, K_FIRST: first, **{h: along + h - 1 for h in range(1, nz)}, K_FINISH: along + nz - 1}


class Sum:
    def __init__(self, at, held, landing, out, sems, line_only, stages):
        self.at, self.held, self.out, self.line_only, self.stages = at, held, out, line_only, stages
        if line_only:
            self.rc, self.ru, self.rd = landing
        else:
            self.rc, self.r2, self.r1, self.ru, self.rd = landing
        self.ps, self.pr, self.us, self.ur, self.ds, self.dr = sems
        self.late = []
    def copy(self, src, dst, s, r, dev):
        return pltpu.make_async_remote_copy(src_ref=src, dst_ref=dst, send_sem=s, recv_sem=r, device_id=dev, device_id_type=MESH)
    def send(self, pred, src, dst, s, r, dev):
        when(pred, lambda: self.copy(src, dst, s, r, dev).start())
        self.late.append((pred, lambda: self.copy(src, dst, s, r, dev).wait_send()))
    def fetch(self, pred, ref, s, r):
        stage, sem = self.stages.room(ref)
        def go():
            self.copy(ref, ref, s, r, self.at.pair).wait_recv()
            pltpu.make_async_copy(ref, stage, sem).start()
        when(pred, go)
        def add(mine):
            def body():
                pltpu.make_async_copy(ref, stage, sem).wait()
                mine[...] = mine[...] + stage[...]
            when(pred, body)
        return add
    def line(self, y, x):
        return self.held.at[y, x, :, self.at.c]
    def cell(self, z):
        return self.held.at[:, z, self.at.c] if self.line_only else self.held.at[self.at.y, self.at.x, z, self.at.c]
    def start(self):
        p = self.at
        other = self.held.at[:, :, 1 - p.c] if self.line_only else self.held.at[:, :, :, 1 - p.c]
        self.send(None, other, self.rc, self.ps.at[0], self.pr.at[0], p.pair)
    def after_pair(self):
        p = self.at
        if self.line_only:
            add = self.fetch(None, self.rc, self.ps.at[0], self.pr.at[0])
            return [lambda: add(self.held.at[:, :, p.c])]
        stage, sem = self.stages.room(self.rc)
        self.copy(self.rc, self.rc, self.ps.at[0], self.pr.at[0], p.pair).wait_recv()
        fetch = pltpu.make_async_copy(self.rc, stage, sem)
        fetch.start()
        def adds():
            fetch.wait()
            def plus(y, x):
                mine = self.line(y, x)
                mine[...] = mine[...] + stage[y, x]
            for k, (y, x) in enumerate(((p.y2, p.x2), (p.yo, p.xo))):
                plus(y, x)
                self.send(None, self.line(y, x), self.r2.at[k], self.ps.at[1 + k], self.pr.at[1 + k], p.second)
            plus(p.y1, p.x1)
            plus(p.y, p.x)
        return [adds]
    def after_second(self):
        p = self.at
        if self.line_only:
            return []
        far = self.fetch(None, self.r2.at[1], self.ps.at[2], self.pr.at[2])
        near = self.fetch(None, self.r2.at[0], self.ps.at[1], self.pr.at[1])
        def adds():
            far(self.line(p.y1, p.x1))
            self.send(None, self.line(p.y1, p.x1), self.r1, self.ps.at[3], self.pr.at[3], p.first)
            near(self.line(p.y, p.x))
        return [adds]
    def after_first(self):
        if self.line_only:
            return []
        add = self.fetch(None, self.r1, self.ps.at[3], self.pr.at[3])
        return [lambda: add(self.line(self.at.y, self.at.x))]
    def z_step(self, h):
        p, nz = self.at, self.at.nz
        todo = []
        for j in range(nz - h, 0, -1):
            for here, goal, land, s, r, dev in ((p.z == h - 1, h - 1 + j, self.ru, self.us, self.ur, p.up),
                                                (p.z == nz - h, nz - h - j, self.rd, self.ds, self.dr, p.down)):
                add = self.fetch(here, land.at[j], s.at[j + 1], r.at[j]) if h > 1 else None
                def go(add=add, here=here, goal=goal, land=land, s=s, r=r, dev=dev, j=j):
                    if add:
                        add(self.cell(goal))
                    self.send(here, self.cell(goal), land.at[j - 1], s.at[j], r.at[j - 1], dev)
                todo.append(go)
        return todo
    def finish(self):
        p = self.at
        up = self.fetch(p.has_down, self.ru.at[0], self.us.at[1], self.ur.at[0])
        down = self.fetch(p.has_up, self.rd.at[0], self.ds.at[1], self.dr.at[0])
        def go():
            mine = self.cell(p.z)
            up(mine)
            down(mine)
            if self.line_only:
                self.out[...] = mine[...]
            else:
                self.out[...] = mine[...][:self.out.shape[0]].astype(self.out.dtype)
        return [go]
    def drain(self):
        for pred, done in self.late:
            when(pred, done)


class Stages:
    def __init__(self, pools, sems):
        self.pools, self.sems = pools, sems
        self.reset()
    def reset(self):
        self.used, self.count = {}, 0
    def room(self, ref):
        lead = ref.shape[:-1]
        n = 1
        for k in lead:
            n *= k
        key = (ref.shape[-1], jnp.dtype(ref.dtype).name)
        off = self.used.get(key, 0)
        self.used[key] = off + n
        sem = self.sems.at[self.count]
        self.count += 1
        return self.pools[key].at[off:off + n].reshape(ref.shape), sem


def landing_shapes(shape, line_only, nz):
    if line_only:
        m, _, _, r, n = shape
        return [(m, nz, r, n), (nz - 1, m, r, n), (nz - 1, m, r, n)]
    r, n = shape[-2:]
    return [(2, 2, nz, r, n), (2, nz, r, n), (nz, r, n), (nz - 1, r, n), (nz - 1, r, n)]


def sum_piece_shape(whole, name, c):
    cut = sum(k == name for k, _ in SUMS)
    r, n = whole[-2:]
    rows, cols = slice(0, r), slice(0, n)
    if name == K_DN:
        rows = slice(r // 16 * c // cut * 16, r // 16 * (c + 1) // cut * 16)
    elif cut > 1:
        cols = slice(n // cut * c, n // cut * (c + 1))
    return whole[:-2] + (rows.stop - rows.start, cols.stop - cols.start), rows, cols


def backward_scatter(z, weights, saved, back_y, wanted, times, shards, nz):
    names = list(WEIGHTS)
    shapes = weight_shapes(z)
    S = jax.ShapeDtypeStruct
    tok = z.length // 2
    blocked = {k: (2, 2, nz, 2, shapes[k][0] // GROUPS, shapes[k][1]) for k in names}
    blocked[K_SMALL] = (2, 2, nz, 2, 8, 128)
    blocked[K_Y] = blocked[K_X] = (z.MB, nz, 2, tok, z.width)
    kinds = {k: F32 if k == K_SMALL else BF for k in blocked}
    lines = (K_Y, K_X)
    placed = [sum_piece_shape(blocked[k], k, c) for k, c in SUMS]
    landings = [S(s, kinds[k]) for (k, c), (shape, _, _) in zip(SUMS, placed) for s in landing_shapes(shape, k in lines, nz)]
    outs = {K_POOL_GRAD: S((z.MB * z.keys, z.width), F32)}
    for k in names:
        outs[k] = S(shards[k].shape, F32)
    outs.update(small=S((8, 128), F32), y=S((z.MB, tok, z.width), BF), x=S((z.MB, tok, z.width), BF))
    part = z.keys // 2
    share = {K_H1: K_H2, K_X: K_H2, K_N2: K_N3, K_N1: K_N3, K_A: K_C, K_JOIN: K_GL, K_PS: K_PC}
    after = {(K_TILE, 0): (K_GL,), (K_TILE, 1): ("w up",), (K_TILE, 2): (K_SPT, K_VEC, K_H2, K_N3), (K_TILE, 3): (K_C, "w co"),
             (K_GRAD, K_DN, CUTS[K_DN] - 1): (K_JOIN, K_CQ, K_CKV), (K_GRAD, K_UP, 0): (K_PC, K_EP),
             (K_GRAD, K_UP, CUTS[K_UP] - 1): (K_H1, K_N2, "w cq"), (K_GRAD, K_CO, 0): (K_A, "w ao", "w qkv"),
             (K_GRAD, K_KV, 0): (K_PS,), (K_GRAD, K_CQ, 0): (K_X, K_N1)}
    room = {k: saved[k] for k in saved if k not in share and k != K_SLOPE}
    local = {K_DU: ((z.rows, z.ff), BF), K_UPB_SUM: ((1, z.ff), F32), K_DH: ((z.rows, z.width), F32), K_E: ((z.rows, z.width), BF),
             K_DC: ((z.rows, z.att), BF), K_TABLE: ((z.length, HEADS * z.length), F32),
             K_TILES: ((2, max(z.rows, part), max(z.ff // 4, z.width)), F32), K_SMALL_GRAD: ((2, 2, nz, 2, 8, 128), F32), "line": ((z.MB, nz, 2, tok, z.width), BF)}
    steps = max(i + max(lags_of(i, nz).values()) for i in range(len(SUMS))) + 1
    plan = {}
    most = [0]

    def schedule(t):
        return [(i, name) for i in range(len(SUMS)) for name, lag in lags_of(i, nz).items() if i + lag == t]
    def asks(i, name):
        (k, c), (shape, _, _) = SUMS[i], placed[i]
        got = landing_shapes(shape, k in lines, nz)
        if name == K_PAIR:
            return [got[0]]
        if name in (K_SECOND, K_FIRST):
            return [] if k in lines else [got[1][1:]] * 2 if name == K_SECOND else [got[2]]
        z_block = got[-1][1:]
        return [z_block] * 2 if name == K_FINISH else [z_block] * (2 * (nz - name) if name > 1 else 0)
    for t in range(steps):
        need, count = {}, 0
        for i, name in schedule(t):
            for s in asks(i, name):
                n = 1
                for d in s[:-1]:
                    n *= d
                key = (s[-1], jnp.dtype(kinds[SUMS[i][0]]).name)
                need[key] = need.get(key, 0) + n
                count += 1
        for key, n in need.items():
            plan[key] = max(plan.get(key, 0), n)
        most[0] = max(most[0], count)

    def kernel(*refs):
        refs = list(refs)
        take = lambda k: [refs.pop(0) for _ in range(k)]
        stored = dict(zip(names, take(len(names))))
        kept = dict(zip(saved, take(len(saved))))
        y_in = take(1)[0]
        r = Refs([K_WANTED, K_TIMES], take(2))
        result = dict(zip(outs, take(len(outs))))
        land = take(len(landings))
        bufs = dict(zip(names, take(len(names))))
        slots = dict(zip(room, take(len(room))))
        r.__dict__.update(zip(local, take(len(local))))
        pools = dict(zip(plan, take(len(plan))))
        wsem, ssem, tsem, psem, ysem, dsem, stage_sem = take(7)
        sems = take(6)
        at = Place(nz)
        def slot(k):
            ref = slots[share.get(k, k)]
            if k == K_JOIN:
                return ref.at[:, :3 * z.att]
            if k == K_PS:
                return ref.reshape(z.MB, HEADS // 2, 2 * z.win * z.pool, NL).at[:, :, :2 * z.length]
            return ref
        for k in saved:
            if k != K_SLOPE:
                setattr(r, k, slot(k))
        small_held = r.small_grad
        r.small_grad = small_held.reshape(GROUPS * 8, 128)
        r.dq, r.dcq, r.dckv = r.join, r.cq, r.ckv
        r.back_x = r.line.reshape(z.MB, z.stream, z.width)
        step = z.ff // 4
        slope_tiles, r.pool_tiles = r.tiles.at[:, :z.rows, :step], r.tiles.at[:, :part, :z.width]
        r.pool_hi, r.pool_lo = r.ep, bufs[K_UP].reshape(shapes[K_UP]).at[:z.MB * z.keys, 2 * z.att:2 * z.att + z.wide]
        held = {**bufs, K_SMALL: small_held, K_Y: r.line, K_X: r.line}
        load = lambda k: pltpu.make_async_copy(stored[k], bufs[k], wsem.at[names.index(k)])
        get = lambda k: pltpu.make_async_copy(kept[k], slot(k), ssem.at[list(saved).index(k)])
        slope = lambda i: pltpu.make_async_copy(kept[K_SLOPE].at[:, i * step:(i + 1) * step], slope_tiles.at[i % 2], tsem.at[i % 2])
        y_load = pltpu.make_async_copy(y_in, r.line, ysem)
        dn_load = lambda i: pltpu.make_async_copy(stored[K_DN].at[i // 2, i % 2], bufs[K_DN].at[i // 2, i % 2], dsem.at[i])
        get(K_CT).start()
        for i in range(4):
            dn_load(i).start()
            if i < 2:
                slope(i).start()
        y_load.start()
        begin = lambda k: load(k[2:]).start() if k[:2] == "w " else get(k).start()
        at.barrier()
        def slope_tile(i):
            slope(i).wait()
            return slope_tiles[i % 2]
        pool_copy = lambda i: pltpu.make_async_copy(r.pool_tiles.at[i % 2], result[K_POOL_GRAD].at[i * part:(i + 1) * part], psem.at[i % 2])
        def put_pool(i, value):
            if i >= 2:
                pool_copy(i - 2).wait()
            r.pool_tiles[i % 2] = value
            pool_copy(i).start()
        r.slope_tile, r.put_pool, r.cuts = slope_tile, put_pool, CUTS
        ready = lambda k: bufs[k].reshape(shapes[k])

        stages = Stages(pools, stage_sem)
        sums, spot = [], 0
        for i, ((k, c), (shape, rows, cols)) in enumerate(zip(SUMS, placed)):
            n = len(landing_shapes(shape, k in lines, nz))
            out = result[k]
            if k in names:
                lead = (slice(None),) * 4
                part_of = held[k].at[lead + (rows, cols)]
                last = min(rows.stop, out.shape[0])
                out = out.at[rows.start:last, cols]
            else:
                part_of = held[k]
            sums.append(Sum(at, part_of, land[spot:spot + n], out, [s.at[i] for s in sems], k in lines, stages))
            spot += n

        work = backward_steps(z, ready, r)
        made = set()
        def until(piece):
            if piece == (K_Y, 0):
                y_load.wait()
                return
            if piece == (K_X, 0):
                sums[0].drain()
                sums[0].late = []
            while piece not in made:
                event = next(work)
                kind = event and event[0]
                if kind == K_WEIGHT:
                    load(event[1]).wait()
                if kind == K_SAVED:
                    for k in event[1]:
                        get(k).wait()
                if kind == K_GRAD:
                    made.add(event[1:])
                if kind == K_TILE:
                    i = event[1]
                    dn_load(i).wait()
                    if 1 <= i <= 2:
                        slope(i + 1).start()
                for k in after.get(event, ()):
                    begin(k)

        spare = bufs[K_UP].at[:, :, :, :, :, :shapes[K_KV][1]]
        again = pltpu.make_async_copy(stored[K_KV], spare, wsem.at[names.index(K_KV)])
        pool_work = pool_steps(z, lambda k: bufs[K_UP].reshape(shapes[K_UP]).at[:, :shapes[K_KV][1]], r)
        def idle():
            event = next(pool_work, K_DONE)
            if event and event != K_DONE:
                again.wait()
                event = next(pool_work)
            return event != K_DONE

        for t in range(steps):
            if t < len(SUMS):
                until(SUMS[t])
                sums[t].start()
                if t + 1 == len(SUMS):
                    for i, (k, _) in enumerate(SUMS):
                        if k == K_UP:
                            sums[i].drain()
                            sums[i].late = []
                    again.start()
            for part_of_step in ((K_PAIR, K_SECOND, K_FIRST), None):
                todo = []
                stages.reset()
                for i, name in schedule(t):
                    s = sums[i]
                    if (part_of_step is None) == (name in (K_PAIR, K_SECOND, K_FIRST)):
                        continue
                    if name == K_FINISH:
                        todo += s.finish()
                    elif name == K_PAIR:
                        todo += s.after_pair()
                    elif name == K_SECOND:
                        todo += s.after_second()
                    elif name == K_FIRST:
                        todo += s.after_first()
                    else:
                        todo += s.z_step(name)
                if t >= len(SUMS):
                    idle()
                for go in todo:
                    go()
        while idle():
            pass
        for s in sums:
            s.drain()
        for i in (z.MB * 2 - 2, z.MB * 2 - 1):
            pool_copy(i).wait()

    V = pl.BlockSpec(memory_space=pltpu.VMEM)
    A = pl.BlockSpec(memory_space=pl.ANY)
    D = pltpu.SemaphoreType.DMA
    n = len(SUMS)
    got = pl.pallas_call(kernel, name="backward_scatter", out_shape=list(outs.values()) + landings,
        in_specs=[A] * (len(names) + len(saved) + 1) + [V] * 2,
        out_specs=[A] + [V] * (len(outs) - 1) + [A] * len(landings),
        scratch_shapes=[pltpu.VMEM(blocked[k], BF) for k in names] + [pltpu.VMEM(v.shape, v.dtype) for v in room.values()]
            + [pltpu.VMEM(*v) for v in local.values()] + [pltpu.VMEM((rows, key[0]), jnp.dtype(key[1])) for key, rows in plan.items()]
            + [D((len(names),)), D((len(saved),)), D((2,)), D((2,)), D, D((4,)), D((most[0],))]
            + [D((n, 4)), D((n, 4)), D((n, nz + 1)), D((n, nz + 1)), D((n, nz + 1)), D((n, nz + 1))],
        compiler_params=pltpu.CompilerParams(collective_id=2, has_side_effects=True, vmem_limit_bytes=63 * MIB),
    )(*[weights[k].reshape(blocked[k]) for k in names], *saved.values(), back_y.reshape(blocked[K_Y]), wanted, times)
    return dict(zip(outs, got))


def vectors(norm1_gain, norm2_gain, norm3_gain, attn_out_bias, cca_out_bias, ffw_down_bias, rel_table, ffw_up_bias):
    return [norm1_gain, norm2_gain, norm3_gain, attn_out_bias, cca_out_bias, ffw_down_bias, rel_table, ffw_up_bias]


def to_groups(v):
    small = v.shape[0] // GROUPS
    big = (small + 15) // 16 * 16
    return jnp.pad(v.reshape(GROUPS, small, -1), ((0, 0), (0, big - small), (0, 0))).reshape(GROUPS * big, -1)


def from_groups(v, rows):
    return v.reshape(GROUPS, v.shape[0] // GROUPS, -1)[:, :rows // GROUPS].reshape(rows, -1)


def body(tokens, cotangent, lengths, deal, pool, neighbour_ids, norm1_gain, attn_qkv, attn_out, attn_out_bias, rel_table,
         norm2_gain, cca_query, cca_kv, cca_out, cca_out_bias, norm3_gain, ffw_up, ffw_up_bias, ffw_down, ffw_down_bias):
    members, member = lax.axis_size(K_FSDP), lax.axis_index(K_FSDP)
    devices = members * lax.axis_size(K_DP)
    MB, tok_rows, width = tokens.shape
    length = 2 * tok_rows
    z = Sizes(MB, length, width, HEADS * HEAD_DIM, ffw_up.shape[1], pool.shape[1])
    z.stream = members * tok_rows
    shards = {K_QKV: attn_qkv, K_AO: attn_out, K_CQ: cca_query, K_KV: cca_kv, K_CO: cca_out, K_UP: ffw_up, K_DN: ffw_down}
    vecs = vectors(norm1_gain, norm2_gain, norm3_gain, attn_out_bias, cca_out_bias, ffw_down_bias, rel_table, ffw_up_bias)

    ids = jnp.arange(members, dtype=jnp.int32)
    lens, dealt = lengths[:, 0], deal[:, 0]
    starts = jnp.sum(jnp.where(ids[None, :, None] > ids[None, None, :], lens[:, None, :], 0), 2)
    mine = dealt == member
    own_start = jnp.sum(jnp.where(mine, starts, 0), 1)
    own_len = jnp.sum(jnp.where(mine, lens, 0), 1)
    place = jnp.arange(length, dtype=jnp.int32)
    wanted = jnp.where(place[None] < own_len[:, None], own_start[:, None] + place[None], -1).reshape(-1)
    wanted = jnp.broadcast_to(wanted[:, None], (MB * length, 128))
    spans = length // CH
    ids3 = neighbour_ids.reshape(MB, spans, K_NB)
    held = jnp.sum((ids3[..., None] == jnp.arange(z.pool, dtype=jnp.int32)).astype(F32), 2)
    row = jnp.arange(low_row, length, dtype=jnp.int32)
    in_span = ((row[:, None] - (CH - 1)) // CH == jnp.arange(spans, dtype=jnp.int32)) & (row[:, None] >= CH - 1)
    times = jnp.sum(jnp.where(in_span[None, :, :, None], held[:, None], 0.0), 2)
    times = jnp.broadcast_to(times[..., None], times.shape + (NL,)).reshape(MB, z.win, z.keys)
    neighbours = pool.reshape(MB * z.keys, width)

    direct = lax.axis_size(K_DP) == 4 and members % 2 == 0 and devices == GROUPS
    nz = members // 2
    if direct:
        packed = jnp.concatenate([jnp.pad(v[None], ((0, 0), (0, 128 - v.shape[0]))) for v in vecs] + [jnp.zeros((SMALLS - 8, 128), BF)], 0)
        weights, saved = forward_gather(z, {K_SMALL: packed, K_TOK: tokens, K_CT: cotangent, **shards}, wanted, times, neighbours, nz)
        back_y = saved.pop(K_BACK_Y)
        outs = backward_scatter(z, weights, saved, back_y, wanted, times, shards, nz)
        act, dx, small, mine = outs[K_Y], outs[K_X], outs[K_SMALL], outs
        parts = [small[i, :v.shape[0]] for i, v in enumerate(vecs)]
    else:
        whole = lambda v: lax.all_gather(v, (K_DP, K_FSDP), axis=0, tiled=True)
        rows = [jnp.pad(w, ((0, 0), (0, 128 - w.shape[1])))[:, None] for w in [whole(v).reshape(GROUPS, -1) for v in vecs]]
        packed = jnp.concatenate(rows + [jnp.zeros((GROUPS, SMALLS - 8, 128), BF)], 1).reshape(GROUPS * SMALLS, 128)
        gathered = {K_SMALL: packed, **{k: to_groups(whole(v)) for k, v in shards.items()},
                    K_TOK: lax.all_gather(tokens, K_FSDP, axis=1, tiled=True), K_CT: lax.all_gather(cotangent, K_FSDP, axis=1, tiled=True)}
        weights = {k: gathered[k] for k in WEIGHTS}
        saved = forward_plain(z, gathered, wanted, times, neighbours)
        back_y = saved.pop(K_BACK_Y)
        grads, outs = backward_plain(z, weights, saved, wanted, times)
        back_x, small = outs[K_BACK_X], outs[K_SMALL_GRAD]
        down = lambda v: lax.psum_scatter(v.astype(F32), (K_DP, K_FSDP), scatter_dimension=0, tiled=True)
        line = lambda v: lax.psum_scatter(v, K_FSDP, scatter_dimension=1, tiled=True)
        act, dx = line(back_y), line(back_x)
        mine = {k: down(from_groups(grads[k], shards[k].shape[0] * devices)) for k in shards}
        small = small.reshape(GROUPS, 8, 128)
        parts = [down(small[:, i, :v.shape[0] * devices // GROUPS].reshape(-1)) for i, v in enumerate(vecs)]
    g1, g2, g3, ba, bc, bd, rel, upb = parts
    return (act, dx, outs[K_POOL_GRAD].reshape(pool.shape), g1, mine[K_QKV], mine[K_AO], ba, rel, g2, mine[K_CQ], mine[K_KV],
            mine[K_CO], bc, g3, mine[K_UP], upb, mine[K_DN], bd)


def solution(mesh):
    everywhere = (K_DP, K_FSDP)
    rows, vec = P(everywhere, None), P(everywhere)
    slots = P(None, everywhere, None)
    return jax.shard_map(
        body,
        mesh=mesh,
        in_specs=(slots, slots, P(None, K_DP, None), P(None, K_DP, None), P(None, everywhere, None, None), slots,
                  vec, rows, rows, vec, vec, vec, rows, rows, rows, vec, vec, rows, vec, rows, vec),
        out_specs=(slots, slots, P(None, everywhere, None, None), vec, rows, rows, vec, vec, vec, rows, rows, rows, vec, vec,
                   rows, vec, rows, vec),
        check_vma=False,
    )
```

time: 443 us -> 389 us (0.88)
  Pallas kernels: 411 us -> 355 us
    pallas_call x2 -> x1, Pallas kernels: 253 us -> 197 us  [backward_scatter(): pl.pallas_call(kernel, name='backward_scatter', out_shape=list(outs.value...]
    unnamed x17 -> x24, local copies, waits for them, and re-layouts: 11.1 us -> 11.8 us
where the time goes in v3:
time: 389 us; the launch traced here: 384 us
  Pallas kernels  355 us (91%)
  local copies, waits for them, and re-layouts  24.1 us (6%)
    pallas_call x1, Pallas kernels, backward_scatter(): pl.pallas_call(kernel, name='backward_scatter', out_shape=list(outs.value...  197 us
    pallas_call x1, Pallas kernels, forward_gather(): pl.pallas_call(kernel, name='gather_forward', out_shape=list(whole.values...  159 us
    unnamed x24, local copies, waits for them, and re-layouts  11.8 us

profile of v3, /device:TPU:0, one launch (start us, length us, event | category | flops | bytes accessed | tf_op | source)
XLA Modules:
  0.0 383.9 jit_solution(8049701976100057152)
XLA Ops:
  0.7 0.7 broadcast_compare_fusion
  1.3 0.7 pad.27
  2.0 0.7 pad.30
  2.7 0.7 pad.33
  3.3 0.7 pad.28
  4.0 0.7 pad.31
  4.7 0.7 pad.29
  5.3 0.7 pad.34
  6.0 0.7 pad.32
  6.7 0.8 select_reduce_fusion
  7.5 0.8 fusion.2
  8.4 0.8 fusion
  9.4 1.2 concatenate.3.refs_0_
  10.6 0.1 copy.40
  10.7 0.8 broadcast_in_dim.114.refs_10_.refs_27_
  11.5 0.2 broadcast_in_dim.118
  11.7 0.8 reshape.183.refs_11_.refs_28_
  12.5 158.6 %gather_forward.1 = (bf16[2,2,4,2,16,128]{5,4,3,2,1,0:T(8,128)(2,1)}, bf16[2,4,2,64,896]{4,3,2,1,0:T(8,128)(2,1)}, bf16[2,4,2,64,896]{4,3,2,1,0:T(8,128)(2,1)}, ...) custom-call(bf16[16,128]{1,0:T(8,128)(2,1)} %concatenate.3.refs_0_, ...), custom_call_target="tpu_custom_call" | custom-call | tf_op jit(solution)/shard_map/gather_forward/pallas_call | solution.py:939
  171.2 196.8 %backward_scatter.1 = (f32[768,896]{1,0:T(8,128)}, f32[28,3072]{1,0:T(8,128)}, f32[32,896]{1,0:T(8,128)}, f32[28,1024]{1,0:T(8,128)}, f32[28,2048]{1,0:T(8,128)}...) custom-call(bf16[2,2,4,2,32,3072]{5,4,3,2,1,0:T(8,128)(2,1)} %get-tu, ...), custom_call_target="tpu_custom_call" | custom-call | tf_op jit(solution)/shard_map/backward_scatter/pallas_call | solution.py:1305
  368.0 1.2 slice_bitcast_fusion.5
  369.2 1.2 slice_bitcast_fusion.1
  370.4 1.4 slice_bitcast_fusion
  371.8 1.6 copy.54
  373.5 1.6 copy.55
  375.1 3.6 copy.56
  378.7 0.7 copy.57
  379.5 0.6 copy.58
  380.1 0.7 copy.59
  380.8 0.7 copy.60
  381.5 0.6 copy.61
  382.1 0.8 copy.62
  382.9 0.7 copy.63
  (22 shorter events, 0.3 us)
Async XLA Ops:
  375.1 3.6 copy-start.2
  375.1 4.3 %copy-start.6 = (f32[32,896]{1,0:T(8,128)S(1)}, f32[32,896]{1,0:T(8,128)}, u32[]{:S(2)}) copy-start(f32[32,896]{1,0:T(8,128)} %get-tuple-element.125) | copy-start | bytes 344068
  375.1 5.0 %copy-start.4 = (f32[28,1024]{1,0:T(8,128)S(1)}, f32[28,1024]{1,0:T(8,128)}, u32[]{:S(2)}) copy-start(f32[28,1024]{1,0:T(8,128)} %get-tuple-element.129) | copy-start | bytes 344068
  375.1 5.6 %copy-start.3 = (f32[28,2048]{1,0:T(8,128)S(1)}, f32[28,2048]{1,0:T(8,128)}, u32[]{:S(2)}) copy-start(f32[28,2048]{1,0:T(8,128)} %get-tuple-element.130) | copy-start | bytes 688132
  378.7 2.8 copy-start.5
  378.7 3.4 copy-start
  378.7 4.2 %copy-start.1 = (f32[112,896]{1,0:T(8,128)S(1)}, f32[112,896]{1,0:T(8,128)}, u32[]{:S(2)}) copy-start(f32[112,896]{1,0:T(8,128)} %get-tuple-element.136) | copy-start | bytes 1204228

commit v4 on v3

--- a/solution.py
+++ b/solution.py
@@ -801,7 +801,7 @@
 PIECES = ((K_SMALL, 0), (K_KV, 0), (K_TOK, 0), (K_KV, 1), (K_TOK, 1), (K_QKV, 0), (K_QKV, 1), (K_QKV, 2), (K_AO, 0), (K_CT, 0), (K_CQ, 0),
           (K_CO, 0), (K_CT, 1), (K_UP, 0), (K_UP, 1), (K_UP, 2), (K_UP, 3), (K_DN, 0), (K_DN, 1))
 lines_only = (K_TOK, K_CT)
-hop_lag, first_lag, second_lag, whole_lag, send_ahead, units_per_step = 0, 3, 4, 5, 2, 4
+first_lag, second_lag, whole_lag, send_ahead, units_per_step = 3, 5, 6, 2, 4
 
 
 def piece(ref, name, c):
@@ -1328,6 +1328,19 @@
     return v.reshape(GROUPS, v.shape[0] // GROUPS, -1)[:, :rows // GROUPS].reshape(rows, -1)
 
 
+def copied(arrays):
+    n = len(arrays)
+    def kernel(*refs):
+        copies = [pltpu.make_async_copy(refs[i], refs[n + i], refs[2 * n].at[i]) for i in range(n)]
+        for c in copies:
+            c.start()
+        for c in copies:
+            c.wait()
+    A = pl.BlockSpec(memory_space=pl.ANY)
+    return pl.pallas_call(kernel, name="copy_out", out_shape=[jax.ShapeDtypeStruct(v.shape, v.dtype) for v in arrays],
+                          in_specs=[A] * n, out_specs=[A] * n, scratch_shapes=[pltpu.SemaphoreType.DMA((n,))])(*arrays)
+
+
 def body(tokens, cotangent, lengths, deal, pool, neighbour_ids, norm1_gain, attn_qkv, attn_out, attn_out_bias, rel_table,
          norm2_gain, cca_query, cca_kv, cca_out, cca_out_bias, norm3_gain, ffw_up, ffw_up_bias, ffw_down, ffw_down_bias):
     members, member = lax.axis_size(K_FSDP), lax.axis_index(K_FSDP)
@@ -1360,11 +1373,14 @@
     direct = lax.axis_size(K_DP) == 4 and members % 2 == 0 and devices == GROUPS
     nz = members // 2
     if direct:
-        packed = jnp.concatenate([jnp.pad(v[None], ((0, 0), (0, 128 - v.shape[0]))) for v in vecs] + [jnp.zeros((SMALLS - 8, 128), BF)], 0)
+        packed = jnp.concatenate([w for v in vecs for w in (v, jnp.zeros((128 - v.shape[0],), BF))] + [jnp.zeros(((SMALLS - 8) * 128,), BF)])
+        packed = packed.reshape(SMALLS, 128)
         weights, saved = forward_gather(z, {K_SMALL: packed, K_TOK: tokens, K_CT: cotangent, **shards}, wanted, times, neighbours, nz)
         back_y = saved.pop(K_BACK_Y)
         outs = backward_scatter(z, weights, saved, back_y, wanted, times, shards, nz)
-        act, dx, small, mine = outs[K_Y], outs[K_X], outs[K_SMALL], outs
+        small = outs.pop(K_SMALL)
+        mine = dict(zip(outs, copied(list(outs.values()))))
+        act, dx, outs = mine[K_Y], mine[K_X], mine
         parts = [small[i, :v.shape[0]] for i, v in enumerate(vecs)]
     else:
         whole = lambda v: lax.all_gather(v, (K_DP, K_FSDP), axis=0, tiled=True)

time: 389 us -> 524 us (1.35)
  Pallas kernels: 355 us -> 504 us
  local copies, waits for them, and re-layouts: 24.1 us -> 9.63 us
    pallas_call x0 -> x1, Pallas kernels: none -> 155 us  [copied(): pl.pallas_call(kernel, name='copy_out', out_shape=[jax.ShapeDtypeStruct(v...]
    unnamed x24 -> x2, local copies, waits for them, and re-layouts: 11.8 us -> 0.01 us
    pallas_call x1, Pallas kernels: 159 us -> 152 us  [forward_gather(): pl.pallas_call(kernel, name='gather_forward', out_shape=list(whole.values...]
    pad x8 -> x0, local copies, waits for them, and re-layouts: 5.29 us -> none  [body(): jnp.pad(v[None], ((0, 0), (0, 128 - v.shape[0])))]
where the time goes in v4:
time: 524 us; the launch traced here: 518 us
  Pallas kernels  504 us (96%)
  local copies, waits for them, and re-layouts  9.63 us (2%)
    pallas_call x1, Pallas kernels, backward_scatter(): pl.pallas_call(kernel, name='backward_scatter', out_shape=list(outs.value...  196 us
    pallas_call x1, Pallas kernels, copied(): pl.pallas_call(kernel, name='copy_out', out_shape=[jax.ShapeDtypeStruct(v...  155 us
    pallas_call x1, Pallas kernels, forward_gather(): pl.pallas_call(kernel, name='gather_forward', out_shape=list(whole.values...  152 us

profile of v4, /device:TPU:0, one launch (start us, length us, event | category | flops | bytes accessed | tf_op | source)
XLA Modules:
  0.0 518.1 jit_solution(15990494947874840997)
XLA Ops:
  0.7 0.7 broadcast_compare_fusion
  1.4 0.8 select_reduce_fusion
  2.2 0.8 fusion.2
  3.0 0.1 fusion.1
  3.1 0.8 fusion
  3.9 0.1 copy.39
  4.0 0.1 select_reduce_fusion.1
  4.1 6.0 %concatenate.3 = bf16[2048]{0:T(1024)(128)(2,1)} concatenate(bf16[28]{0:T(256)(128)(2,1)} %param.27, bf16[100]{0:T(256)(128)(2,1)S(1)} %broadcast.118, bf16[28]{0:T(256)(128)(2,1)} %param.32, bf16[100]{0:T(256)(128)(2,1)S(1)} %broadcast.118, bf16[28]{0:T(256)(128)(2,1)} %param.37, bf16[100]{0:T(256)(128)(2,1)S(1)} %broadcast.118, bf16[28]{0:T(256)(128)(2,1)} %param.30, ...), dimensions={0} | concatenate | bytes 8192 | tf_op jit(solution)/shard_map/concatenate | solution.py:1376
  10.1 0.1 copy.40
  10.3 0.8 broadcast_in_dim.86.refs_10_.refs_27_
  11.0 0.2 broadcast_in_dim.90
  11.3 0.8 reshape.187.refs_11_.refs_28_
  12.1 152.4 %gather_forward.1 = (bf16[2,2,4,2,16,128]{5,4,3,2,1,0:T(8,128)(2,1)}, bf16[2,4,2,64,896]{4,3,2,1,0:T(8,128)(2,1)}, bf16[2,4,2,64,896]{4,3,2,1,0:T(8,128)(2,1)}, ...) custom-call(bf16[16,128]{1,0:T(8,128)(2,1)} %bitcast.32, ...), custom_call_target="tpu_custom_call" | custom-call | tf_op jit(solution)/shard_map/gather_forward/pallas_call | solution.py:939
  164.5 196.5 %backward_scatter.1 = (f32[768,896]{1,0:T(8,128)}, f32[28,3072]{1,0:T(8,128)}, f32[32,896]{1,0:T(8,128)}, f32[28,1024]{1,0:T(8,128)}, f32[28,2048]{1,0:T(8,128)}...) custom-call(bf16[2,2,4,2,32,3072]{5,4,3,2,1,0:T(8,128)(2,1)} %get-tu, ...), custom_call_target="tpu_custom_call" | custom-call | tf_op jit(solution)/shard_map/backward_scatter/pallas_call | solution.py:1305
  360.9 0.0 copy-start
  360.9 155.3 %copy_out.1 = (f32[768,896]{1,0:T(8,128)}, f32[28,3072]{1,0:T(8,128)}, f32[32,896]{1,0:T(8,128)}, f32[28,1024]{1,0:T(8,128)}, f32[28,2048]{1,0:T(8,128)}, /*inde...) custom-call(f32[768,896]{1,0:T(8,128)} %get-tuple-element.93.refs_0_, ...), custom_call_target="tpu_custom_call" | custom-call | tf_op jit(solution)/shard_map/copy_out/pallas_call | solution.py:1340
  516.3 0.0 copy-done
  516.3 0.5 slice_bitcast_fusion.5
  516.8 0.5 slice_bitcast_fusion.1
  517.3 0.5 slice_bitcast_fusion
  (8 shorter events, 0.0 us)
Async XLA Ops:
  360.9 155.3 %copy-start = (f32[8,128]{1,0:T(8,128)S(1)}, f32[8,128]{1,0:T(8,128)}, u32[]{:S(2)}) copy-start(f32[8,128]{1,0:T(8,128)} %get-tuple-element.106) | copy-start | bytes 12292

commit v5 on v3

--- a/solution.py
+++ b/solution.py
@@ -801,7 +801,7 @@
 PIECES = ((K_SMALL, 0), (K_KV, 0), (K_TOK, 0), (K_KV, 1), (K_TOK, 1), (K_QKV, 0), (K_QKV, 1), (K_QKV, 2), (K_AO, 0), (K_CT, 0), (K_CQ, 0),
           (K_CO, 0), (K_CT, 1), (K_UP, 0), (K_UP, 1), (K_UP, 2), (K_UP, 3), (K_DN, 0), (K_DN, 1))
 lines_only = (K_TOK, K_CT)
-hop_lag, first_lag, second_lag, whole_lag, send_ahead, units_per_step = 0, 3, 4, 5, 2, 4
+first_lag, second_lag, whole_lag, send_ahead, units_per_step = 3, 5, 6, 2, 4
 
 
 def piece(ref, name, c):
@@ -1360,7 +1360,8 @@
     direct = lax.axis_size(K_DP) == 4 and members % 2 == 0 and devices == GROUPS
     nz = members // 2
     if direct:
-        packed = jnp.concatenate([jnp.pad(v[None], ((0, 0), (0, 128 - v.shape[0]))) for v in vecs] + [jnp.zeros((SMALLS - 8, 128), BF)], 0)
+        packed = jnp.concatenate([w for v in vecs for w in (v, jnp.zeros((128 - v.shape[0],), BF))] + [jnp.zeros(((SMALLS - 8) * 128,), BF)])
+        packed = packed.reshape(SMALLS, 128)
         weights, saved = forward_gather(z, {K_SMALL: packed, K_TOK: tokens, K_CT: cotangent, **shards}, wanted, times, neighbours, nz)
         back_y = saved.pop(K_BACK_Y)
         outs = backward_scatter(z, weights, saved, back_y, wanted, times, shards, nz)

time: 389 us -> 383 us (0.985)
  Pallas kernels: 355 us -> 349 us
    pallas_call x1, Pallas kernels: 159 us -> 152 us  [forward_gather(): pl.pallas_call(kernel, name='gather_forward', out_shape=list(whole.values...]
    pad x8 -> x0, local copies, waits for them, and re-layouts: 5.29 us -> none  [body(): jnp.pad(v[None], ((0, 0), (0, 128 - v.shape[0])))]
    concatenate x1, local copies, waits for them, and re-layouts: 1.19 us -> 6.02 us  [body(): jnp.concatenate([w for v in vecs for w in (v, jnp.zeros((128 - v.shape[0]...]
where the time goes in v5:
time: 383 us; the launch traced here: 377 us
  Pallas kernels  349 us (91%)
  local copies, waits for them, and re-layouts  23.7 us (6%)
    pallas_call x1, Pallas kernels, backward_scatter(): pl.pallas_call(kernel, name='backward_scatter', out_shape=list(outs.value...  196 us
    pallas_call x1, Pallas kernels, forward_gather(): pl.pallas_call(kernel, name='gather_forward', out_shape=list(whole.values...  152 us
    unnamed x24, local copies, waits for them, and re-layouts  11.8 us

profile of v5, /device:TPU:0, one launch (start us, length us, event | category | flops | bytes accessed | tf_op | source)
XLA Modules:
  0.0 376.8 jit_solution(5394388625790730075)
XLA Ops:
  0.7 0.7 broadcast_compare_fusion
  1.4 0.8 select_reduce_fusion
  2.2 0.8 fusion.2
  3.0 0.1 fusion.1
  3.1 0.8 fusion
  3.9 0.1 copy.39
  4.0 0.1 select_reduce_fusion.1
  4.1 6.0 %concatenate.3 = bf16[2048]{0:T(1024)(128)(2,1)} concatenate(bf16[28]{0:T(256)(128)(2,1)} %param.27, bf16[100]{0:T(256)(128)(2,1)S(1)} %broadcast.118, bf16[28]{0:T(256)(128)(2,1)} %param.32, bf16[100]{0:T(256)(128)(2,1)S(1)} %broadcast.118, bf16[28]{0:T(256)(128)(2,1)} %param.37, bf16[100]{0:T(256)(128)(2,1)S(1)} %broadcast.118, bf16[28]{0:T(256)(128)(2,1)} %param.30, ...), dimensions={0} | concatenate | bytes 8192 | tf_op jit(solution)/shard_map/concatenate | solution.py:1363
  10.1 0.1 copy.40
  10.3 0.8 broadcast_in_dim.86.refs_10_.refs_27_
  11.0 0.2 broadcast_in_dim.90
  11.3 0.8 reshape.187.refs_11_.refs_28_
  12.1 152.4 %gather_forward.1 = (bf16[2,2,4,2,16,128]{5,4,3,2,1,0:T(8,128)(2,1)}, bf16[2,4,2,64,896]{4,3,2,1,0:T(8,128)(2,1)}, bf16[2,4,2,64,896]{4,3,2,1,0:T(8,128)(2,1)}, ...) custom-call(bf16[16,128]{1,0:T(8,128)(2,1)} %bitcast.33, ...), custom_call_target="tpu_custom_call" | custom-call | tf_op jit(solution)/shard_map/gather_forward/pallas_call | solution.py:939
  164.5 196.5 %backward_scatter.1 = (f32[768,896]{1,0:T(8,128)}, f32[28,3072]{1,0:T(8,128)}, f32[32,896]{1,0:T(8,128)}, f32[28,1024]{1,0:T(8,128)}, f32[28,2048]{1,0:T(8,128)}...) custom-call(bf16[2,2,4,2,32,3072]{5,4,3,2,1,0:T(8,128)(2,1)} %get-tu, ...), custom_call_target="tpu_custom_call" | custom-call | tf_op jit(solution)/shard_map/backward_scatter/pallas_call | solution.py:1305
  360.9 1.2 slice_bitcast_fusion.5
  362.1 1.2 slice_bitcast_fusion.1
  363.3 1.4 slice_bitcast_fusion
  364.7 1.6 copy.54
  366.4 1.6 copy.55
  368.0 3.6 copy.56
  371.6 0.0 copy-done.2
  371.6 0.7 copy.57
  372.4 0.0 copy-done.6
  372.4 0.6 copy.58
  373.0 0.0 copy-done.4
  373.0 0.7 copy.59
  373.7 0.0 copy-done.3
  373.7 0.7 copy.60
  374.4 0.6 copy.61
  375.0 0.8 copy.62
  375.8 0.0 copy-done.1
  375.8 0.7 copy.63
  (17 shorter events, 0.1 us)
Async XLA Ops:
  368.0 3.6 copy-start.2
  368.0 4.3 %copy-start.6 = (f32[32,896]{1,0:T(8,128)S(1)}, f32[32,896]{1,0:T(8,128)}, u32[]{:S(2)}) copy-start(f32[32,896]{1,0:T(8,128)} %get-tuple-element.125) | copy-start | bytes 344068
  368.0 5.0 %copy-start.4 = (f32[28,1024]{1,0:T(8,128)S(1)}, f32[28,1024]{1,0:T(8,128)}, u32[]{:S(2)}) copy-start(f32[28,1024]{1,0:T(8,128)} %get-tuple-element.129) | copy-start | bytes 344068
  368.0 5.6 %copy-start.3 = (f32[28,2048]{1,0:T(8,128)S(1)}, f32[28,2048]{1,0:T(8,128)}, u32[]{:S(2)}) copy-start(f32[28,2048]{1,0:T(8,128)} %get-tuple-element.130) | copy-start | bytes 688132
  371.6 2.8 copy-start.5
  371.6 3.4 copy-start
  371.6 4.2 %copy-start.1 = (f32[112,896]{1,0:T(8,128)S(1)}, f32[112,896]{1,0:T(8,128)}, u32[]{:S(2)}) copy-start(f32[112,896]{1,0:T(8,128)} %get-tuple-element.136) | copy-start | bytes 1204228
